TPU v7x, 256 devices: a whole 4x4x8 slice. The times are simulated.
256 devices in a mesh: seq: 32 (over y, z_hi, core), head: 8 (over z_lo, x).
Axes of the slice: x: 4, y: 4, z: 8 (z_hi: 4, z_lo: 2; z = z_hi * 2 + z_lo), core: 2. Of those that a mesh axis runs over, the one named last changes fastest.
Arguments:
- queries: bfloat16 [8192, 3072], P('seq', 'head'), may hold values from -8 to 8
- keys: bfloat16 [8192, 3072], P('seq', 'head'), may hold values from -8 to 8
- values: bfloat16 [8192, 3072], P('seq', 'head'), may hold values from -6 to 6
- layer_grad: bfloat16 [8192, 3072], P('seq', 'head'), may hold values from -6 to 6
- out_weight: bfloat16 [3072, 3072], P('head'), may hold values from -0.109375 to 0.109375
- text_keys: bfloat16 [256, 3072], P(None, 'head'), may hold values from -6 to 6
- text_values: bfloat16 [256, 3072], P(None, 'head'), may hold values from -6 to 6
- extents: int32 [24, 3], P('head'), may hold values from 0 to 2, as said below
- text_mask: int32 [256], replicated, may hold values 0 or 1
Outputs:
- query_gradient: bfloat16 [8192, 3072], P('seq', 'head')
- key_grad: float32 [8192, 3072], P('seq', 'head')
- value_grad: float32 [8192, 3072], P('seq', 'head')
- text_key_grad: float32 [256, 3072], P('seq', 'head')
- text_value_gradient: float32 [256, 3072], P('seq', 'head')
Inputs may be any that keep to these rules, and one draw needn't show every extreme that they name: `extents`: the time and height reach are 0 or 1, the width reach 0 to 2.
All inputs are finite; a program needn't handle non-finite values.
Results may differ from a plain program's by a relative error of at most 0.0066.
Values may be sent and summed in bfloat16 or wider, within the bound.
No kernel may reach another device: no remote copies, remote signals or barrier semaphores. Data moves between devices by JAX's collectives and lax.ppermute only.
A program may use at most 128 MiB of HBM per device.

v0:
```python
import jax
import jax.numpy as jnp
from jax import lax
from jax.sharding import PartitionSpec as P

DH = 128
TT = 2
TH = 8
TW = 8
HT = 4
TEXT_TOKENS = 256


def from_behind(block, axis, distance):
    devices = range(lax.axis_size(axis))
    route = [(i - distance, i) for i in devices if i - distance in devices]
    return lax.ppermute(block, axis, route)


def window_mask(ext_one, row_index, n_rows, tokens):
    tile_size = TT * TH * TW
    tile_index = jnp.arange(tokens, dtype=jnp.int32) // tile_size
    time_off = jnp.array([-1, -1, -1, 0, 0, 0, 1, 1, 1], jnp.int32)
    height_off = jnp.array([-1, 0, 1, -1, 0, 1, -1, 0, 1], jnp.int32)
    n_time = n_rows // HT
    time_at = row_index // HT + time_off
    height_at = row_index % HT + height_off
    inside = (time_at >= 0) & (time_at < n_time) & (height_at >= 0) & (height_at < HT)
    near_block = inside & (jnp.abs(time_off) <= ext_one[0]) & (jnp.abs(height_off) <= ext_one[1])
    near_width = jnp.abs(tile_index[None, :] - tile_index[:, None]) <= ext_one[2]
    allowed = near_block[None, :, None] & near_width[:, None, :]
    return allowed.reshape(tokens, 9 * tokens)


def fetch_direct(kv_pair, offset):
    return from_behind(kv_pair, "seq", offset)


def return_direct(partial_sum, offset):
    return from_behind(partial_sum, "seq", offset)


def per_device(
    queries, keys, values, layer_grad, out_weight, text_keys, text_values, extents, text_mask
):
    tokens, feat_width = queries.shape
    head_count = feat_width // DH
    inv_root = DH ** (-0.5)
    offsets = [(time_off, height_off) for time_off in (-1, 0, 1) for height_off in (-1, 0, 1)]
    attn_grad = lax.dot_general(
        lax.all_gather(layer_grad, "head", axis=1, tiled=True),
        out_weight,
        (((1,), (1,)), ((), ())),
        preferred_element_type=jnp.float32,
    ).astype(jnp.bfloat16)
    row_index = lax.axis_index("seq")
    n_rows = lax.axis_size("seq")
    video_tokens = 9 * tokens
    kv_pair = jnp.stack([keys, values])
    gathered = jnp.stack(
        [
            (
                kv_pair
                if time_off == 0 and height_off == 0
                else fetch_direct(kv_pair, -(time_off * HT + height_off))
            )
            for time_off, height_off in offsets
        ]
    )
    near_key = jnp.concatenate([gathered[:, 0].reshape(video_tokens, feat_width), text_keys], 0)
    near_value = jnp.concatenate([gathered[:, 1].reshape(video_tokens, feat_width), text_values], 0)
    text_allowed = jnp.broadcast_to((text_mask == 1)[None, :], (tokens, TEXT_TOKENS))
    text_start = 0

    def one_head(head_index):
        first_col = head_index * DH
        ext_one = lax.dynamic_index_in_dim(extents, head_index, 0, keepdims=False)
        allowed = jnp.concatenate(
            [window_mask(ext_one, row_index, n_rows, tokens), text_allowed], 1
        )
        query_head = lax.dynamic_slice_in_dim(queries, first_col, DH, 1)
        grad_head = lax.dynamic_slice_in_dim(attn_grad, first_col, DH, 1)
        key_head = lax.dynamic_slice_in_dim(near_key, first_col, DH, 1)
        value_head = lax.dynamic_slice_in_dim(near_value, first_col, DH, 1)
        scores = (
            lax.dot_general(
                query_head, key_head, (((1,), (1,)), ((), ())), preferred_element_type=jnp.float32
            )
            * inv_root
        )
        scores = jnp.where(allowed, scores, -jnp.inf)
        row_max = jnp.max(scores, -1, keepdims=True)
        weights = jnp.where(allowed, jnp.exp(scores - row_max), jnp.float32(0.0))
        total = jnp.sum(weights, -1, keepdims=True)
        probs = weights / total
        probs_b = probs.astype(jnp.bfloat16)
        dprobs = lax.dot_general(
            grad_head, value_head, (((1,), (1,)), ((), ())), preferred_element_type=jnp.float32
        )
        delta = jnp.sum(probs * dprobs, -1, keepdims=True)
        dscores = (probs * (dprobs - delta)).astype(jnp.bfloat16)
        query_part = jnp.dot(dscores, key_head, preferred_element_type=jnp.float32) * inv_root
        key_part = (
            lax.dot_general(
                dscores, query_head, (((0,), (0,)), ((), ())), preferred_element_type=jnp.float32
            )
            * inv_root
        )
        value_portion = lax.dot_general(
            probs_b, grad_head, (((0,), (0,)), ((), ())), preferred_element_type=jnp.float32
        )
        log_norm = row_max[:, 0] + jnp.log(total[:, 0])
        return (query_part, key_part, value_portion, log_norm, delta[:, 0])

    query_all, key_all, value_all, norm_all, delta_all = lax.map(
        one_head, jnp.arange(head_count, dtype=jnp.int32)
    )
    query_gradient = query_all.transpose(1, 0, 2).reshape(tokens, feat_width).astype(jnp.bfloat16)

    def video_part(stacked):
        return (
            stacked[:, :video_tokens]
            .reshape(head_count, 9, tokens, DH)
            .transpose(1, 2, 0, 3)
            .reshape(9, tokens, feat_width)
        )

    def text_part(stacked):
        return (
            stacked[:, video_tokens - text_start :]
            .transpose(1, 0, 2)
            .reshape(TEXT_TOKENS, feat_width)
        )

    partials = jnp.stack([video_part(key_all), video_part(value_all)], 1)
    own_sum = partials[4]
    for which, (time_off, height_off) in enumerate(offsets):
        if which != 4:
            own_sum = own_sum + return_direct(partials[which], time_off * HT + height_off)
    text_key_sum, text_value_sum = (
        lax.psum_scatter(text_part(key_all), "seq", scatter_dimension=0, tiled=True),
        lax.psum_scatter(text_part(value_all), "seq", scatter_dimension=0, tiled=True),
    )
    return (query_gradient, own_sum[0], own_sum[1], text_key_sum, text_value_sum)


def solution(mesh):
    return jax.shard_map(
        per_device,
        mesh=mesh,
        in_specs=(
            P("seq", "head"),
            P("seq", "head"),
            P("seq", "head"),
            P("seq", "head"),
            P("head", None),
            P(None, "head"),
            P(None, "head"),
            P("head", None),
            P(),
        ),
        out_specs=(
            P("seq", "head"),
            P("seq", "head"),
            P("seq", "head"),
            P("seq", "head"),
            P("seq", "head"),
        ),
        check_vma=False,
    )
```

profile of v0, /device:TPU:33, one launch (start us, length us, event | category | flops | bytes accessed | tf_op | source)
XLA Modules:
  0.0 666.0 jit_solution(16249771968825158333)
XLA Ops:
  7.2 1.2 pad_maximum_fusion.3
  8.5 8.4 %collective-permute-start = (bf16[2,256,384]{2,1,0:T(8,128)(2,1)S(1)}, bf16[2,256,384]{2,1,0:T(8,128)(2,1)}, u32[]{:S(2)}, u32[]{:S(2)}) collective-permute-start(bf16[2,256,384]{2,1,0:T(8,128)(2,1)S(1)} %pad_maximum_fusion.3), channel_id=1, source_target_pairs={{0,40},{8,48},{16,56},{24,64},{32,72},{40,80},{48,88},{56,96},{64,... | collective-permute-start | bytes 1179656 | tf_op jit(solution)/shard_map/ppermute | solution.py:17
  16.9 4.1 collective-permute-start.1
  20.9 7.0 %collective-permute-start.2 = (bf16[2,256,384]{2,1,0:T(8,128)(2,1)S(1)}, bf16[2,256,384]{2,1,0:T(8,128)(2,1)}, u32[]{:S(2)}, u32[]{:S(2)}) collective-permute-start(bf16[2,256,384]{2,1,0:T(8,128)(2,1)S(1)} %pad_maximum_fusion.3), channel_id=1, source_target_pairs={{0,24},{8,32},{16,40},{24,48},{32,56},{40,64},{48,72},{56,80},{64,... | collective-permute-start | bytes 1179656 | tf_op jit(solution)/shard_map/ppermute | solution.py:17
  28.0 1.9 collective-permute-start.3
  29.9 3.1 collective-permute-start.4
  33.8 1.3 collective-permute-start.5
  35.1 1.0 bitcast_dynamic-update-slice_fusion.8
  36.2 28.2 %collective-permute-done.1 = bf16[2,256,384]{2,1,0:T(8,128)(2,1)} collective-permute-done((bf16[2,256,384]{2,1,0:T(8,128)(2,1)S(1)}, bf16[2,256,384]{2,1,0:T(8,128)(2,1)}, u32[]{:S(2)}, u32[]{:S(2)}) %collective-permute-start.1) | collective-permute-done | bytes 393248 | tf_op jit(solution)/shard_map/ppermute | solution.py:17
  64.4 1.3 collective-permute-start.6
  65.7 1.1 bitcast_dynamic-update-slice_fusion.7
  66.8 8.0 %collective-permute-done.2 = bf16[2,256,384]{2,1,0:T(8,128)(2,1)} collective-permute-done((bf16[2,256,384]{2,1,0:T(8,128)(2,1)S(1)}, bf16[2,256,384]{2,1,0:T(8,128)(2,1)}, u32[]{:S(2)}, u32[]{:S(2)}) %collective-permute-start.2) | collective-permute-done | bytes 393248 | tf_op jit(solution)/shard_map/ppermute | solution.py:17
  74.8 1.3 collective-permute-start.7
  76.1 1.1 bitcast_dynamic-update-slice_fusion.6
  77.2 1.1 bitcast_dynamic-update-slice_fusion.5
  78.3 2.1 collective-permute-done.4
  80.5 31.7 %collective-permute-done.5 = bf16[2,256,384]{2,1,0:T(8,128)(2,1)S(1)} collective-permute-done((bf16[2,256,384]{2,1,0:T(8,128)(2,1)S(1)}, bf16[2,256,384]{2,1,0:T(8,128)(2,1)S(1)}, u32[]{:S(2)}, u32[]{:S(2)}) %collective-permute-start.5) | collective-permute-done | bytes 393248 | tf_op jit(solution)/shard_map/ppermute | solution.py:17
  112.3 9.2 %collective-permute-done.6 = bf16[2,256,384]{2,1,0:T(8,128)(2,1)S(1)} collective-permute-done((bf16[2,256,384]{2,1,0:T(8,128)(2,1)S(1)}, bf16[2,256,384]{2,1,0:T(8,128)(2,1)S(1)}, u32[]{:S(2)}, u32[]{:S(2)}) %collective-permute-start.6) | collective-permute-done | bytes 393248 | tf_op jit(solution)/shard_map/ppermute | solution.py:17
  122.7 2.3 pad_maximum_fusion
  125.1 2.5 convolution_convert_fusion
  127.7 57.7 %while.20 = (s32[]{:T(128)}, bf16[3,256,128]{1,2,0:T(8,128)(2,1)S(1)}, f32[3,2560,128]{2,1,0:T(8,128)}, f32[3,2560,128]{2,1,0:T(8,128)}, s32[]{:T(128)}, /*index...) while((s32[]{:T(128)}, ...), condition=%wide.region_4.5_spmd.clone.clone, body=%wide.region_0.4_spmd.sunk.clone.clone.sunk | while | flops 857081216 | bytes 33532196 | solution.py:115
  131.6 1.3 bitcast_and_fusion.3
  135.6 1.8 fusion.79
  138.2 2.2 fusion.83
  140.4 2.1 multiply_reduce_fusion.2
  142.5 1.0 multiply_convert_fusion.2
  143.6 1.6 fusion.82
  145.2 1.6 fusion.81
  150.8 1.3 bitcast_and_fusion.3
  154.8 1.8 fusion.79
  157.4 2.2 fusion.83
  159.6 2.1 multiply_reduce_fusion.2
  161.8 1.0 multiply_convert_fusion.2
  162.8 1.6 fusion.82
  164.4 1.6 fusion.81
  170.1 1.3 bitcast_and_fusion.3
  174.1 1.8 fusion.79
  176.7 2.2 fusion.83
  178.8 2.1 multiply_reduce_fusion.2
  181.0 1.0 multiply_convert_fusion.2
  182.0 1.7 fusion.82
  183.7 1.6 fusion.81
  185.4 4.1 slice.80
  189.5 5.2 copy.59
  194.6 4.1 slice.81
  198.7 5.2 copy.60
  203.8 5.0 fusion.41
  208.8 1.5 collective-permute-start.10
  210.3 6.7 %collective-permute-start.11 = (f32[2,256,384]{1,2,0:T(8,128)}, f32[2,256,384]{1,2,0:T(8,128)S(1)}, u32[]{:S(2)}, u32[]{:S(2)}) collective-permute-start(f32[2,256,384]{1,2,0:T(8,128)} %get-tuple-element.539), channel_id=1, source_target_pairs={{8,0},{16,8},{24,16},{32,24},{40,32},{48,40},{56,48},{64,56},{72,6... | collective-permute-start | bytes 2359304 | tf_op jit(solution)/shard_map/ppermute | solution.py:17
  217.0 1.9 collective-permute-start.12
  218.9 5.4 copy.69
  224.4 5.5 copy.70
  229.9 1.8 slice.124
  231.6 1.8 slice.125
  233.4 14.3 %collective-permute-start.13 = (f32[2,256,384]{1,2,0:T(8,128)}, f32[2,256,384]{1,2,0:T(8,128)}, u32[]{:S(2)}, u32[]{:S(2)}) collective-permute-start(f32[2,256,384]{1,2,0:T(8,128)} %get-tuple-element.541), channel_id=1, source_target_pairs={{0,24},{8,32},{16,40},{24,48},{32,56},{40,64},{48,72},{56,80},{64,... | collective-permute-start | bytes 2359304 | tf_op jit(solution)/shard_map/ppermute | solution.py:17
  247.7 4.0 collective-permute-start.14
  251.7 4.2 collective-permute-start.15
  255.9 1.3 collective-permute-start.8
  257.2 1.3 collective-permute-start.9
  260.6 389.7 %all-reduce.5.cloned.1.call-done = (f32[256,384]{0,1:T(8,128)}, f32[256,384]{0,1:T(8,128)}) async-done(((f32[256,384]{0,1:T(8,128)}, f32[256,384]{0,1:T(8,128)}), (f32[256,384]{0,1:T(8,128)}, f32[256,384]{0,1:T(8,128)})) %all-reduce.5.cloned.1.call-update) | async-done | bytes 786448
  650.3 1.0 constant_dynamic-slice_fusion.2
  652.0 1.0 constant_dynamic-slice_fusion.1
  653.9 3.4 fusion.39
  657.3 0.9 copy.72
  (103 shorter events, 20.6 us)
Async XLA Ops:
  7.2 117.9 %copy-start = (bf16[384,3072]{1,0:T(8,128)(2,1)S(1)}, bf16[384,3072]{1,0:T(8,128)(2,1)}, u32[]{:S(2)}) copy-start(bf16[384,3072]{1,0:T(8,128)(2,1)} %param.17) | copy-start | bytes 7077892
  7.2 71.0 %copy-start.4 = (bf16[256,384]{1,0:T(8,128)(2,1)S(1)}, bf16[256,384]{1,0:T(8,128)(2,1)}, u32[]{:S(2)}) copy-start(bf16[256,384]{1,0:T(8,128)(2,1)} %param.14) | copy-start | bytes 589828
  7.2 71.0 %copy-start.3 = (bf16[256,384]{1,0:T(8,128)(2,1)S(1)}, bf16[256,384]{1,0:T(8,128)(2,1)}, u32[]{:S(2)}) copy-start(bf16[256,384]{1,0:T(8,128)(2,1)} %param.15) | copy-start | bytes 589828
  7.2 117.9 %all-gather.2.cloned.1.call-start = ((), (), s32[]{:S(2)}) async-start(), calls=%async_computation | async-start | bytes 1769472 | tf_op jit(solution)/shard_map/all_gather | solution.py:51
  8.5 25.4 %collective-permute-start = (bf16[2,256,384]{2,1,0:T(8,128)(2,1)S(1)}, bf16[2,256,384]{2,1,0:T(8,128)(2,1)}, u32[]{:S(2)}, u32[]{:S(2)}) collective-permute-start(bf16[2,256,384]{2,1,0:T(8,128)(2,1)S(1)} %pad_maximum_fusion.3), channel_id=1, source_target_pairs={{0,40},{8,48},{16,56},{24,64},{32,72},{40,80},{48,88},{56,96},{64,... | collective-permute-start | bytes 1179656 | tf_op jit(solution)/shard_map/ppermute | solution.py:17
  16.9 47.5 %collective-permute-start.1 = (bf16[2,256,384]{2,1,0:T(8,128)(2,1)S(1)}, bf16[2,256,384]{2,1,0:T(8,128)(2,1)}, u32[]{:S(2)}, u32[]{:S(2)}) collective-permute-start(bf16[2,256,384]{2,1,0:T(8,128)(2,1)S(1)} %pad_maximum_fusion.3), channel_id=1, source_target_pairs={{0,32},{8,40},{16,48},{24,56},{32,64},{40,72},{48,80},{56,88},{64,... | collective-permute-start | bytes 1179656 | tf_op jit(solution)/shard_map/ppermute | solution.py:17
  20.9 53.8 %collective-permute-start.2 = (bf16[2,256,384]{2,1,0:T(8,128)(2,1)S(1)}, bf16[2,256,384]{2,1,0:T(8,128)(2,1)}, u32[]{:S(2)}, u32[]{:S(2)}) collective-permute-start(bf16[2,256,384]{2,1,0:T(8,128)(2,1)S(1)} %pad_maximum_fusion.3), channel_id=1, source_target_pairs={{0,24},{8,32},{16,40},{24,48},{32,56},{40,64},{48,72},{56,80},{64,... | collective-permute-start | bytes 1179656 | tf_op jit(solution)/shard_map/ppermute | solution.py:17
  28.0 49.2 %collective-permute-start.3 = (bf16[2,256,384]{2,1,0:T(8,128)(2,1)S(1)}, bf16[2,256,384]{2,1,0:T(8,128)(2,1)}, u32[]{:S(2)}, u32[]{:S(2)}) collective-permute-start(bf16[2,256,384]{2,1,0:T(8,128)(2,1)S(1)} %pad_maximum_fusion.3), channel_id=1, source_target_pairs={{0,8},{8,16},{16,24},{24,32},{32,40},{40,48},{48,56},{56,64},{64,7... | collective-permute-start | bytes 1179656 | tf_op jit(solution)/shard_map/ppermute | solution.py:17
  29.9 50.6 %collective-permute-start.4 = (bf16[2,256,384]{2,1,0:T(8,128)(2,1)S(1)}, bf16[2,256,384]{2,1,0:T(8,128)(2,1)S(1)}, u32[]{:S(2)}, u32[]{:S(2)}) collective-permute-start(bf16[2,256,384]{2,1,0:T(8,128)(2,1)S(1)} %pad_maximum_fusion.3), channel_id=1, source_target_pairs={{8,0},{16,8},{24,16},{32,24},{40,32},{48,40},{56,48},{64,56},{72,6... | collective-permute-start | bytes 1179656 | tf_op jit(solution)/shard_map/ppermute | solution.py:17
  33.0 617.3 %all-reduce.5.cloned.1.call-start = ((), (), s32[]{:S(2)}) async-start(), calls=%async_computation.1 | async-start | bytes 1572864
  33.8 78.4 %collective-permute-start.5 = (bf16[2,256,384]{2,1,0:T(8,128)(2,1)S(1)}, bf16[2,256,384]{2,1,0:T(8,128)(2,1)S(1)}, u32[]{:S(2)}, u32[]{:S(2)}) collective-permute-start(bf16[2,256,384]{2,1,0:T(8,128)(2,1)S(1)} %pad_maximum_fusion.3), channel_id=1, source_target_pairs={{24,0},{32,8},{40,16},{48,24},{56,32},{64,40},{72,48},{80,56},{88,... | collective-permute-start | bytes 1179656 | tf_op jit(solution)/shard_map/ppermute | solution.py:17
  64.4 57.1 %collective-permute-start.6 = (bf16[2,256,384]{2,1,0:T(8,128)(2,1)S(1)}, bf16[2,256,384]{2,1,0:T(8,128)(2,1)S(1)}, u32[]{:S(2)}, u32[]{:S(2)}) collective-permute-start(bf16[2,256,384]{2,1,0:T(8,128)(2,1)S(1)} %pad_maximum_fusion.3), channel_id=1, source_target_pairs={{32,0},{40,8},{48,16},{56,24},{64,32},{72,40},{80,48},{88,56},{96,... | collective-permute-start | bytes 1179656 | tf_op jit(solution)/shard_map/ppermute | solution.py:17
  74.8 46.8 %collective-permute-start.7 = (bf16[2,256,384]{2,1,0:T(8,128)(2,1)S(1)}, bf16[2,256,384]{2,1,0:T(8,128)(2,1)S(1)}, u32[]{:S(2)}, u32[]{:S(2)}) collective-permute-start(bf16[2,256,384]{2,1,0:T(8,128)(2,1)S(1)} %pad_maximum_fusion.3), channel_id=1, source_target_pairs={{40,0},{48,8},{56,16},{64,24},{72,32},{80,40},{88,48},{96,56},{104... | collective-permute-start | bytes 1179656 | tf_op jit(solution)/shard_map/ppermute | solution.py:17
  121.7 0.9 copy-start.7
  121.7 1.0 copy-start.8
  125.0 2.6 copy-start.5
  125.0 2.6 copy-start.6
  125.0 2.6 copy-start.9
  125.0 2.6 copy-start.10
  125.0 2.6 copy-start.11
  125.0 2.6 copy-start.12
  208.8 42.9 %collective-permute-start.10 = (f32[2,256,384]{1,2,0:T(8,128)}, f32[2,256,384]{1,2,0:T(8,128)S(1)}, u32[]{:S(2)}, u32[]{:S(2)}) collective-permute-start(f32[2,256,384]{1,2,0:T(8,128)} %get-tuple-element.538), channel_id=1, source_target_pairs={{24,0},{32,8},{40,16},{48,24},{56,32},{64,40},{72,48},{80,56},{88,... | collective-permute-start | bytes 2359304 | tf_op jit(solution)/shard_map/ppermute | solution.py:17
  210.3 45.6 %collective-permute-start.11 = (f32[2,256,384]{1,2,0:T(8,128)}, f32[2,256,384]{1,2,0:T(8,128)S(1)}, u32[]{:S(2)}, u32[]{:S(2)}) collective-permute-start(f32[2,256,384]{1,2,0:T(8,128)} %get-tuple-element.539), channel_id=1, source_target_pairs={{8,0},{16,8},{24,16},{32,24},{40,32},{48,40},{56,48},{64,56},{72,6... | collective-permute-start | bytes 2359304 | tf_op jit(solution)/shard_map/ppermute | solution.py:17
  217.0 40.2 %collective-permute-start.12 = (f32[2,256,384]{1,2,0:T(8,128)}, f32[2,256,384]{1,2,0:T(8,128)}, u32[]{:S(2)}, u32[]{:S(2)}) collective-permute-start(f32[2,256,384]{1,2,0:T(8,128)} %get-tuple-element.540), channel_id=1, source_target_pairs={{0,8},{8,16},{16,24},{24,32},{32,40},{40,48},{48,56},{56,64},{64,7... | collective-permute-start | bytes 2359304 | tf_op jit(solution)/shard_map/ppermute | solution.py:17
  224.4 34.1 %copy-start.13 = (u32[256]{0:T(256)S(1)}, u32[256]{0:T(256)}, u32[]{:S(2)}) copy-start(u32[256]{0:T(256)} %constant.185) | copy-start | bytes 3076
  233.4 420.4 %collective-permute-start.13 = (f32[2,256,384]{1,2,0:T(8,128)}, f32[2,256,384]{1,2,0:T(8,128)}, u32[]{:S(2)}, u32[]{:S(2)}) collective-permute-start(f32[2,256,384]{1,2,0:T(8,128)} %get-tuple-element.541), channel_id=1, source_target_pairs={{0,24},{8,32},{16,40},{24,48},{32,56},{40,64},{48,72},{56,80},{64,... | collective-permute-start | bytes 2359304 | tf_op jit(solution)/shard_map/ppermute | solution.py:17
  247.7 406.1 %collective-permute-start.14 = (f32[2,256,384]{1,2,0:T(8,128)}, f32[2,256,384]{1,2,0:T(8,128)}, u32[]{:S(2)}, u32[]{:S(2)}) collective-permute-start(f32[2,256,384]{1,2,0:T(8,128)} %get-tuple-element.543), channel_id=1, source_target_pairs={{0,32},{8,40},{16,48},{24,56},{32,64},{40,72},{48,80},{56,88},{64,... | collective-permute-start | bytes 2359304 | tf_op jit(solution)/shard_map/ppermute | solution.py:17
  251.7 402.1 %collective-permute-start.15 = (f32[2,256,384]{1,2,0:T(8,128)}, f32[2,256,384]{1,2,0:T(8,128)}, u32[]{:S(2)}, u32[]{:S(2)}) collective-permute-start(f32[2,256,384]{1,2,0:T(8,128)} %get-tuple-element.542), channel_id=1, source_target_pairs={{0,40},{8,48},{16,56},{24,64},{32,72},{40,80},{48,88},{56,96},{64,... | collective-permute-start | bytes 2359304 | tf_op jit(solution)/shard_map/ppermute | solution.py:17
  255.9 397.9 %copy-start.2 = (f32[2,256,384]{1,2,0:T(8,128)}, f32[2,256,384]{1,2,0:T(8,128)S(1)}, u32[]{:S(2)}) copy-start(f32[2,256,384]{1,2,0:T(8,128)S(1)} %collective-permute-done.11) | copy-start | bytes 2359300
  255.9 397.9 %collective-permute-start.8 = (f32[2,256,384]{1,2,0:T(8,128)S(1)}, f32[2,256,384]{1,2,0:T(8,128)}, u32[]{:S(2)}, u32[]{:S(2)}) collective-permute-start(f32[2,256,384]{1,2,0:T(8,128)S(1)} %get-tuple-element.536), channel_id=1, source_target_pairs={{40,0},{48,8},{56,16},{64,24},{72,32},{80,40},{88,48},{96,56},{104... | collective-permute-start | bytes 2359304 | tf_op jit(solution)/shard_map/ppermute | solution.py:17
  257.2 396.6 %collective-permute-start.9 = (f32[2,256,384]{1,2,0:T(8,128)S(1)}, f32[2,256,384]{1,2,0:T(8,128)}, u32[]{:S(2)}, u32[]{:S(2)}) collective-permute-start(f32[2,256,384]{1,2,0:T(8,128)S(1)} %get-tuple-element.537), channel_id=1, source_target_pairs={{32,0},{40,8},{48,16},{56,24},{64,32},{72,40},{80,48},{88,56},{96,... | collective-permute-start | bytes 2359304 | tf_op jit(solution)/shard_map/ppermute | solution.py:17
  653.8 5.3 copy-start.1
Sparse Core Ops, SparseCore 0:
  33.2 57.1 all-gather.1
  233.5 416.7 all-reduce.4
where the time goes:
time: 670 us; the launch traced here: 666 us
  waiting for transfers between devices  469 us (70%)
  starting transfers between devices  63.6 us (9%)
  local copies, waits for them, and re-layouts  54.2 us (8%)
  matrix products  30.6 us (5%)
  other arithmetic  25.1 us (4%)
  between operations  15.2 us (2%)
  loops' own time  8.09 us (1%)
    unnamed x3, waiting for transfers between devices  390 us
    ppermute x16, waiting for transfers between devices, from_behind(): return lax.ppermute(block, axis, route)  79.4 us
    ppermute x16, starting transfers between devices, from_behind(): return lax.ppermute(block, axis, route)  63.5 us
  transfers between devices with their start and end apart: 18, of which 6 were waited for; matrix products, arithmetic and copies ran while one was open for 4% of the time, Pallas kernels for 0%

commit v1 on v0

v1 whole, which is shorter than its diff:
```python
import functools
import math

import jax
import jax.numpy as jnp
from jax import lax
from jax.experimental import pallas as pl
from jax.experimental.pallas import tpu as pltpu
from jax.sharding import PartitionSpec as P

DH = 128
TOK = 256
TEXT = 256
ROWS = 4
SPAN = 3 * TOK
QALL = ROWS * TOK
MSG = 3 * TOK + 16
INV_ROOT = DH ** (-0.5)
LOG2E = math.log2(math.e)
F32 = jnp.float32
BF16 = jnp.bfloat16
ANY = pl.BlockSpec(memory_space=pl.ANY)
VMEM = pl.BlockSpec(memory_space=pltpu.VMEM)
SMEM = pl.BlockSpec(memory_space=pltpu.SMEM)


def params():
    return pltpu.CompilerParams(vmem_limit_bytes=40 * 1024 * 1024)


def sds(shape, dtype):
    return jax.ShapeDtypeStruct(shape, dtype)


def dot_nt(a, b):
    return lax.dot_general(a, b, (((1,), (1,)), ((), ())), preferred_element_type=F32)


def dot_nn(a, b):
    return lax.dot_general(a, b, (((1,), (0,)), ((), ())), preferred_element_type=F32)


def dot_tn(a, b):
    return lax.dot_general(a, b, (((0,), (0,)), ((), ())), preferred_element_type=F32)


def out_pairs(phase):
    pairs = []
    for y in range(4):
        for zt in range(2):
            for h in range(4):
                head = (h - phase) % 4
                if head < 3:
                    pairs.append((y * 8 + zt * 4 + h, y * 8 + head * 2 + zt))
    return pairs


def back_pairs(phase):
    return [(b, a) for a, b in out_pairs(phase)]


def core_pairs():
    return [(s, s ^ 1) for s in range(32) if (s // 2) % 4 < 3]


def time_pairs():
    pairs = []
    for s in range(32):
        y, z_hi, c = s // 8, (s // 2) % 4, s % 2
        if z_hi < 3:
            other = y + 1 if c else y - 1
            if 0 <= other < 4:
                pairs.append((s, other * 8 + z_hi * 2 + 1 - c))
    return pairs


def head_pairs(dx, dz):
    return [(g, ((g // 4 + dz) % 2) * 4 + (g % 4 + dx) % 4) for g in range(8)]


def start_all(copies):
    for one in copies:
        one.start()


def wait_all(copies):
    for one in copies:
        one.wait()


def home_height():
    return lax.rem(lax.axis_index("seq"), 4)


def work_chip():
    return lax.rem(lax.div(lax.axis_index("seq"), 2), 4)


def pack_kernel(q_ref, k_ref, v_ref, o0, o1, o2, o3, sem):
    h = home_height()
    copies = []
    for phase, out in enumerate((o0, o1, o2, o3)):
        head = jnp.minimum(lax.rem(h - phase + 4, 4), 2)
        columns = pl.ds(pl.multiple_of(head * DH, DH), DH)
        for which, src in enumerate((q_ref, k_ref, v_ref)):
            copies.append(
                pltpu.make_async_copy(src.at[:, columns], out.at[which], sem.at[phase * 3 + which])
            )
    start_all(copies)
    wait_all(copies)


def project_kernel(c0, c1, c2, c3, c4, c5, c6, c7, w_ref, o0, o1, o2, o3):
    chunks = (c0, c1, c2, c3, c4, c5, c6, c7)
    g = lax.axis_index("head")
    h = home_height()
    gz, gx = lax.div(g, 4), lax.rem(g, 4)
    width = c0.shape[1]
    for phase, out in enumerate((o0, o1, o2, o3)):
        head = jnp.minimum(lax.rem(h - phase + 4, 4), 2)
        rows = pl.ds(pl.multiple_of(head * DH, DH), DH)
        total = None
        for which, chunk in enumerate(chunks):
            dz, dx = which // 4, which % 4
            src = lax.rem(gz + dz, 2) * 4 + lax.rem(gx - dx + 4, 4)
            columns = pl.ds(pl.multiple_of(src * width, width), width)
            term = dot_nt(chunk[...], w_ref[rows, columns])
            total = term if total is None else total + term
        out[...] = total.astype(BF16)


def window(ext_ref, chip):
    head = jnp.minimum(chip, 2)
    reach_t, reach_h, reach_w = ext_ref[head, 0], ext_ref[head, 1], ext_ref[head, 2]
    s = lax.axis_index("seq")
    y, c = lax.div(s, 8), lax.rem(s, 2)
    near = reach_t >= 1
    outside = ((y == 0) & (c == 0)) | ((y == 3) & (c == 1))
    return (True, near, near & jnp.logical_not(outside)), reach_h, reach_w >= 1


def span_bias(block_ok, reach_h, wide, key_h, first_h):
    lane = lax.broadcasted_iota(jnp.int32, (1, TOK), 1)
    left = lane < TOK // 2
    top, low = [], []
    for j in range(3):
        ok = jnp.abs(first_h + j - key_h) <= reach_h
        if block_ok is not True:
            ok = ok & block_ok
        same = jnp.where(ok, 0.0, -jnp.inf).astype(F32)
        cross = jnp.where(ok & wide, 0.0, -jnp.inf).astype(F32)
        top.append(jnp.where(left, same, cross))
        low.append(jnp.where(left, cross, same))
    return jnp.concatenate(top, 1), jnp.concatenate(low, 1)


def first_height(key_h):
    return jnp.clip(key_h - 1, 0, 1)


def fold(x, how):
    return how(x.reshape(x.shape[0] // 8, 8, x.shape[1]), 0)


def stats_kernel(
    ext_ref, m0, m1, m2, m3, core_kv, time_kv, tk_ref, tv_ref, tb_ref,
    lse_ref, mean_ref,
    kb, vb, qb, sb, st, run, sem,
):
    chip = work_chip()
    copies = []
    for phase, msg in enumerate((m0, m1, m2, m3)):
        h = lax.rem(chip + phase, 4)
        copies += [
            pltpu.make_async_copy(msg.at[0], qb.at[pl.ds(pl.multiple_of(h * TOK, TOK), TOK)], sem.at[phase * 7]),
            pltpu.make_async_copy(msg.at[1], kb.at[h], sem.at[phase * 7 + 1]),
            pltpu.make_async_copy(msg.at[2], vb.at[h], sem.at[phase * 7 + 2]),
            pltpu.make_async_copy(core_kv.at[phase, 0], kb.at[4 + h], sem.at[phase * 7 + 3]),
            pltpu.make_async_copy(core_kv.at[phase, 1], vb.at[4 + h], sem.at[phase * 7 + 4]),
            pltpu.make_async_copy(time_kv.at[phase, 0], kb.at[8 + h], sem.at[phase * 7 + 5]),
            pltpu.make_async_copy(time_kv.at[phase, 1], vb.at[8 + h], sem.at[phase * 7 + 6]),
        ]
    start_all(copies)
    wait_all(copies)
    block_ok, reach_h, wide = window(ext_ref, chip)
    head = jnp.minimum(chip, 2)
    columns = pl.ds(pl.multiple_of(head * DH, DH), DH)
    factor = INV_ROOT * LOG2E

    text = dot_nt(tk_ref[:, columns], qb[...]) * factor + tb_ref[...]
    st[...] = text
    run[...] = fold(text, jnp.max)

    for part in range(3):

        def first(key_h, carry, part=part):
            h0 = first_height(key_h)
            rows = pl.ds(pl.multiple_of(h0 * TOK, TOK), SPAN)
            top, low = span_bias(block_ok[part], reach_h, wide, key_h, h0)
            s = dot_nt(kb[part * 4 + key_h], qb[rows, :]) * factor
            a, b = s[: TOK // 2] + top, s[TOK // 2 :] + low
            sb[part * 4 + key_h, : TOK // 2] = a
            sb[part * 4 + key_h, TOK // 2 :] = b
            run[:, rows] = jnp.maximum(run[:, rows], jnp.maximum(fold(a, jnp.max), fold(b, jnp.max)))
            return carry

        lax.fori_loop(0, 4, first, 0)

    top_score = jnp.max(run[...], 0, keepdims=True)
    lse_ref[...] = top_score
    weights = jnp.exp2(st[...] - top_score)
    run[...] = fold(weights, jnp.sum)
    mean_ref[...] = dot_tn(tv_ref[:, columns], weights.astype(BF16))

    def second(block, carry):
        key_h = lax.rem(block, 4)
        rows = pl.ds(pl.multiple_of(first_height(key_h) * TOK, TOK), SPAN)
        weights = jnp.exp2(sb[block] - lse_ref[:, rows])
        run[:, rows] += fold(weights, jnp.sum)
        mean_ref[:, rows] += dot_tn(vb[block], weights.astype(BF16))
        return carry

    lax.fori_loop(0, 12, second, 0)
    total = jnp.sum(run[...], 0, keepdims=True)
    lse_ref[...] = top_score + jnp.log2(total)
    mean_ref[...] = mean_ref[...] / total


def block_terms(keys, values, query, grad, bias, delta, factor):
    s = dot_nt(keys, query) * factor
    if isinstance(bias, tuple):
        top, low = bias
        half = TOK // 2
        probs = jnp.concatenate([jnp.exp2(s[:half] + top), jnp.exp2(s[half:] + low)], 0)
    else:
        probs = jnp.exp2(s + bias)
    dprobs = dot_nt(values, grad)
    dscores = (probs * (dprobs - delta)).astype(BF16)
    return probs.astype(BF16), dscores


def grad_kernel(part, m_refs, g_refs, kv_ref, ext_ref, lse_ref, delta_ref, dq_in, out_ref, dq_out, kb, vb, qb, gb, sem):
    chip = work_chip()
    copies = []
    for phase in range(4):
        h = lax.rem(chip + phase, 4)
        rows = pl.ds(pl.multiple_of(h * TOK, TOK), TOK)
        msg = m_refs[phase]
        key_src = msg.at[1] if part == 0 else kv_ref.at[phase, 0]
        value_src = msg.at[2] if part == 0 else kv_ref.at[phase, 1]
        copies += [
            pltpu.make_async_copy(msg.at[0], qb.at[rows], sem.at[phase * 4]),
            pltpu.make_async_copy(g_refs[phase], gb.at[rows], sem.at[phase * 4 + 1]),
            pltpu.make_async_copy(key_src, kb.at[h], sem.at[phase * 4 + 2]),
            pltpu.make_async_copy(value_src, vb.at[h], sem.at[phase * 4 + 3]),
        ]
    start_all(copies)
    wait_all(copies)
    if dq_in is None:
        dq_out[...] = jnp.zeros_like(dq_out)
    else:
        dq_out[...] = dq_in[...]
    block_ok, reach_h, wide = window(ext_ref, chip)
    factor = INV_ROOT * LOG2E

    def body(key_h, carry):
        h0 = first_height(key_h)
        rows = pl.ds(pl.multiple_of(h0 * TOK, TOK), SPAN)
        top, low = span_bias(block_ok[part], reach_h, wide, key_h, h0)
        lse = lse_ref[:, rows]
        query, grad, keys = qb[rows, :], gb[rows, :], kb[key_h]
        probs, dscores = block_terms(
            keys, vb[key_h], query, grad, (top - lse, low - lse), delta_ref[:, rows], factor
        )
        out_ref[key_h, 0] = (dot_nn(dscores, query) * INV_ROOT).astype(out_ref.dtype)
        out_ref[key_h, 1] = dot_nn(probs, grad).astype(out_ref.dtype)
        dq_out[:, rows] += dot_tn(keys, dscores)
        return carry

    lax.fori_loop(0, 4, body, 0)


def time_grad_kernel(
    ext_ref, m0, m1, m2, m3, g0, g1, g2, g3, kv_ref, lse_ref, mean_ref, tk_ref, tv_ref, tb_ref,
    out_ref, dq_ref, delta_ref, text_ref,
    kb, vb, qb, gb, sem,
):
    chip = work_chip()
    copies = []
    for phase, src in enumerate((g0, g1, g2, g3)):
        h = lax.rem(chip + phase, 4)
        rows = pl.ds(pl.multiple_of(h * TOK, TOK), TOK)
        copies.append(pltpu.make_async_copy(src, gb.at[rows], sem.at[phase]))
    start_all(copies)
    wait_all(copies)
    delta_ref[...] = jnp.sum(gb[...].astype(F32).T * mean_ref[...], 0, keepdims=True)
    grad_kernel(
        2, (m0, m1, m2, m3), (g0, g1, g2, g3), kv_ref, ext_ref, lse_ref, delta_ref, None,
        out_ref, dq_ref, kb, vb, qb, gb, sem,
    )
    head = jnp.minimum(chip, 2)
    columns = pl.ds(pl.multiple_of(head * DH, DH), DH)
    keys = tk_ref[:, columns]
    probs, dscores = block_terms(
        keys, tv_ref[:, columns], qb[...], gb[...], tb_ref[...] - lse_ref[...], delta_ref[...],
        INV_ROOT * LOG2E,
    )
    dq_ref[...] += dot_tn(keys, dscores)
    text_ref[:, :DH] = (dot_nn(dscores, qb[...]) * INV_ROOT).astype(BF16)
    text_ref[:, DH:] = dot_nn(probs, gb[...]).astype(BF16)


def core_grad_kernel(
    ext_ref, m0, m1, m2, m3, g0, g1, g2, g3, kv_ref, lse_ref, delta_ref, dq_in,
    out_ref, dq_ref, kb, vb, qb, gb, sem,
):
    grad_kernel(
        1, (m0, m1, m2, m3), (g0, g1, g2, g3), kv_ref, ext_ref, lse_ref, delta_ref, dq_in,
        out_ref, dq_ref, kb, vb, qb, gb, sem,
    )


def own_grad_kernel(
    ext_ref, m0, m1, m2, m3, g0, g1, g2, g3, lse_ref, delta_ref, dq_in,
    out_ref, dq_final, dq_run, kb, vb, qb, gb, sem,
):
    grad_kernel(
        0, (m0, m1, m2, m3), (g0, g1, g2, g3), None, ext_ref, lse_ref, delta_ref, dq_in,
        out_ref, dq_run, kb, vb, qb, gb, sem,
    )
    for h in range(ROWS):
        dq_final[h] = (dq_run[:, h * TOK : (h + 1) * TOK].T * INV_ROOT).astype(BF16)


def combine_kernel(own, core, time, dq, text, o0, o1, o2, o3, text_sum):
    chip = work_chip()
    text_sum[...] = jnp.sum(text[...].astype(F32), 0)
    for phase, out in enumerate((o0, o1, o2, o3)):
        h = lax.rem(chip + phase, 4)
        out[:TOK] = dq[h]
        for which in range(2):
            total = own[h, which] + core[h, which].astype(F32) + time[h, which].astype(F32)
            out[(1 + which) * TOK : (2 + which) * TOK] = total.astype(BF16)
        share = text_sum[pl.ds(pl.multiple_of(h * 8, 8), 8), :]
        out[3 * TOK :] = jnp.concatenate([share[:, :DH], share[:, DH:]], 0).astype(BF16)


def unpack_kernel(r0, r1, r2, r3, dq, dk, dv, tk, tv, buf, sem):
    h = home_height()
    copies = []
    for phase, src in enumerate((r0, r1, r2, r3)):
        head = lax.rem(h - phase + 4, 4)
        copies.append(pltpu.make_async_copy(src, buf.at[head], sem.at[phase]))
    start_all(copies)
    wait_all(copies)
    for head in range(3):
        columns = slice(head * DH, (head + 1) * DH)
        dq[:, columns] = buf[head, :TOK]
        dk[:, columns] = buf[head, TOK : 2 * TOK].astype(F32)
        dv[:, columns] = buf[head, 2 * TOK : 3 * TOK].astype(F32)
        share = buf[head, 3 * TOK :].astype(F32)
        tk[:, columns] = share[:8]
        tv[:, columns] = share[8:]


def per_device(queries, keys, values, layer_grad, out_weight, text_keys, text_values, extents, text_mask):
    block = sds((TOK, DH), BF16)
    text_bias = jnp.where(text_mask == 1, 0.0, -jnp.inf).astype(F32)[:, None]

    packed = pl.pallas_call(
        pack_kernel,
        in_specs=[ANY] * 3,
        out_specs=[ANY] * 4,
        out_shape=[sds((3, TOK, DH), BF16)] * 4,
        scratch_shapes=[pltpu.SemaphoreType.DMA((12,))],
        compiler_params=params(),
        name="pack_heads",
    )(queries, keys, values)

    chunks = [
        layer_grad if which == 0 else lax.ppermute(layer_grad, "head", head_pairs(which % 4, which // 4))
        for which in range(8)
    ]
    msgs = [lax.ppermute(one, "seq", out_pairs(phase)) for phase, one in enumerate(packed)]
    kv = jnp.stack([one[1:] for one in msgs])
    core_kv = lax.ppermute(kv, "seq", core_pairs())
    time_kv = lax.ppermute(kv, "seq", time_pairs())

    grads = pl.pallas_call(
        project_kernel,
        in_specs=[VMEM] * 9,
        out_specs=[VMEM] * 4,
        out_shape=[block] * 4,
        compiler_params=params(),
        name="project",
    )(*chunks, out_weight)
    grads = [lax.ppermute(one, "seq", out_pairs(phase)) for phase, one in enumerate(grads)]

    flops_block = 2 * TOK * SPAN * DH
    lse, mean = pl.pallas_call(
        stats_kernel,
        in_specs=[SMEM] + [ANY] * 6 + [VMEM] * 3,
        out_specs=[VMEM] * 2,
        out_shape=[sds((1, QALL), F32), sds((DH, QALL), F32)],
        scratch_shapes=[
            pltpu.VMEM((12, TOK, DH), BF16),
            pltpu.VMEM((12, TOK, DH), BF16),
            pltpu.VMEM((QALL, DH), BF16),
            pltpu.VMEM((12, TOK, SPAN), F32),
            pltpu.VMEM((TEXT, QALL), F32),
            pltpu.VMEM((8, QALL), F32),
            pltpu.SemaphoreType.DMA((28,)),
        ],
        compiler_params=params(),
        cost_estimate=pl.CostEstimate(flops=26 * flops_block, bytes_accessed=3_000_000, transcendentals=12 * TOK * SPAN),
        name="softmax_stats",
    )(extents, *msgs, core_kv, time_kv, text_keys, text_values, text_bias)

    scratch = [
        pltpu.VMEM((4, TOK, DH), BF16),
        pltpu.VMEM((4, TOK, DH), BF16),
        pltpu.VMEM((QALL, DH), BF16),
        pltpu.VMEM((QALL, DH), BF16),
        pltpu.SemaphoreType.DMA((16,)),
    ]
    cost = pl.CostEstimate(flops=20 * flops_block, bytes_accessed=2_000_000, transcendentals=4 * TOK * SPAN)
    half_sum = sds((4, 2, TOK, DH), BF16)
    dq_run = sds((DH, QALL), F32)
    time_part, dq, delta, text_part = pl.pallas_call(
        time_grad_kernel,
        in_specs=[SMEM] + [ANY] * 9 + [VMEM] * 5,
        out_specs=[VMEM] * 4,
        out_shape=[half_sum, dq_run, sds((1, QALL), F32), sds((TEXT, 2 * DH), BF16)],
        scratch_shapes=scratch,
        compiler_params=params(),
        cost_estimate=cost,
        name="time_and_text_grads",
    )(extents, *msgs, *grads, time_kv, lse, mean, text_keys, text_values, text_bias)
    time_back = lax.ppermute(time_part, "seq", time_pairs())
    groups = [[y * 8 + z_hi * 2 + c for y in range(4) for c in range(2)] for z_hi in range(4)]
    text_back = lax.all_to_all(
        text_part.reshape(8, TEXT // 8, 2 * DH), "seq", 0, 0, axis_index_groups=groups
    )

    core_part, dq = pl.pallas_call(
        core_grad_kernel,
        in_specs=[SMEM] + [ANY] * 9 + [VMEM] * 3,
        out_specs=[VMEM] * 2,
        out_shape=[half_sum, dq_run],
        scratch_shapes=scratch,
        compiler_params=params(),
        cost_estimate=cost,
        name="core_grads",
    )(extents, *msgs, *grads, core_kv, lse, delta, dq)
    core_back = lax.ppermute(core_part, "seq", core_pairs())

    own_part, dq = pl.pallas_call(
        own_grad_kernel,
        in_specs=[SMEM] + [ANY] * 8 + [VMEM] * 3,
        out_specs=[VMEM] * 2,
        out_shape=[sds((4, 2, TOK, DH), F32), sds((4, TOK, DH), BF16)],
        scratch_shapes=[pltpu.VMEM((DH, QALL), F32)] + scratch,
        compiler_params=params(),
        cost_estimate=cost,
        name="own_grads",
    )(extents, *msgs, *grads, lse, delta, dq)

    results = pl.pallas_call(
        combine_kernel,
        in_specs=[VMEM] * 5,
        out_specs=[VMEM] * 4,
        out_shape=[sds((MSG, DH), BF16)] * 4,
        scratch_shapes=[pltpu.VMEM((TEXT // 8, 2 * DH), F32)],
        compiler_params=params(),
        name="combine",
    )(own_part, core_back, time_back, dq, text_back)
    results = [lax.ppermute(one, "seq", back_pairs(phase)) for phase, one in enumerate(results)]

    width = 3 * DH
    return pl.pallas_call(
        unpack_kernel,
        in_specs=[ANY] * 4,
        out_specs=[VMEM] * 5,
        out_shape=[
            sds((TOK, width), BF16),
            sds((TOK, width), F32),
            sds((TOK, width), F32),
            sds((8, width), F32),
            sds((8, width), F32),
        ],
        scratch_shapes=[pltpu.VMEM((4, MSG, DH), BF16), pltpu.SemaphoreType.DMA((4,))],
        compiler_params=params(),
        name="unpack",
    )(*results)


def solution(mesh):
    return jax.shard_map(
        per_device,
        mesh=mesh,
        in_specs=(
            P("seq", "head"),
            P("seq", "head"),
            P("seq", "head"),
            P("seq", "head"),
            P("head", None),
            P(None, "head"),
            P(None, "head"),
            P("head", None),
            P(),
        ),
        out_specs=(P("seq", "head"),) * 5,
        check_vma=False,
    )
```

time: 670 us -> 152 us (0.23)
  the two profiles are of different devices: /device:TPU:33 before, /device:TPU:1 now
where the time goes in v1:
time: 152 us; the launch traced here: 151 us
  starting transfers between devices  73.9 us (49%)
  waiting for transfers between devices  33.7 us (22%)
  Pallas kernels  33.5 us (22%)
  local copies, waits for them, and re-layouts  8.33 us (5%)
    ppermute x8, starting transfers between devices, per_device(): lax.ppermute(one, 'seq', out_pairs(phase))  33.8 us
    ppermute x4, waiting for transfers between devices, per_device(): lax.ppermute(one, 'seq', back_pairs(phase))  18.3 us
    ppermute x7, starting transfers between devices, per_device(): lax.ppermute(layer_grad, 'head', head_pairs(which % 4, which // 4))  16.1 us
    ppermute x7, waiting for transfers between devices, per_device(): lax.ppermute(layer_grad, 'head', head_pairs(which % 4, which // 4))  10.8 us
    pallas_call x1, Pallas kernels, per_device(): pl.pallas_call(stats_kernel, in_specs=[SMEM] + [ANY] * 6 + [VMEM] * 3, ou...  10.1 us
    ppermute x4, starting transfers between devices, per_device(): lax.ppermute(one, 'seq', back_pairs(phase))  8.96 us
    unnamed x48, local copies, waits for them, and re-layouts  7.49 us
    pallas_call x1, Pallas kernels, per_device(): pl.pallas_call(time_grad_kernel, in_specs=[SMEM] + [ANY] * 9 + [VMEM] * 5...  7.14 us
  transfers between devices with their start and end apart: 24, of which 9 were waited for; matrix products, arithmetic and copies ran while one was open for 1% of the time, Pallas kernels for 12%

profile of v1, /device:TPU:1, one launch (start us, length us, event | category | flops | bytes accessed | tf_op | source)
XLA Modules:
  0.0 151.4 jit_solution(10056806213777265560)
XLA Ops:
  0.7 1.1 copy-done.1
  1.7 0.9 copy-done.2
  2.6 0.9 copy-done.3
  3.6 0.3 pack_heads.1
  3.9 6.3 %collective-permute-start = (bf16[3,256,128]{2,1,0:T(8,128)(2,1)S(1)}, bf16[3,256,128]{2,1,0:T(8,128)(2,1)S(1)}, u32[]{:S(2)}, u32[]{:S(2)}) collective-permute-start(bf16[3,256,128]{2,1,0:T(8,128)(2,1)S(1)} %get-tuple-element.27), channel_id=1, source_target_pairs={{0,0},{8,16},{16,32},{32,8},{40,24},{48,40},{64,64},{72,80},{80,96... | collective-permute-start | bytes 589832 | tf_op jit(solution)/shard_map/ppermute | solution.py:384
  10.2 4.2 %collective-permute-start.9 = (bf16[256,384]{1,0:T(8,128)(2,1)}, bf16[256,384]{1,0:T(8,128)(2,1)S(1)}, u32[]{:S(2)}, u32[]{:S(2)}) collective-permute-start(bf16[256,384]{1,0:T(8,128)(2,1)} %c0.1), channel_id=1, source_target_pairs={{0,6},{1,7},{2,4},{3,5},{4,2},{5,3},{6,0},{7,1},{8,14},{9,15},{10,... | collective-permute-start | bytes 589832 | tf_op jit(solution)/shard_map/ppermute | solution.py:381
  14.3 1.9 %collective-permute-start.1 = (bf16[3,256,128]{2,1,0:T(8,128)(2,1)S(1)}, bf16[3,256,128]{2,1,0:T(8,128)(2,1)S(1)}, u32[]{:S(2)}, u32[]{:S(2)}) collective-permute-start(bf16[3,256,128]{2,1,0:T(8,128)(2,1)S(1)} %get-tuple-element.28), channel_id=1, source_target_pairs={{8,0},{16,16},{24,32},{40,8},{48,24},{56,40},{72,64},{80,80},{88,9... | collective-permute-start | bytes 589832 | tf_op jit(solution)/shard_map/ppermute | solution.py:384
  16.3 1.3 collective-permute-start.2
  17.6 8.3 %collective-permute-start.3 = (bf16[3,256,128]{2,1,0:T(8,128)(2,1)S(1)}, bf16[3,256,128]{2,1,0:T(8,128)(2,1)S(1)}, u32[]{:S(2)}, u32[]{:S(2)}) collective-permute-start(bf16[3,256,128]{2,1,0:T(8,128)(2,1)S(1)} %get-tuple-element.30), channel_id=1, source_target_pairs={{0,16},{8,32},{24,0},{32,24},{40,40},{56,8},{64,80},{72,96},{88,64... | collective-permute-start | bytes 589832 | tf_op jit(solution)/shard_map/ppermute | solution.py:384
  25.9 0.0 copy-start.6
  25.9 0.7 copy-done.6
  26.6 2.4 %collective-permute-done.1.m1 = bf16[3,256,128]{2,1,0:T(8,128)(2,1)S(1)} collective-permute-done((bf16[3,256,128]{2,1,0:T(8,128)(2,1)S(1)}, bf16[3,256,128]{2,1,0:T(8,128)(2,1)S(1)}, u32[]{:S(2)}, u32[]{:S(2)}) %collective-permute-start.1) | collective-permute-done | bytes 196640 | tf_op jit(solution)/shard_map/ppermute | solution.py:384
  28.9 0.0 copy-start.9
  28.9 0.7 copy-done.9
  29.6 0.0 copy-start.12
  29.6 0.7 copy-done.12
  30.3 1.9 %collective-permute-done.3.m3 = bf16[3,256,128]{2,1,0:T(8,128)(2,1)S(1)} collective-permute-done((bf16[3,256,128]{2,1,0:T(8,128)(2,1)S(1)}, bf16[3,256,128]{2,1,0:T(8,128)(2,1)S(1)}, u32[]{:S(2)}, u32[]{:S(2)}) %collective-permute-start.3) | collective-permute-done | bytes 196640 | tf_op jit(solution)/shard_map/ppermute | solution.py:384
  32.3 0.7 copy-done.15
  32.9 0.9 pad_maximum_fusion
  33.8 2.6 %collective-permute-start.16 = (bf16[4,2,256,128]{3,2,1,0:T(8,128)(2,1)}, bf16[4,2,256,128]{3,2,1,0:T(8,128)(2,1)}, u32[]{:S(2)}, u32[]{:S(2)}) collective-permute-start(bf16[4,2,256,128]{3,2,1,0:T(8,128)(2,1)} %pad_maximum_fusion), channel_id=1, source_target_pairs={{8,64},{24,80},{40,96},{64,8},{72,128},{80,24},{88,144},{96,40},{1... | collective-permute-start | bytes 1572872 | tf_op jit(solution)/shard_map/ppermute | solution.py:387
  36.4 1.9 %collective-permute-start.15 = (bf16[4,2,256,128]{3,2,1,0:T(8,128)(2,1)}, bf16[4,2,256,128]{3,2,1,0:T(8,128)(2,1)}, u32[]{:S(2)}, u32[]{:S(2)}) collective-permute-start(bf16[4,2,256,128]{3,2,1,0:T(8,128)(2,1)} %pad_maximum_fusion), channel_id=1, source_target_pairs={{0,8},{8,0},{16,24},{24,16},{32,40},{40,32},{64,72},{72,64},{80,88... | collective-permute-start | bytes 1572872 | tf_op jit(solution)/shard_map/ppermute | solution.py:386
  38.4 5.5 %collective-permute-start.8 = (bf16[256,384]{1,0:T(8,128)(2,1)S(1)}, bf16[256,384]{1,0:T(8,128)(2,1)S(1)}, u32[]{:S(2)}, u32[]{:S(2)}) collective-permute-start(bf16[256,384]{1,0:T(8,128)(2,1)S(1)} %copy-done.4), channel_id=1, source_target_pairs={{0,5},{1,6},{2,7},{3,4},{4,1},{5,2},{6,3},{7,0},{8,13},{9,14},{10,... | collective-permute-start | bytes 589832 | tf_op jit(solution)/shard_map/ppermute | solution.py:381
  43.8 0.0 collective-permute-start.7
  43.9 0.0 collective-permute-done.9.c6
  43.9 2.2 %collective-permute-start.6 = (bf16[256,384]{1,0:T(8,128)(2,1)S(1)}, bf16[256,384]{1,0:T(8,128)(2,1)S(1)}, u32[]{:S(2)}, u32[]{:S(2)}) collective-permute-start(bf16[256,384]{1,0:T(8,128)(2,1)S(1)} %copy-done.4), channel_id=1, source_target_pairs={{0,3},{1,0},{2,1},{3,2},{4,7},{5,4},{6,5},{7,6},{8,11},{9,8},{10,9... | collective-permute-start | bytes 589832 | tf_op jit(solution)/shard_map/ppermute | solution.py:381
  46.1 3.8 %collective-permute-done.8.c5 = bf16[256,384]{1,0:T(8,128)(2,1)S(1)} collective-permute-done((bf16[256,384]{1,0:T(8,128)(2,1)S(1)}, bf16[256,384]{1,0:T(8,128)(2,1)S(1)}, u32[]{:S(2)}, u32[]{:S(2)}) %collective-permute-start.8) | collective-permute-done | bytes 196640 | tf_op jit(solution)/shard_map/ppermute | solution.py:381
  49.9 0.5 collective-permute-start.5
  50.5 2.3 %collective-permute-done.7.c4 = bf16[256,384]{1,0:T(8,128)(2,1)S(1)} collective-permute-done((bf16[256,384]{1,0:T(8,128)(2,1)S(1)}, bf16[256,384]{1,0:T(8,128)(2,1)S(1)}, u32[]{:S(2)}, u32[]{:S(2)}) %collective-permute-start.7) | collective-permute-done | bytes 196640 | tf_op jit(solution)/shard_map/ppermute | solution.py:381
  52.7 0.4 collective-permute-start.4
  53.2 0.0 collective-permute-done.6.c3
  53.2 3.2 %collective-permute-start.10 = (bf16[256,384]{1,0:T(8,128)(2,1)S(1)}, bf16[256,384]{1,0:T(8,128)(2,1)}, u32[]{:S(2)}, u32[]{:S(2)}) collective-permute-start(bf16[256,384]{1,0:T(8,128)(2,1)S(1)} %copy-done.4), channel_id=1, source_target_pairs={{0,7},{1,4},{2,5},{3,6},{4,3},{5,0},{6,1},{7,2},{8,15},{9,12},{10,... | collective-permute-start | bytes 589832 | tf_op jit(solution)/shard_map/ppermute | solution.py:381
  56.4 0.8 copy.14.tb_ref
  57.3 0.0 copy-start.18
  57.3 0.0 copy-start.19
  57.3 0.0 collective-permute-done.5.c2
  57.3 4.7 %collective-permute-done.4.c1 = bf16[256,384]{1,0:T(8,128)(2,1)} collective-permute-done((bf16[256,384]{1,0:T(8,128)(2,1)S(1)}, bf16[256,384]{1,0:T(8,128)(2,1)}, u32[]{:S(2)}, u32[]{:S(2)}) %collective-permute-start.4) | collective-permute-done | bytes 196640 | tf_op jit(solution)/shard_map/ppermute | solution.py:381
  62.0 0.0 collective-permute-done.10.c7
  62.0 2.9 %project.1 = (bf16[256,128]{1,0:T(8,128)(2,1)S(1)}, bf16[256,128]{1,0:T(8,128)(2,1)S(1)}, bf16[256,128]{1,0:T(8,128)(2,1)S(1)}, bf16[256,128]{1,0:T(8,128)(2,1)S(1)}) custom-call(bf16[256,384]{1,0:T(8,128)(2,1)S(1)} %copy-done.4, bf16[256,384]{1,0:T(8,128)(2,1)} %collective-permute-done.4.c1, bf16[256,384]{1,0:T(8,128)(2,1)S(1)} %collective-permute-done.5.c2, ...), custom_call_target="tpu_custom_call" | custom-call | tf_op jit(solution)/shard_map/project/pallas_call | solution.py:389
  64.8 4.5 %collective-permute-start.11 = (bf16[256,128]{1,0:T(8,128)(2,1)S(1)}, bf16[256,128]{1,0:T(8,128)(2,1)S(1)}, u32[]{:S(2)}, u32[]{:S(2)}) collective-permute-start(bf16[256,128]{1,0:T(8,128)(2,1)S(1)} %get-tuple-element.31), channel_id=1, source_target_pairs={{0,0},{8,16},{16,32},{32,8},{40,24},{48,40},{64,64},{72,80},{80,96... | collective-permute-start | bytes 196616 | tf_op jit(solution)/shard_map/ppermute | solution.py:397
  69.4 1.9 %collective-permute-start.12 = (bf16[256,128]{1,0:T(8,128)(2,1)S(1)}, bf16[256,128]{1,0:T(8,128)(2,1)S(1)}, u32[]{:S(2)}, u32[]{:S(2)}) collective-permute-start(bf16[256,128]{1,0:T(8,128)(2,1)S(1)} %get-tuple-element.32), channel_id=1, source_target_pairs={{8,0},{16,16},{24,32},{40,8},{48,24},{56,40},{72,64},{80,80},{88,9... | collective-permute-start | bytes 196616 | tf_op jit(solution)/shard_map/ppermute | solution.py:397
  71.3 1.3 collective-permute-start.13
  72.6 8.3 %collective-permute-start.14 = (bf16[256,128]{1,0:T(8,128)(2,1)S(1)}, bf16[256,128]{1,0:T(8,128)(2,1)S(1)}, u32[]{:S(2)}, u32[]{:S(2)}) collective-permute-start(bf16[256,128]{1,0:T(8,128)(2,1)S(1)} %get-tuple-element.34), channel_id=1, source_target_pairs={{0,16},{8,32},{24,0},{32,24},{40,40},{56,8},{64,80},{72,96},{88,64... | collective-permute-start | bytes 196616 | tf_op jit(solution)/shard_map/ppermute | solution.py:397
  81.0 10.1 %softmax_stats.1 = (f32[1,1024]{1,0:T(1,128)S(1)}, f32[128,1024]{1,0:T(8,128)S(1)}) custom-call(s32[3,3]{1,0:T(4,128)S(1)} %copy-done.20, bf16[3,256,128]{2,1,0:T(8,128)(2,1)S(1)} %copy-done.7, bf16[3,256,128]{2,1,0:T(8,128)(2,1)S(1)} %copy-done.10, bf16[3,256,128]{2,1,0:T(8,128)(2,1)S(1)} %copy-done.13, bf16[3,256,128]{2,1,0:T(8,128)(2,1)S(1)} %copy-done.16, ...), custom_call_target="tpu_custom_call" | custom-call | flops 1308622848 | bytes 3000000 | tf_op jit(solution)/shard_map/softmax_stats/pallas_call | solution.py:400
  91.2 7.1 %time_and_text_grads.1 = (bf16[4,2,256,128]{3,2,1,0:T(8,128)(2,1)}, f32[128,1024]{1,0:T(8,128)S(1)}, f32[1,1024]{1,0:T(1,128)S(1)}, bf16[256,256]{1,0:T(8,128)(2,1)}) custom-call(s32[3,3]{1,0:T(4,128)S(1)} %copy-done.20, bf16[3,256,128]{2,1,0:T(8,128)(2,1)S(1)} %copy-done.7, bf16[3,256,128]{2,1,0:T(8,128)(2,1)S(1)} %copy-done.10, ...), custom_call_target="tpu_custom_call" | custom-call | flops 1006632960 | bytes 2000000 | tf_op jit(solution)/shard_map/time_and_text_grads/pallas_call | solution.py:429
  98.3 0.0 copy-start.8
  98.3 0.0 copy-start.11
  98.3 0.0 copy-start.14
  98.4 5.8 %core_grads.1 = (bf16[4,2,256,128]{3,2,1,0:T(8,128)(2,1)}, f32[128,1024]{1,0:T(8,128)S(1)}) custom-call(s32[3,3]{1,0:T(4,128)S(1)} %copy-done.20, bf16[3,256,128]{2,1,0:T(8,128)(2,1)S(1)} %copy-done.7, bf16[3,256,128]{2,1,0:T(8,128)(2,1)S(1)} %copy-done.10, bf16[3,256,128]{2,1,0:T(8,128)(2,1)S(1)} %copy-done.13, bf16[3,256,128]{2,1,0:T(8,128)(2,1)S(1)} %copy-done.16, ...), custom_call_target="tpu_custom_call" | custom-call | flops 1006632960 | bytes 2000000 | tf_op jit(solution)/shard_map/core_grads/pallas_call | solution.py:445
  104.2 0.8 copy-done.21
  105.0 1.9 %collective-permute-start.17 = (bf16[4,2,256,128]{3,2,1,0:T(8,128)(2,1)}, bf16[4,2,256,128]{3,2,1,0:T(8,128)(2,1)S(1)}, u32[]{:S(2)}, u32[]{:S(2)}) collective-permute-start(bf16[4,2,256,128]{3,2,1,0:T(8,128)(2,1)} %get-tuple-element.41), channel_id=1, source_target_pairs={{0,8},{8,0},{16,24},{24,16},{32,40},{40,32},{64,72},{72,64},{80,88... | collective-permute-start | bytes 1572872 | tf_op jit(solution)/shard_map/ppermute | solution.py:455
  106.9 4.0 %collective-permute-start.18 = (bf16[4,2,256,128]{3,2,1,0:T(8,128)(2,1)}, bf16[4,2,256,128]{3,2,1,0:T(8,128)(2,1)S(1)}, u32[]{:S(2)}, u32[]{:S(2)}) collective-permute-start(bf16[4,2,256,128]{3,2,1,0:T(8,128)(2,1)} %get-tuple-element.42), channel_id=1, source_target_pairs={{8,64},{24,80},{40,96},{64,8},{72,128},{80,24},{88,144},{96,40},{1... | collective-permute-start | bytes 1572872 | tf_op jit(solution)/shard_map/ppermute | solution.py:439
  110.9 4.6 %all-to-all-start = ((bf16[8,32,256]{2,1,0:T(8,128)(2,1)}), bf16[8,32,256]{2,1,0:T(8,128)(2,1)S(1)}, u32[]{:S(2)}, u32[]{:S(2)}) async-start(bf16[8,32,256]{2,1,0:T(8,128)(2,1)} %bitcast.5), calls=%async_computation | async-start | bytes 262144 | tf_op jit(solution)/shard_map/all_to_all | solution.py:441
  115.5 1.0 copy-done.22
  116.5 5.1 %own_grads.1 = (f32[4,2,256,128]{3,2,1,0:T(8,128)S(1)}, bf16[4,256,128]{2,1,0:T(8,128)(2,1)S(1)}) custom-call(s32[3,3]{1,0:T(4,128)S(1)} %copy-done.20, bf16[3,256,128]{2,1,0:T(8,128)(2,1)S(1)} %copy-done.8, bf16[3,256,128]{2,1,0:T(8,128)(2,1)S(1)} %copy-done.11, bf16[3,256,128]{2,1,0:T(8,128)(2,1)S(1)} %copy-done.14, bf16[3,256,128]{2,1,0:T(8,128)(2,1)S(1)} %copy-done.17, ...), custom_call_target="tpu_custom_call" | custom-call | flops 1006632960 | bytes 2000000 | tf_op jit(solution)/shard_map/own_grads/pallas_call | solution.py:457
  121.6 0.3 all-to-all-done.text
  121.9 0.2 combine.1
  122.1 3.8 %collective-permute-start.19 = (bf16[784,128]{1,0:T(8,128)(2,1)S(1)}, bf16[784,128]{1,0:T(8,128)(2,1)S(1)}, u32[]{:S(2)}, u32[]{:S(2)}) collective-permute-start(bf16[784,128]{1,0:T(8,128)(2,1)S(1)} %get-tuple-element.45), channel_id=1, source_target_pairs={{0,0},{16,8},{32,16},{8,32},{24,40},{40,48},{64,64},{80,72},{96,80... | collective-permute-start | bytes 602120 | tf_op jit(solution)/shard_map/ppermute | solution.py:477
  126.0 1.9 %collective-permute-start.20 = (bf16[784,128]{1,0:T(8,128)(2,1)S(1)}, bf16[784,128]{1,0:T(8,128)(2,1)S(1)}, u32[]{:S(2)}, u32[]{:S(2)}) collective-permute-start(bf16[784,128]{1,0:T(8,128)(2,1)S(1)} %get-tuple-element.46), channel_id=1, source_target_pairs={{0,8},{16,16},{32,24},{8,40},{24,48},{40,56},{64,72},{80,80},{96,8... | collective-permute-start | bytes 602120 | tf_op jit(solution)/shard_map/ppermute | solution.py:477
  127.9 1.3 collective-permute-start.21
  129.2 1.9 %collective-permute-start.22 = (bf16[784,128]{1,0:T(8,128)(2,1)S(1)}, bf16[784,128]{1,0:T(8,128)(2,1)S(1)}, u32[]{:S(2)}, u32[]{:S(2)}) collective-permute-start(bf16[784,128]{1,0:T(8,128)(2,1)S(1)} %get-tuple-element.48), channel_id=1, source_target_pairs={{16,0},{32,8},{0,24},{24,32},{40,40},{8,56},{80,64},{96,72},{64,88... | collective-permute-start | bytes 602120 | tf_op jit(solution)/shard_map/ppermute | solution.py:477
  131.1 2.4 %collective-permute-done.19.r0 = bf16[784,128]{1,0:T(8,128)(2,1)S(1)} collective-permute-done((bf16[784,128]{1,0:T(8,128)(2,1)S(1)}, bf16[784,128]{1,0:T(8,128)(2,1)S(1)}, u32[]{:S(2)}, u32[]{:S(2)}) %collective-permute-start.19) | collective-permute-done | bytes 200736 | tf_op jit(solution)/shard_map/ppermute | solution.py:477
  133.6 3.7 %collective-permute-done.21.r2 = bf16[784,128]{1,0:T(8,128)(2,1)S(1)} collective-permute-done((bf16[784,128]{1,0:T(8,128)(2,1)S(1)}, bf16[784,128]{1,0:T(8,128)(2,1)S(1)}, u32[]{:S(2)}, u32[]{:S(2)}) %collective-permute-start.21) | collective-permute-done | bytes 200736 | tf_op jit(solution)/shard_map/ppermute | solution.py:477
  137.3 12.1 %collective-permute-done.22.r3 = bf16[784,128]{1,0:T(8,128)(2,1)S(1)} collective-permute-done((bf16[784,128]{1,0:T(8,128)(2,1)S(1)}, bf16[784,128]{1,0:T(8,128)(2,1)S(1)}, u32[]{:S(2)}, u32[]{:S(2)}) %collective-permute-start.22) | collective-permute-done | bytes 200736 | tf_op jit(solution)/shard_map/ppermute | solution.py:477
  149.4 2.0 %unpack.1 = (bf16[256,384]{1,0:T(8,128)(2,1)}, f32[256,384]{1,0:T(8,128)}, f32[256,384]{1,0:T(8,128)}, f32[8,384]{1,0:T(8,128)}, f32[8,384]{1,0:T(8,128)}) custom-call(bf16[784,128]{1,0:T(8,128)(2,1)S(1)} %collective-permute-done.19.r0, bf16[784,128]{1,0:T(8,128)(2,1)S(1)} %collective-permute-done.20.r1, bf16[784,128]{1,0:T(8,128)(2,1)S(1)} %collective-permute-done.21.r2, ...), custom_call_target="tpu_custom_call" | custom-call | tf_op jit(solution)/shard_map/unpack/pallas_call | solution.py:480
  (47 shorter events, 0.1 us)
Async XLA Ops:
  0.6 61.3 %copy-start = (bf16[384,3072]{1,0:T(8,128)(2,1)S(1)}, bf16[384,3072]{1,0:T(8,128)(2,1)}, u32[]{:S(2)}) copy-start(bf16[384,3072]{1,0:T(8,128)(2,1)} %w_ref.1) | copy-start | bytes 7077892
  0.6 1.1 copy-start.1
  1.7 0.9 copy-start.2
  2.6 0.9 copy-start.3
  3.6 34.8 %copy-start.4 = (bf16[256,384]{1,0:T(8,128)(2,1)S(1)}, bf16[256,384]{1,0:T(8,128)(2,1)}, u32[]{:S(2)}) copy-start(bf16[256,384]{1,0:T(8,128)(2,1)} %c0.1) | copy-start | bytes 589828
  3.6 52.9 %copy-start.23 = (s32[256]{0:T(256)S(1)}, s32[256]{0:T(256)}, u32[]{:S(2)}) copy-start(s32[256]{0:T(256)} %param.17) | copy-start | bytes 3076
  3.9 22.0 %collective-permute-start = (bf16[3,256,128]{2,1,0:T(8,128)(2,1)S(1)}, bf16[3,256,128]{2,1,0:T(8,128)(2,1)S(1)}, u32[]{:S(2)}, u32[]{:S(2)}) collective-permute-start(bf16[3,256,128]{2,1,0:T(8,128)(2,1)S(1)} %get-tuple-element.27), channel_id=1, source_target_pairs={{0,0},{8,16},{16,32},{32,8},{40,24},{48,40},{64,64},{72,80},{80,96... | collective-permute-start | bytes 589832 | tf_op jit(solution)/shard_map/ppermute | solution.py:384
  10.2 33.7 %collective-permute-start.9 = (bf16[256,384]{1,0:T(8,128)(2,1)}, bf16[256,384]{1,0:T(8,128)(2,1)S(1)}, u32[]{:S(2)}, u32[]{:S(2)}) collective-permute-start(bf16[256,384]{1,0:T(8,128)(2,1)} %c0.1), channel_id=1, source_target_pairs={{0,6},{1,7},{2,4},{3,5},{4,2},{5,3},{6,0},{7,1},{8,14},{9,15},{10,... | collective-permute-start | bytes 589832 | tf_op jit(solution)/shard_map/ppermute | solution.py:381
  14.3 14.6 %collective-permute-start.1 = (bf16[3,256,128]{2,1,0:T(8,128)(2,1)S(1)}, bf16[3,256,128]{2,1,0:T(8,128)(2,1)S(1)}, u32[]{:S(2)}, u32[]{:S(2)}) collective-permute-start(bf16[3,256,128]{2,1,0:T(8,128)(2,1)S(1)} %get-tuple-element.28), channel_id=1, source_target_pairs={{8,0},{16,16},{24,32},{40,8},{48,24},{56,40},{72,64},{80,80},{88,9... | collective-permute-start | bytes 589832 | tf_op jit(solution)/shard_map/ppermute | solution.py:384
  16.3 13.4 %collective-permute-start.2 = (bf16[3,256,128]{2,1,0:T(8,128)(2,1)S(1)}, bf16[3,256,128]{2,1,0:T(8,128)(2,1)S(1)}, u32[]{:S(2)}, u32[]{:S(2)}) collective-permute-start(bf16[3,256,128]{2,1,0:T(8,128)(2,1)S(1)} %get-tuple-element.29), channel_id=1, source_target_pairs={{0,32},{16,0},{24,16},{32,40},{48,8},{56,24},{64,96},{80,64},{88,8... | collective-permute-start | bytes 589832 | tf_op jit(solution)/shard_map/ppermute | solution.py:384
  17.6 14.7 %collective-permute-start.3 = (bf16[3,256,128]{2,1,0:T(8,128)(2,1)S(1)}, bf16[3,256,128]{2,1,0:T(8,128)(2,1)S(1)}, u32[]{:S(2)}, u32[]{:S(2)}) collective-permute-start(bf16[3,256,128]{2,1,0:T(8,128)(2,1)S(1)} %get-tuple-element.30), channel_id=1, source_target_pairs={{0,16},{8,32},{24,0},{32,24},{40,40},{56,8},{64,80},{72,96},{88,64... | collective-permute-start | bytes 589832 | tf_op jit(solution)/shard_map/ppermute | solution.py:384
  25.9 0.7 copy-start.6
  28.9 0.7 copy-start.9
  29.6 0.7 copy-start.12
  32.3 0.7 copy-start.15
  32.9 48.0 %copy-start.20 = (s32[3,3]{1,0:T(4,128)S(1)}, s32[3,3]{1,0:T(4,128)}, u32[]{:S(2)}) copy-start(s32[3,3]{1,0:T(4,128)} %ext_ref.7) | copy-start | bytes 112
  33.8 38.8 %collective-permute-start.16 = (bf16[4,2,256,128]{3,2,1,0:T(8,128)(2,1)}, bf16[4,2,256,128]{3,2,1,0:T(8,128)(2,1)}, u32[]{:S(2)}, u32[]{:S(2)}) collective-permute-start(bf16[4,2,256,128]{3,2,1,0:T(8,128)(2,1)} %pad_maximum_fusion), channel_id=1, source_target_pairs={{8,64},{24,80},{40,96},{64,8},{72,128},{80,24},{88,144},{96,40},{1... | collective-permute-start | bytes 1572872 | tf_op jit(solution)/shard_map/ppermute | solution.py:387
  36.4 44.5 %collective-permute-start.15 = (bf16[4,2,256,128]{3,2,1,0:T(8,128)(2,1)}, bf16[4,2,256,128]{3,2,1,0:T(8,128)(2,1)}, u32[]{:S(2)}, u32[]{:S(2)}) collective-permute-start(bf16[4,2,256,128]{3,2,1,0:T(8,128)(2,1)} %pad_maximum_fusion), channel_id=1, source_target_pairs={{0,8},{8,0},{16,24},{24,16},{32,40},{40,32},{64,72},{72,64},{80,88... | collective-permute-start | bytes 1572872 | tf_op jit(solution)/shard_map/ppermute | solution.py:386
  38.4 11.6 %collective-permute-start.8 = (bf16[256,384]{1,0:T(8,128)(2,1)S(1)}, bf16[256,384]{1,0:T(8,128)(2,1)S(1)}, u32[]{:S(2)}, u32[]{:S(2)}) collective-permute-start(bf16[256,384]{1,0:T(8,128)(2,1)S(1)} %copy-done.4), channel_id=1, source_target_pairs={{0,5},{1,6},{2,7},{3,4},{4,1},{5,2},{6,3},{7,0},{8,13},{9,14},{10,... | collective-permute-start | bytes 589832 | tf_op jit(solution)/shard_map/ppermute | solution.py:381
  43.8 8.9 %collective-permute-start.7 = (bf16[256,384]{1,0:T(8,128)(2,1)S(1)}, bf16[256,384]{1,0:T(8,128)(2,1)S(1)}, u32[]{:S(2)}, u32[]{:S(2)}) collective-permute-start(bf16[256,384]{1,0:T(8,128)(2,1)S(1)} %copy-done.4), channel_id=1, source_target_pairs={{0,4},{1,5},{2,6},{3,7},{4,0},{5,1},{6,2},{7,3},{8,12},{9,13},{10,... | collective-permute-start | bytes 589832 | tf_op jit(solution)/shard_map/ppermute | solution.py:381
  43.9 9.3 %collective-permute-start.6 = (bf16[256,384]{1,0:T(8,128)(2,1)S(1)}, bf16[256,384]{1,0:T(8,128)(2,1)S(1)}, u32[]{:S(2)}, u32[]{:S(2)}) collective-permute-start(bf16[256,384]{1,0:T(8,128)(2,1)S(1)} %copy-done.4), channel_id=1, source_target_pairs={{0,3},{1,0},{2,1},{3,2},{4,7},{5,4},{6,5},{7,6},{8,11},{9,8},{10,9... | collective-permute-start | bytes 589832 | tf_op jit(solution)/shard_map/ppermute | solution.py:381
  49.9 7.3 %collective-permute-start.5 = (bf16[256,384]{1,0:T(8,128)(2,1)S(1)}, bf16[256,384]{1,0:T(8,128)(2,1)S(1)}, u32[]{:S(2)}, u32[]{:S(2)}) collective-permute-start(bf16[256,384]{1,0:T(8,128)(2,1)S(1)} %copy-done.4), channel_id=1, source_target_pairs={{0,2},{1,3},{2,0},{3,1},{4,6},{5,7},{6,4},{7,5},{8,10},{9,11},{10,... | collective-permute-start | bytes 589832 | tf_op jit(solution)/shard_map/ppermute | solution.py:381
  52.7 9.2 %collective-permute-start.4 = (bf16[256,384]{1,0:T(8,128)(2,1)S(1)}, bf16[256,384]{1,0:T(8,128)(2,1)}, u32[]{:S(2)}, u32[]{:S(2)}) collective-permute-start(bf16[256,384]{1,0:T(8,128)(2,1)S(1)} %copy-done.4), channel_id=1, source_target_pairs={{0,1},{1,2},{2,3},{3,0},{4,5},{5,6},{6,7},{7,4},{8,9},{9,10},{10,1... | collective-permute-start | bytes 589832 | tf_op jit(solution)/shard_map/ppermute | solution.py:381
  53.2 8.8 %collective-permute-start.10 = (bf16[256,384]{1,0:T(8,128)(2,1)S(1)}, bf16[256,384]{1,0:T(8,128)(2,1)}, u32[]{:S(2)}, u32[]{:S(2)}) collective-permute-start(bf16[256,384]{1,0:T(8,128)(2,1)S(1)} %copy-done.4), channel_id=1, source_target_pairs={{0,7},{1,4},{2,5},{3,6},{4,3},{5,0},{6,1},{7,2},{8,15},{9,12},{10,... | collective-permute-start | bytes 589832 | tf_op jit(solution)/shard_map/ppermute | solution.py:381
  57.2 23.7 %copy-start.5 = (f32[256,1]{1,0:T(8,128)S(1)}, f32[256,1]{1,0:T(8,128)}, u32[]{:S(2)}) copy-start(f32[256,1]{1,0:T(8,128)} %copy.14.tb_ref) | copy-start | bytes 3076
  57.2 23.7 %copy-start.7 = (bf16[3,256,128]{2,1,0:T(8,128)(2,1)S(1)}, bf16[3,256,128]{2,1,0:T(8,128)(2,1)}, u32[]{:S(2)}) copy-start(bf16[3,256,128]{2,1,0:T(8,128)(2,1)} %copy-done.6) | copy-start | bytes 589828
  57.2 23.7 %copy-start.10 = (bf16[3,256,128]{2,1,0:T(8,128)(2,1)S(1)}, bf16[3,256,128]{2,1,0:T(8,128)(2,1)}, u32[]{:S(2)}) copy-start(bf16[3,256,128]{2,1,0:T(8,128)(2,1)} %copy-done.9) | copy-start | bytes 589828
  57.2 23.7 %copy-start.13 = (bf16[3,256,128]{2,1,0:T(8,128)(2,1)S(1)}, bf16[3,256,128]{2,1,0:T(8,128)(2,1)}, u32[]{:S(2)}) copy-start(bf16[3,256,128]{2,1,0:T(8,128)(2,1)} %copy-done.12) | copy-start | bytes 589828
  57.2 23.7 %copy-start.16 = (bf16[3,256,128]{2,1,0:T(8,128)(2,1)S(1)}, bf16[3,256,128]{2,1,0:T(8,128)(2,1)}, u32[]{:S(2)}) copy-start(bf16[3,256,128]{2,1,0:T(8,128)(2,1)} %copy-done.15) | copy-start | bytes 589828
  57.3 23.7 %copy-start.18 = (bf16[256,384]{1,0:T(8,128)(2,1)S(1)}, bf16[256,384]{1,0:T(8,128)(2,1)}, u32[]{:S(2)}) copy-start(bf16[256,384]{1,0:T(8,128)(2,1)} %tk_ref.3) | copy-start | bytes 589828
  57.3 23.7 %copy-start.19 = (bf16[256,384]{1,0:T(8,128)(2,1)S(1)}, bf16[256,384]{1,0:T(8,128)(2,1)}, u32[]{:S(2)}) copy-start(bf16[256,384]{1,0:T(8,128)(2,1)} %tv_ref.3) | copy-start | bytes 589828
  64.8 26.3 %collective-permute-start.11 = (bf16[256,128]{1,0:T(8,128)(2,1)S(1)}, bf16[256,128]{1,0:T(8,128)(2,1)S(1)}, u32[]{:S(2)}, u32[]{:S(2)}) collective-permute-start(bf16[256,128]{1,0:T(8,128)(2,1)S(1)} %get-tuple-element.31), channel_id=1, source_target_pairs={{0,0},{8,16},{16,32},{32,8},{40,24},{48,40},{64,64},{72,80},{80,96... | collective-permute-start | bytes 196616 | tf_op jit(solution)/shard_map/ppermute | solution.py:397
  69.4 21.8 %collective-permute-start.12 = (bf16[256,128]{1,0:T(8,128)(2,1)S(1)}, bf16[256,128]{1,0:T(8,128)(2,1)S(1)}, u32[]{:S(2)}, u32[]{:S(2)}) collective-permute-start(bf16[256,128]{1,0:T(8,128)(2,1)S(1)} %get-tuple-element.32), channel_id=1, source_target_pairs={{8,0},{16,16},{24,32},{40,8},{48,24},{56,40},{72,64},{80,80},{88,9... | collective-permute-start | bytes 196616 | tf_op jit(solution)/shard_map/ppermute | solution.py:397
  71.3 19.8 %collective-permute-start.13 = (bf16[256,128]{1,0:T(8,128)(2,1)S(1)}, bf16[256,128]{1,0:T(8,128)(2,1)S(1)}, u32[]{:S(2)}, u32[]{:S(2)}) collective-permute-start(bf16[256,128]{1,0:T(8,128)(2,1)S(1)} %get-tuple-element.33), channel_id=1, source_target_pairs={{0,32},{16,0},{24,16},{32,40},{48,8},{56,24},{64,96},{80,64},{88,8... | collective-permute-start | bytes 196616 | tf_op jit(solution)/shard_map/ppermute | solution.py:397
  72.6 18.5 %collective-permute-start.14 = (bf16[256,128]{1,0:T(8,128)(2,1)S(1)}, bf16[256,128]{1,0:T(8,128)(2,1)S(1)}, u32[]{:S(2)}, u32[]{:S(2)}) collective-permute-start(bf16[256,128]{1,0:T(8,128)(2,1)S(1)} %get-tuple-element.34), channel_id=1, source_target_pairs={{0,16},{8,32},{24,0},{32,24},{40,40},{56,8},{64,80},{72,96},{88,64... | collective-permute-start | bytes 196616 | tf_op jit(solution)/shard_map/ppermute | solution.py:397
  98.3 17.1 %copy-start.8 = (bf16[3,256,128]{2,1,0:T(8,128)(2,1)S(1)}, bf16[3,256,128]{2,1,0:T(8,128)(2,1)}, u32[]{:S(2)}) copy-start(bf16[3,256,128]{2,1,0:T(8,128)(2,1)} %copy-done.6) | copy-start | bytes 589828
  98.3 17.1 %copy-start.11 = (bf16[3,256,128]{2,1,0:T(8,128)(2,1)S(1)}, bf16[3,256,128]{2,1,0:T(8,128)(2,1)}, u32[]{:S(2)}) copy-start(bf16[3,256,128]{2,1,0:T(8,128)(2,1)} %copy-done.9) | copy-start | bytes 589828
  98.3 17.1 %copy-start.14 = (bf16[3,256,128]{2,1,0:T(8,128)(2,1)S(1)}, bf16[3,256,128]{2,1,0:T(8,128)(2,1)}, u32[]{:S(2)}) copy-start(bf16[3,256,128]{2,1,0:T(8,128)(2,1)} %copy-done.12) | copy-start | bytes 589828
  98.4 17.1 %copy-start.17 = (bf16[3,256,128]{2,1,0:T(8,128)(2,1)S(1)}, bf16[3,256,128]{2,1,0:T(8,128)(2,1)}, u32[]{:S(2)}) copy-start(bf16[3,256,128]{2,1,0:T(8,128)(2,1)} %copy-done.15) | copy-start | bytes 589828
  104.2 0.8 copy-start.21
  105.0 17.0 %collective-permute-start.17 = (bf16[4,2,256,128]{3,2,1,0:T(8,128)(2,1)}, bf16[4,2,256,128]{3,2,1,0:T(8,128)(2,1)S(1)}, u32[]{:S(2)}, u32[]{:S(2)}) collective-permute-start(bf16[4,2,256,128]{3,2,1,0:T(8,128)(2,1)} %get-tuple-element.41), channel_id=1, source_target_pairs={{0,8},{8,0},{16,24},{24,16},{32,40},{40,32},{64,72},{72,64},{80,88... | collective-permute-start | bytes 1572872 | tf_op jit(solution)/shard_map/ppermute | solution.py:455
  106.9 15.0 %collective-permute-start.18 = (bf16[4,2,256,128]{3,2,1,0:T(8,128)(2,1)}, bf16[4,2,256,128]{3,2,1,0:T(8,128)(2,1)S(1)}, u32[]{:S(2)}, u32[]{:S(2)}) collective-permute-start(bf16[4,2,256,128]{3,2,1,0:T(8,128)(2,1)} %get-tuple-element.42), channel_id=1, source_target_pairs={{8,64},{24,80},{40,96},{64,8},{72,128},{80,24},{88,144},{96,40},{1... | collective-permute-start | bytes 1572872 | tf_op jit(solution)/shard_map/ppermute | solution.py:439
  110.9 11.1 %all-to-all-start = ((bf16[8,32,256]{2,1,0:T(8,128)(2,1)}), bf16[8,32,256]{2,1,0:T(8,128)(2,1)S(1)}, u32[]{:S(2)}, u32[]{:S(2)}) async-start(bf16[8,32,256]{2,1,0:T(8,128)(2,1)} %bitcast.5), calls=%async_computation | async-start | bytes 262144 | tf_op jit(solution)/shard_map/all_to_all | solution.py:441
  115.5 1.0 copy-start.22
  122.1 11.4 %collective-permute-start.19 = (bf16[784,128]{1,0:T(8,128)(2,1)S(1)}, bf16[784,128]{1,0:T(8,128)(2,1)S(1)}, u32[]{:S(2)}, u32[]{:S(2)}) collective-permute-start(bf16[784,128]{1,0:T(8,128)(2,1)S(1)} %get-tuple-element.45), channel_id=1, source_target_pairs={{0,0},{16,8},{32,16},{8,32},{24,40},{40,48},{64,64},{80,72},{96,80... | collective-permute-start | bytes 602120 | tf_op jit(solution)/shard_map/ppermute | solution.py:477
  126.0 7.6 %collective-permute-start.20 = (bf16[784,128]{1,0:T(8,128)(2,1)S(1)}, bf16[784,128]{1,0:T(8,128)(2,1)S(1)}, u32[]{:S(2)}, u32[]{:S(2)}) collective-permute-start(bf16[784,128]{1,0:T(8,128)(2,1)S(1)} %get-tuple-element.46), channel_id=1, source_target_pairs={{0,8},{16,16},{32,24},{8,40},{24,48},{40,56},{64,72},{80,80},{96,8... | collective-permute-start | bytes 602120 | tf_op jit(solution)/shard_map/ppermute | solution.py:477
  127.9 9.4 %collective-permute-start.21 = (bf16[784,128]{1,0:T(8,128)(2,1)S(1)}, bf16[784,128]{1,0:T(8,128)(2,1)S(1)}, u32[]{:S(2)}, u32[]{:S(2)}) collective-permute-start(bf16[784,128]{1,0:T(8,128)(2,1)S(1)} %get-tuple-element.47), channel_id=1, source_target_pairs={{32,0},{0,16},{16,24},{40,32},{8,48},{24,56},{96,64},{64,80},{80,8... | collective-permute-start | bytes 602120 | tf_op jit(solution)/shard_map/ppermute | solution.py:477
  129.2 20.2 %collective-permute-start.22 = (bf16[784,128]{1,0:T(8,128)(2,1)S(1)}, bf16[784,128]{1,0:T(8,128)(2,1)S(1)}, u32[]{:S(2)}, u32[]{:S(2)}) collective-permute-start(bf16[784,128]{1,0:T(8,128)(2,1)S(1)} %get-tuple-element.48), channel_id=1, source_target_pairs={{16,0},{32,8},{0,24},{24,32},{40,40},{8,56},{80,64},{96,72},{64,88... | collective-permute-start | bytes 602120 | tf_op jit(solution)/shard_map/ppermute | solution.py:477

commit v2 on v1

v2 whole, which is shorter than its diff:
```python
import functools
import math

import jax
import jax.numpy as jnp
from jax import lax
from jax.experimental import pallas as pl
from jax.experimental.pallas import tpu as pltpu
from jax.sharding import PartitionSpec as P

DH = 128
TOK = 256
TEXT = 256
ROWS = 4
SPAN = 3 * TOK
QALL = ROWS * TOK
MSG = 3 * TOK + 16
INV_ROOT = DH ** (-0.5)
LOG2E = math.log2(math.e)
F32 = jnp.float32
BF16 = jnp.bfloat16
ANY = pl.BlockSpec(memory_space=pltpu.HBM)
VMEM = pl.BlockSpec(memory_space=pltpu.VMEM)
SMEM = pl.BlockSpec(memory_space=pltpu.SMEM)


def params(mib=12):
    return pltpu.CompilerParams(vmem_limit_bytes=mib * 1024 * 1024)


def sds(shape, dtype):
    return jax.ShapeDtypeStruct(shape, dtype)


def dot_nt(a, b):
    return lax.dot_general(a, b, (((1,), (1,)), ((), ())), preferred_element_type=F32)


def dot_nn(a, b):
    return lax.dot_general(a, b, (((1,), (0,)), ((), ())), preferred_element_type=F32)


def dot_tn(a, b):
    return lax.dot_general(a, b, (((0,), (0,)), ((), ())), preferred_element_type=F32)


def sent_head(phase, h):
    far, swap = (1, 0, 1, 0)[phase], phase // 2
    return ((h >> 1) ^ far) + 2 * ((h & 1) ^ swap)


def received_height(phase, chip):
    far, swap = (1, 0, 1, 0)[phase], phase // 2
    return 2 * ((chip & 1) ^ far) + ((chip >> 1) ^ swap)


def out_pairs(phase):
    pairs = []
    for y in range(4):
        for zt in range(2):
            for h in range(4):
                head = sent_head(phase, h)
                if head < 3:
                    pairs.append((y * 8 + zt * 4 + h, y * 8 + head * 2 + zt))
    return pairs


def back_pairs(phase):
    return [(b, a) for a, b in out_pairs(phase)]


def core_pairs():
    return [(s, s ^ 1) for s in range(32) if (s // 2) % 4 < 3]


def time_pairs():
    pairs = []
    for s in range(32):
        y, z_hi, c = s // 8, (s // 2) % 4, s % 2
        if z_hi < 3:
            other = y + 1 if c else y - 1
            if 0 <= other < 4:
                pairs.append((s, other * 8 + z_hi * 2 + 1 - c))
    return pairs


def head_pairs(dx, dz):
    return [(g, ((g // 4 + dz) % 2) * 4 + (g % 4 + dx) % 4) for g in range(8)]


def start_all(copies):
    for one in copies:
        one.start()


def wait_all(copies):
    for one in copies:
        one.wait()


def home_height():
    return lax.axis_index("seq") & 3


def work_chip():
    return (lax.axis_index("seq") >> 1) & 3


def pack_kernel(q_ref, k_ref, v_ref, o0, o1, o2, o3, sem):
    h = home_height()
    copies = []
    for phase, out in enumerate((o0, o1, o2, o3)):
        head = jnp.minimum(sent_head(phase, h), 2)
        columns = pl.ds(pl.multiple_of(head * DH, DH), DH)
        for which, src in enumerate((q_ref, k_ref, v_ref)):
            copies.append(
                pltpu.make_async_copy(src.at[:, columns], out.at[which], sem.at[phase * 3 + which])
            )
    start_all(copies)
    wait_all(copies)


def project_kernel(c0, c1, c2, c3, c4, c5, c6, c7, w_ref, o0, o1, o2, o3):
    chunks = (c0, c1, c2, c3, c4, c5, c6, c7)
    g = lax.axis_index("head")
    h = home_height()
    gz, gx = lax.div(g, 4), lax.rem(g, 4)
    width = c0.shape[1]
    for phase, out in enumerate((o0, o1, o2, o3)):
        head = jnp.minimum(sent_head(phase, h), 2)
        rows = pl.ds(pl.multiple_of(head * DH, DH), DH)
        total = None
        for which, chunk in enumerate(chunks):
            dz, dx = which // 4, which % 4
            src = lax.rem(gz + dz, 2) * 4 + lax.rem(gx - dx + 4, 4)
            columns = pl.ds(pl.multiple_of(src * width, width), width)
            term = dot_nt(chunk[...], w_ref[rows, columns])
            total = term if total is None else total + term
        out[...] = total.astype(BF16)


def window(ext_ref, chip):
    head = jnp.minimum(chip, 2)
    reach_t, reach_h, reach_w = ext_ref[head, 0], ext_ref[head, 1], ext_ref[head, 2]
    s = lax.axis_index("seq")
    y, c = lax.div(s, 8), lax.rem(s, 2)
    near = reach_t >= 1
    outside = ((y == 0) & (c == 0)) | ((y == 3) & (c == 1))
    return (True, near, near & jnp.logical_not(outside)), reach_h, reach_w >= 1


def span_bias(block_ok, reach_h, wide, key_h, first_h):
    lane = lax.broadcasted_iota(jnp.int32, (1, TOK), 1)
    left = lane < TOK // 2
    top, low = [], []
    for j in range(3):
        ok = jnp.abs(first_h + j - key_h) <= reach_h
        if block_ok is not True:
            ok = ok & block_ok
        same = jnp.where(ok, 0.0, -jnp.inf).astype(F32)
        cross = jnp.where(ok & wide, 0.0, -jnp.inf).astype(F32)
        top.append(jnp.where(left, same, cross))
        low.append(jnp.where(left, cross, same))
    return jnp.concatenate(top, 1), jnp.concatenate(low, 1)


def first_height(key_h):
    return jnp.clip(key_h - 1, 0, 1)


def fold(x, how):
    return how(x.reshape(x.shape[0] // 8, 8, x.shape[1]), 0)


def stats_kernel(
    ext_ref, m0, m1, m2, m3, core_kv, time_kv, tk_ref, tv_ref, tb_ref,
    lse_ref, mean_ref,
    kb, vb, qb, sb, st, run,
):
    chip = work_chip()
    for phase, msg in enumerate((m0, m1, m2, m3)):
        h = received_height(phase, chip)
        qb[pl.ds(pl.multiple_of(h * TOK, TOK), TOK), :] = msg[0]
        kb[h], vb[h] = msg[1], msg[2]
        kb[4 + h], vb[4 + h] = core_kv[phase, 0], core_kv[phase, 1]
        kb[8 + h], vb[8 + h] = time_kv[phase, 0], time_kv[phase, 1]
    block_ok, reach_h, wide = window(ext_ref, chip)
    head = jnp.minimum(chip, 2)
    columns = pl.ds(pl.multiple_of(head * DH, DH), DH)
    factor = INV_ROOT * LOG2E

    text = dot_nt(tk_ref[:, columns], qb[...]) * factor + tb_ref[...]
    st[...] = text
    run[...] = fold(text, jnp.max)

    for part in range(3):

        def first(key_h, carry, part=part):
            h0 = first_height(key_h)
            rows = pl.ds(pl.multiple_of(h0 * TOK, TOK), SPAN)
            top, low = span_bias(block_ok[part], reach_h, wide, key_h, h0)
            s = dot_nt(kb[part * 4 + key_h], qb[rows, :]) * factor
            a, b = s[: TOK // 2] + top, s[TOK // 2 :] + low
            sb[part * 4 + key_h, : TOK // 2] = a
            sb[part * 4 + key_h, TOK // 2 :] = b
            run[:, rows] = jnp.maximum(run[:, rows], jnp.maximum(fold(a, jnp.max), fold(b, jnp.max)))
            return carry

        lax.fori_loop(0, 4, first, 0, unroll=True)

    top_score = jnp.max(run[...], 0, keepdims=True)
    lse_ref[...] = top_score
    weights = jnp.exp2(st[...] - top_score)
    run[...] = fold(weights, jnp.sum)
    mean_ref[...] = dot_tn(tv_ref[:, columns], weights.astype(BF16))

    def second(block, carry):
        key_h = lax.rem(block, 4)
        rows = pl.ds(pl.multiple_of(first_height(key_h) * TOK, TOK), SPAN)
        weights = jnp.exp2(sb[block] - lse_ref[:, rows])
        run[:, rows] += fold(weights, jnp.sum)
        mean_ref[:, rows] += dot_tn(vb[block], weights.astype(BF16))
        return carry

    lax.fori_loop(0, 12, second, 0, unroll=4)
    total = jnp.sum(run[...], 0, keepdims=True)
    lse_ref[...] = top_score + jnp.log2(total)
    mean_ref[...] = mean_ref[...] / total


def block_terms(keys, values, query, grad, bias, delta, factor):
    s = dot_nt(keys, query) * factor
    if isinstance(bias, tuple):
        top, low = bias
        half = TOK // 2
        probs = jnp.concatenate([jnp.exp2(s[:half] + top), jnp.exp2(s[half:] + low)], 0)
    else:
        probs = jnp.exp2(s + bias)
    dprobs = dot_nt(values, grad)
    dscores = (probs * (dprobs - delta)).astype(BF16)
    return probs.astype(BF16), dscores


def place_rows(chip, refs, out):
    for phase, ref in enumerate(refs):
        rows = pl.ds(pl.multiple_of(received_height(phase, chip) * TOK, TOK), TOK)
        out[rows, :] = ref[...]


def part_grads(part, m_refs, kv_ref, ext_ref, lse_ref, delta_ref, out_ref, dq_ref, kb, vb, qb, gb):
    chip = work_chip()
    for phase in range(4):
        h = received_height(phase, chip)
        kb[h] = m_refs[phase][1] if part == 0 else kv_ref[phase, 0]
        vb[h] = m_refs[phase][2] if part == 0 else kv_ref[phase, 1]
    block_ok, reach_h, wide = window(ext_ref, chip)
    factor = INV_ROOT * LOG2E

    def body(key_h, carry):
        h0 = first_height(key_h)
        rows = pl.ds(pl.multiple_of(h0 * TOK, TOK), SPAN)
        top, low = span_bias(block_ok[part], reach_h, wide, key_h, h0)
        lse = lse_ref[:, rows]
        query, grad, keys = qb[rows, :], gb[rows, :], kb[key_h]
        probs, dscores = block_terms(
            keys, vb[key_h], query, grad, (top - lse, low - lse), delta_ref[:, rows], factor
        )
        out_ref[key_h, 0] = (dot_nn(dscores, query) * INV_ROOT).astype(out_ref.dtype)
        out_ref[key_h, 1] = dot_nn(probs, grad).astype(out_ref.dtype)
        dq_ref[:, rows] += dot_tn(keys, dscores)
        return carry

    lax.fori_loop(0, 4, body, 0, unroll=True)


def time_grads_kernel(
    ext_ref, m0, m1, m2, m3, g0, g1, g2, g3, time_kv, lse_ref, mean_ref, tk_ref, tv_ref, tb_ref,
    time_out, text_ref, dq_ref, delta_ref, gb,
    kb, vb, qb,
):
    chip = work_chip()
    m_refs = (m0, m1, m2, m3)
    place_rows(chip, [ref.at[0] for ref in m_refs], qb)
    place_rows(chip, (g0, g1, g2, g3), gb)
    delta_ref[...] = jnp.sum(gb[...].astype(F32).T * mean_ref[...], 0, keepdims=True)
    head = jnp.minimum(chip, 2)
    columns = pl.ds(pl.multiple_of(head * DH, DH), DH)
    keys = tk_ref[:, columns]
    probs, dscores = block_terms(
        keys, tv_ref[:, columns], qb[...], gb[...], tb_ref[...] - lse_ref[...], delta_ref[...],
        INV_ROOT * LOG2E,
    )
    dq_ref[...] = dot_tn(keys, dscores)
    text_ref[:, :DH] = (dot_nn(dscores, qb[...]) * INV_ROOT).astype(BF16)
    text_ref[:, DH:] = dot_nn(probs, gb[...]).astype(BF16)
    part_grads(2, m_refs, time_kv, ext_ref, lse_ref, delta_ref, time_out, dq_ref, kb, vb, qb, gb)


def near_grads_kernel(
    ext_ref, m0, m1, m2, m3, core_kv, lse_ref, dq_in, delta_ref, gb,
    core_out, own_out,
    kb, vb, qb, dq_run,
):
    m_refs = (m0, m1, m2, m3)
    place_rows(work_chip(), [ref.at[0] for ref in m_refs], qb)
    dq_run[...] = dq_in[...]
    part_grads(1, m_refs, core_kv, ext_ref, lse_ref, delta_ref, core_out, dq_run, kb, vb, qb, gb)
    part_grads(0, m_refs, None, ext_ref, lse_ref, delta_ref, own_out, dq_run, kb, vb, qb, gb)
    for h in range(ROWS):
        own_out[h, 2] = dq_run[:, h * TOK : (h + 1) * TOK].T * INV_ROOT


def combine_kernel(own, core, time, text, o0, o1, o2, o3, text_sum):
    chip = work_chip()
    text_sum[...] = jnp.sum(text[...].astype(F32), 0)
    for phase, out in enumerate((o0, o1, o2, o3)):
        h = received_height(phase, chip)
        out[:TOK] = own[h, 2].astype(BF16)
        for which in range(2):
            total = own[h, which] + core[h, which].astype(F32) + time[h, which].astype(F32)
            out[(1 + which) * TOK : (2 + which) * TOK] = total.astype(BF16)
        share = text_sum[pl.ds(pl.multiple_of(h * 8, 8), 8), :]
        out[3 * TOK :] = jnp.concatenate([share[:, :DH], share[:, DH:]], 0).astype(BF16)


def unpack_kernel(r0, r1, r2, r3, dq, dk, dv, tk, tv, buf):
    h = home_height()
    for phase, src in enumerate((r0, r1, r2, r3)):
        buf[sent_head(phase, h)] = src[...]
    for head in range(3):
        columns = slice(head * DH, (head + 1) * DH)
        dq[:, columns] = buf[head, :TOK]
        dk[:, columns] = buf[head, TOK : 2 * TOK].astype(F32)
        dv[:, columns] = buf[head, 2 * TOK : 3 * TOK].astype(F32)
        share = buf[head, 3 * TOK :].astype(F32)
        tk[:, columns] = share[:8]
        tv[:, columns] = share[8:]


def per_device(queries, keys, values, layer_grad, out_weight, text_keys, text_values, extents, text_mask):
    block = sds((TOK, DH), BF16)
    text_bias = jnp.where(text_mask == 1, 0.0, -jnp.inf).astype(F32)[:, None]

    packed = pl.pallas_call(
        pack_kernel,
        in_specs=[ANY] * 3,
        out_specs=[ANY] * 4,
        out_shape=[sds((3, TOK, DH), BF16)] * 4,
        scratch_shapes=[pltpu.SemaphoreType.DMA((12,))],
        compiler_params=params(),
        name="pack_heads",
    )(queries, keys, values)

    beside = lax.ppermute(layer_grad, "head", head_pairs(0, 1))
    chunks = [
        src if dx == 0 else lax.ppermute(src, "head", head_pairs(dx, 0))
        for src in (layer_grad, beside)
        for dx in range(4)
    ]
    packed = list(packed)
    packed[1:], chunks[1] = lax.optimization_barrier((packed[1:], chunks[1]))
    msgs = [lax.ppermute(one, "seq", out_pairs(phase)) for phase, one in enumerate(packed)]
    msgs, chunks = lax.optimization_barrier((msgs, chunks))
    kv = jnp.stack([one[1:] for one in msgs])
    core_kv = lax.ppermute(kv, "seq", core_pairs())
    time_kv = lax.ppermute(kv, "seq", time_pairs())

    grads = pl.pallas_call(
        project_kernel,
        in_specs=[VMEM] * 9,
        out_specs=[VMEM] * 4,
        out_shape=[block] * 4,
        compiler_params=params(),
        name="project",
    )(*chunks, out_weight)
    grads = [lax.ppermute(one, "seq", out_pairs(phase)) for phase, one in enumerate(grads)]

    lse, mean = pl.pallas_call(
        stats_kernel,
        in_specs=[SMEM] + [VMEM] * 9,
        out_specs=[VMEM] * 2,
        out_shape=[sds((1, QALL), F32), sds((DH, QALL), F32)],
        scratch_shapes=[
            pltpu.VMEM((12, TOK, DH), BF16),
            pltpu.VMEM((12, TOK, DH), BF16),
            pltpu.VMEM((QALL, DH), BF16),
            pltpu.VMEM((12, TOK, SPAN), F32),
            pltpu.VMEM((TEXT, QALL), F32),
            pltpu.VMEM((8, QALL), F32),
        ],
        compiler_params=params(24),
        cost_estimate=pl.CostEstimate(flops=1000, bytes_accessed=1000, transcendentals=0),
        name="softmax_stats",
    )(extents, *msgs, core_kv, time_kv, text_keys, text_values, text_bias)

    half_sum = sds((4, 2, TOK, DH), BF16)
    scratch = [
        pltpu.VMEM((4, TOK, DH), BF16),
        pltpu.VMEM((4, TOK, DH), BF16),
        pltpu.VMEM((QALL, DH), BF16),
    ]
    cost = pl.CostEstimate(flops=1000, bytes_accessed=1000, transcendentals=0)
    time_part, text_part, dq, delta, grad_rows = pl.pallas_call(
        time_grads_kernel,
        in_specs=[SMEM] + [VMEM] * 14,
        out_specs=[VMEM] * 5,
        out_shape=[
            half_sum,
            sds((TEXT, 2 * DH), BF16),
            sds((DH, QALL), F32),
            sds((1, QALL), F32),
            sds((QALL, DH), BF16),
        ],
        scratch_shapes=scratch,
        compiler_params=params(),
        cost_estimate=cost,
        name="far_grads",
    )(extents, *msgs, *grads, time_kv, lse, mean, text_keys, text_values, text_bias)
    time_back = lax.ppermute(time_part, "seq", time_pairs())
    core_part, own_part = pl.pallas_call(
        near_grads_kernel,
        in_specs=[SMEM] + [VMEM] * 9,
        out_specs=[VMEM] * 2,
        out_shape=[half_sum, sds((4, 3, TOK, DH), F32)],
        scratch_shapes=scratch + [pltpu.VMEM((DH, QALL), F32)],
        compiler_params=params(16),
        cost_estimate=cost,
        name="own_grads",
    )(extents, *msgs, core_kv, lse, dq, delta, grad_rows)
    text_part, own_part = lax.optimization_barrier((text_part, own_part))
    core_back = lax.ppermute(core_part, "seq", core_pairs())
    groups = [[y * 8 + z_hi * 2 + c for y in range(4) for c in range(2)] for z_hi in range(4)]
    text_back = lax.all_to_all(
        text_part.reshape(8, TEXT // 8, 2 * DH), "seq", 0, 0, axis_index_groups=groups
    )

    results = pl.pallas_call(
        combine_kernel,
        in_specs=[VMEM] * 4,
        out_specs=[VMEM] * 4,
        out_shape=[sds((MSG, DH), BF16)] * 4,
        scratch_shapes=[pltpu.VMEM((TEXT // 8, 2 * DH), F32)],
        compiler_params=params(),
        name="combine",
    )(own_part, core_back, time_back, text_back)
    results = [lax.ppermute(one, "seq", back_pairs(phase)) for phase, one in enumerate(results)]

    width = 3 * DH
    return pl.pallas_call(
        unpack_kernel,
        in_specs=[VMEM] * 4,
        out_specs=[VMEM] * 5,
        out_shape=[
            sds((TOK, width), BF16),
            sds((TOK, width), F32),
            sds((TOK, width), F32),
            sds((8, width), F32),
            sds((8, width), F32),
        ],
        scratch_shapes=[pltpu.VMEM((4, MSG, DH), BF16)],
        compiler_params=params(),
        name="unpack",
    )(*results)


def solution(mesh):
    return jax.shard_map(
        per_device,
        mesh=mesh,
        in_specs=(
            P("seq", "head"),
            P("seq", "head"),
            P("seq", "head"),
            P("seq", "head"),
            P("head", None),
            P(None, "head"),
            P(None, "head"),
            P("head", None),
            P(),
        ),
        out_specs=(P("seq", "head"),) * 5,
        check_vma=False,
    )
```

time: 152 us -> 111 us (0.73)
  the two profiles are of different devices: /device:TPU:1 before, /device:TPU:33 now
where the time goes in v2:
time: 111 us; the launch traced here: 110 us
  starting transfers between devices  57.4 us (52%)
  waiting for transfers between devices  23.8 us (21%)
  Pallas kernels  16.6 us (15%)
  blocking collectives  8.18 us (7%)
  local copies, waits for them, and re-layouts  2.98 us (3%)
    ppermute x8, starting transfers between devices, per_device(): lax.ppermute(one, 'seq', out_pairs(phase))  26.1 us
    ppermute x4, starting transfers between devices, per_device(): lax.ppermute(one, 'seq', back_pairs(phase))  13 us
    ppermute x4, waiting for transfers between devices, per_device(): lax.ppermute(one, 'seq', back_pairs(phase))  10.8 us
    ppermute x8, waiting for transfers between devices, per_device(): lax.ppermute(one, 'seq', out_pairs(phase))  8.28 us
    all_to_all x1, blocking collectives, per_device(): lax.all_to_all(text_part.reshape(8, TEXT // 8, 2 * DH), 'seq', 0, 0, axis...  8.18 us
    ppermute x6, starting transfers between devices, per_device(): lax.ppermute(src, 'head', head_pairs(dx, 0))  6.75 us
    pallas_call x1, Pallas kernels, per_device(): pl.pallas_call(near_grads_kernel, in_specs=[SMEM] + [VMEM] * 9, out_specs...  4.89 us
    ppermute x6, waiting for transfers between devices, per_device(): lax.ppermute(src, 'head', head_pairs(dx, 0))  4.78 us
  transfers between devices with their start and end apart: 23, of which 6 were waited for; matrix products, arithmetic and copies ran while one was open for 0% of the time, Pallas kernels for 11%

profile of v2, /device:TPU:33, one launch (start us, length us, event | category | flops | bytes accessed | tf_op | source)
XLA Modules:
  0.0 110.1 jit_solution(12996050466770896615)
XLA Ops:
  0.6 0.0 copy-start
  0.6 0.1 collective-permute-start.7
  0.7 1.3 %collective-permute-start.1 = (bf16[256,384]{1,0:T(8,128)(2,1)}, bf16[256,384]{1,0:T(8,128)(2,1)S(1)}, u32[]{:S(2)}, u32[]{:S(2)}) collective-permute-start(bf16[256,384]{1,0:T(8,128)(2,1)} %c0), channel_id=1, source_target_pairs={{0,1},{1,2},{2,3},{3,0},{4,5},{5,6},{6,7},{7,4},{8,9},{9,10},{10,1... | collective-permute-start | bytes 589832 | tf_op jit(solution)/shard_map/ppermute | solution.py:356
  2.0 1.5 %collective-permute-start.6 = (bf16[256,384]{1,0:T(8,128)(2,1)}, bf16[256,384]{1,0:T(8,128)(2,1)S(1)}, u32[]{:S(2)}, u32[]{:S(2)}) collective-permute-start(bf16[256,384]{1,0:T(8,128)(2,1)} %c0), channel_id=1, source_target_pairs={{0,3},{1,0},{2,1},{3,2},{4,7},{5,4},{6,5},{7,6},{8,11},{9,8},{10,9... | collective-permute-start | bytes 589832 | tf_op jit(solution)/shard_map/ppermute | solution.py:356
  3.5 1.5 %collective-permute-start.5 = (bf16[256,384]{1,0:T(8,128)(2,1)}, bf16[256,384]{1,0:T(8,128)(2,1)S(1)}, u32[]{:S(2)}, u32[]{:S(2)}) collective-permute-start(bf16[256,384]{1,0:T(8,128)(2,1)} %c0), channel_id=1, source_target_pairs={{0,2},{1,3},{2,0},{3,1},{4,6},{5,7},{6,4},{7,5},{8,10},{9,11},{10,... | collective-permute-start | bytes 589832 | tf_op jit(solution)/shard_map/ppermute | solution.py:356
  5.0 0.9 copy-done.3
  6.0 0.9 copy-done.4
  6.9 0.9 copy-done.5
  7.8 0.3 pack_heads.1
  8.1 1.3 %collective-permute-start = (bf16[3,256,128]{2,1,0:T(8,128)(2,1)S(1)}, bf16[3,256,128]{2,1,0:T(8,128)(2,1)S(1)}, u32[]{:S(2)}, u32[]{:S(2)}) collective-permute-start(bf16[3,256,128]{2,1,0:T(8,128)(2,1)S(1)} %get-tuple-element.44), channel_id=1, source_target_pairs={{0,16},{16,0},{24,32},{32,24},{48,8},{56,40},{64,80},{80,64},{88,9... | collective-permute-start | bytes 589832 | tf_op jit(solution)/shard_map/ppermute | solution.py:362
  9.4 0.0 collective-permute-done.7.c4
  9.4 0.9 collective-permute-start.10
  10.3 0.0 collective-permute-done.1.c1
  10.3 11.1 %collective-permute-start.2 = (bf16[3,256,128]{2,1,0:T(8,128)(2,1)S(1)}, bf16[3,256,128]{2,1,0:T(8,128)(2,1)S(1)}, u32[]{:S(2)}, u32[]{:S(2)}) collective-permute-start(bf16[3,256,128]{2,1,0:T(8,128)(2,1)S(1)} %get-tuple-element.48), channel_id=1, source_target_pairs={{0,0},{8,32},{16,16},{32,8},{40,40},{48,24},{64,64},{72,96},{80,80... | collective-permute-start | bytes 589832 | tf_op jit(solution)/shard_map/ppermute | solution.py:362
  21.5 0.0 collective-permute-done.6.c3
  21.5 1.9 %collective-permute-start.3 = (bf16[3,256,128]{2,1,0:T(8,128)(2,1)S(1)}, bf16[3,256,128]{2,1,0:T(8,128)(2,1)S(1)}, u32[]{:S(2)}, u32[]{:S(2)}) collective-permute-start(bf16[3,256,128]{2,1,0:T(8,128)(2,1)S(1)} %get-tuple-element.49), channel_id=1, source_target_pairs={{8,16},{16,32},{24,0},{40,24},{48,40},{56,8},{72,80},{80,96},{88,6... | collective-permute-start | bytes 589832 | tf_op jit(solution)/shard_map/ppermute | solution.py:362
  23.4 0.0 collective-permute-done.5.c2
  23.4 1.3 %collective-permute-start.9 = (bf16[256,384]{1,0:T(8,128)(2,1)S(1)}, bf16[256,384]{1,0:T(8,128)(2,1)S(1)}, u32[]{:S(2)}, u32[]{:S(2)}) collective-permute-start(bf16[256,384]{1,0:T(8,128)(2,1)S(1)} %collective-permute-done.7.c4), channel_id=1, source_target_pairs={{0,2},{1,3},{2,0},{3,1},{4,6},{5,7},{6,4},{7,5},{8,10},{9,11},{10,... | collective-permute-start | bytes 589832 | tf_op jit(solution)/shard_map/ppermute | solution.py:356
  24.8 0.0 collective-permute-done.m0
  24.8 0.2 collective-permute-start.8
  25.0 0.0 collective-permute-done.10.c7
  25.0 1.9 %collective-permute-start.4 = (bf16[3,256,128]{2,1,0:T(8,128)(2,1)S(1)}, bf16[3,256,128]{2,1,0:T(8,128)(2,1)S(1)}, u32[]{:S(2)}, u32[]{:S(2)}) collective-permute-start(bf16[3,256,128]{2,1,0:T(8,128)(2,1)S(1)} %get-tuple-element.50), channel_id=1, source_target_pairs={{0,32},{8,0},{24,16},{32,40},{40,8},{56,24},{64,96},{72,64},{88,80... | collective-permute-start | bytes 589832 | tf_op jit(solution)/shard_map/ppermute | solution.py:362
  26.9 2.8 %collective-permute-done.9.c6 = bf16[256,384]{1,0:T(8,128)(2,1)S(1)} collective-permute-done((bf16[256,384]{1,0:T(8,128)(2,1)S(1)}, bf16[256,384]{1,0:T(8,128)(2,1)S(1)}, u32[]{:S(2)}, u32[]{:S(2)}) %collective-permute-start.9) | collective-permute-done | bytes 196640 | tf_op jit(solution)/shard_map/ppermute | solution.py:356
  29.7 2.0 %collective-permute-done.8.c5 = bf16[256,384]{1,0:T(8,128)(2,1)S(1)} collective-permute-done((bf16[256,384]{1,0:T(8,128)(2,1)S(1)}, bf16[256,384]{1,0:T(8,128)(2,1)S(1)}, u32[]{:S(2)}, u32[]{:S(2)}) %collective-permute-start.8) | collective-permute-done | bytes 196640 | tf_op jit(solution)/shard_map/ppermute | solution.py:356
  31.7 0.0 collective-permute-done.2.m1
  31.7 5.7 %collective-permute-done.3.m2 = bf16[3,256,128]{2,1,0:T(8,128)(2,1)S(1)} collective-permute-done((bf16[3,256,128]{2,1,0:T(8,128)(2,1)S(1)}, bf16[3,256,128]{2,1,0:T(8,128)(2,1)S(1)}, u32[]{:S(2)}, u32[]{:S(2)}) %collective-permute-start.3) | collective-permute-done | bytes 196640 | tf_op jit(solution)/shard_map/ppermute | solution.py:362
  37.4 0.6 collective-permute-done.4.m3
  38.0 0.0 copy-start.8
  38.0 0.0 copy-start.1
  38.1 0.0 copy-start.2
  38.1 0.0 copy-start.7
  38.1 0.1 pad_maximum_fusion
  38.2 2.1 %collective-permute-start.16 = (bf16[4,2,256,128]{3,2,1,0:T(8,128)(2,1)S(1)}, bf16[4,2,256,128]{3,2,1,0:T(8,128)(2,1)S(1)}, u32[]{:S(2)}, u32[]{:S(2)}) collective-permute-start(bf16[4,2,256,128]{3,2,1,0:T(8,128)(2,1)S(1)} %pad_maximum_fusion), channel_id=1, source_target_pairs={{0,8},{8,0},{16,24},{24,16},{32,40},{40,32},{64,72},{72,64},{80,88... | collective-permute-start | bytes 1572872 | tf_op jit(solution)/shard_map/ppermute | solution.py:365
  40.2 3.6 %collective-permute-start.15 = (bf16[4,2,256,128]{3,2,1,0:T(8,128)(2,1)S(1)}, bf16[4,2,256,128]{3,2,1,0:T(8,128)(2,1)S(1)}, u32[]{:S(2)}, u32[]{:S(2)}) collective-permute-start(bf16[4,2,256,128]{3,2,1,0:T(8,128)(2,1)S(1)} %pad_maximum_fusion), channel_id=1, source_target_pairs={{8,64},{24,80},{40,96},{64,8},{72,128},{80,24},{88,144},{96,40},{1... | collective-permute-start | bytes 1572872 | tf_op jit(solution)/shard_map/ppermute | solution.py:366
  43.8 1.9 %project.1 = (bf16[256,128]{1,0:T(8,128)(2,1)S(1)}, bf16[256,128]{1,0:T(8,128)(2,1)S(1)}, bf16[256,128]{1,0:T(8,128)(2,1)S(1)}, bf16[256,128]{1,0:T(8,128)(2,1)S(1)}) custom-call(bf16[256,384]{1,0:T(8,128)(2,1)S(1)} %copy-done.6, bf16[256,384]{1,0:T(8,128)(2,1)S(1)} %collective-permute-done.1.c1, bf16[256,384]{1,0:T(8,128)(2,1)S(1)} %collective-permute-done.5.c2, ...), custom_call_target="tpu_custom_call" | custom-call | tf_op jit(solution)/shard_map/project/pallas_call | solution.py:368
  45.7 1.3 %collective-permute-start.11 = (bf16[256,128]{1,0:T(8,128)(2,1)S(1)}, bf16[256,128]{1,0:T(8,128)(2,1)S(1)}, u32[]{:S(2)}, u32[]{:S(2)}) collective-permute-start(bf16[256,128]{1,0:T(8,128)(2,1)S(1)} %get-tuple-element.64), channel_id=1, source_target_pairs={{0,16},{16,0},{24,32},{32,24},{48,8},{56,40},{64,80},{80,64},{88,9... | collective-permute-start | bytes 196616 | tf_op jit(solution)/shard_map/ppermute | solution.py:376
  47.0 4.5 %collective-permute-start.12 = (bf16[256,128]{1,0:T(8,128)(2,1)S(1)}, bf16[256,128]{1,0:T(8,128)(2,1)S(1)}, u32[]{:S(2)}, u32[]{:S(2)}) collective-permute-start(bf16[256,128]{1,0:T(8,128)(2,1)S(1)} %get-tuple-element.65), channel_id=1, source_target_pairs={{0,0},{8,32},{16,16},{32,8},{40,40},{48,24},{64,64},{72,96},{80,80... | collective-permute-start | bytes 196616 | tf_op jit(solution)/shard_map/ppermute | solution.py:376
  51.5 1.9 %collective-permute-start.13 = (bf16[256,128]{1,0:T(8,128)(2,1)S(1)}, bf16[256,128]{1,0:T(8,128)(2,1)S(1)}, u32[]{:S(2)}, u32[]{:S(2)}) collective-permute-start(bf16[256,128]{1,0:T(8,128)(2,1)S(1)} %get-tuple-element.66), channel_id=1, source_target_pairs={{8,16},{16,32},{24,0},{40,24},{48,40},{56,8},{72,80},{80,96},{88,6... | collective-permute-start | bytes 196616 | tf_op jit(solution)/shard_map/ppermute | solution.py:376
  53.5 0.0 collective-permute-done.16.core_kv
  53.5 2.1 %collective-permute-start.14 = (bf16[256,128]{1,0:T(8,128)(2,1)S(1)}, bf16[256,128]{1,0:T(8,128)(2,1)S(1)}, u32[]{:S(2)}, u32[]{:S(2)}) collective-permute-start(bf16[256,128]{1,0:T(8,128)(2,1)S(1)} %get-tuple-element.67), channel_id=1, source_target_pairs={{0,32},{8,0},{24,16},{32,40},{40,8},{56,24},{64,96},{72,64},{88,80... | collective-permute-start | bytes 196616 | tf_op jit(solution)/shard_map/ppermute | solution.py:376
  55.6 0.1 copy.14.tb_ref
  55.8 0.0 collective-permute-done.15.time_kv
  55.8 4.7 %softmax_stats.1 = (f32[1,1024]{1,0:T(1,128)S(1)}, f32[128,1024]{1,0:T(8,128)S(1)}) custom-call(s32[3,3]{1,0:T(4,128)S(1)} %copy-done.7, bf16[3,256,128]{2,1,0:T(8,128)(2,1)S(1)} %collective-permute-done.m0, bf16[3,256,128]{2,1,0:T(8,128)(2,1)S(1)} %collective-permute-done.2.m1, bf16[3,256,128]{2,1,0:T(8,128)(2,1)S(1)} %collective-permute-done.3.m2, ...), custom_call_target="tpu_custom_call" | custom-call | flops 1000 | bytes 1000 | tf_op jit(solution)/shard_map/softmax_stats/pallas_call | solution.py:378
  60.5 0.0 collective-permute-done.11.g0
  60.5 0.0 collective-permute-done.12.g1
  60.5 0.0 collective-permute-done.13.g2
  60.5 1.9 %collective-permute-done.14.g3 = bf16[256,128]{1,0:T(8,128)(2,1)S(1)} collective-permute-done((bf16[256,128]{1,0:T(8,128)(2,1)S(1)}, bf16[256,128]{1,0:T(8,128)(2,1)S(1)}, u32[]{:S(2)}, u32[]{:S(2)}) %collective-permute-start.14) | collective-permute-done | bytes 65568 | tf_op jit(solution)/shard_map/ppermute | solution.py:376
  62.5 3.6 %far_grads.1 = (bf16[4,2,256,128]{3,2,1,0:T(8,128)(2,1)S(1)}, bf16[256,256]{1,0:T(8,128)(2,1)S(1)}, f32[128,1024]{1,0:T(8,128)S(1)}, f32[1,1024]{1,0:T(1,128)S(1)}, bf16[1024,128]{1,0:T(8,128)(2,1)S(1)}) custom-call(s32[3,3]{1,0:T(4,128)S(1)} %copy-done.7, bf16[3,256,128]{2,1,0:T(8,128)(2,1)S(1)} %collective-permute-done.m0, ...), custom_call_target="tpu_custom_call" | custom-call | flops 1000 | bytes 1000 | tf_op jit(solution)/shard_map/far_grads/pallas_call | solution.py:403
  66.1 4.0 %collective-permute-start.18 = (bf16[4,2,256,128]{3,2,1,0:T(8,128)(2,1)S(1)}, bf16[4,2,256,128]{3,2,1,0:T(8,128)(2,1)S(1)}, u32[]{:S(2)}, u32[]{:S(2)}) collective-permute-start(bf16[4,2,256,128]{3,2,1,0:T(8,128)(2,1)S(1)} %get-tuple-element.77), channel_id=1, source_target_pairs={{8,64},{24,80},{40,96},{64,8},{72,128},{80,24},{88,144},{96,40},{1... | collective-permute-start | bytes 1572872 | tf_op jit(solution)/shard_map/ppermute | solution.py:419
  70.0 4.9 %own_grads.1 = (bf16[4,2,256,128]{3,2,1,0:T(8,128)(2,1)S(1)}, f32[4,3,256,128]{3,2,1,0:T(8,128)S(1)}) custom-call(s32[3,3]{1,0:T(4,128)S(1)} %copy-done.7, bf16[3,256,128]{2,1,0:T(8,128)(2,1)S(1)} %collective-permute-done.m0, bf16[3,256,128]{2,1,0:T(8,128)(2,1)S(1)} %collective-permute-done.2.m1, bf16[3,256,128]{2,1,0:T(8,128)(2,1)S(1)} %collective-permute-done.3.m2, ...), custom_call_target="tpu_custom_call" | custom-call | flops 1000 | bytes 1000 | tf_op jit(solution)/shard_map/own_grads/pallas_call | solution.py:420
  74.9 1.9 %collective-permute-start.17 = (bf16[4,2,256,128]{3,2,1,0:T(8,128)(2,1)S(1)}, bf16[4,2,256,128]{3,2,1,0:T(8,128)(2,1)S(1)}, u32[]{:S(2)}, u32[]{:S(2)}) collective-permute-start(bf16[4,2,256,128]{3,2,1,0:T(8,128)(2,1)S(1)} %get-tuple-element.76), channel_id=1, source_target_pairs={{0,8},{8,0},{16,24},{24,16},{32,40},{40,32},{64,72},{72,64},{80,88... | collective-permute-start | bytes 1572872 | tf_op jit(solution)/shard_map/ppermute | solution.py:431
  76.9 8.2 %all_to_all.5.text = bf16[8,32,256]{2,1,0:T(8,128)(2,1)S(1)} all-to-all(bf16[8,32,256]{2,1,0:T(8,128)(2,1)S(1)} %bitcast.10), channel_id=1, replica_groups={{0,8,64,72,128,136,192,200},{16,24,80,88,144,152,208,216},{32,40,96,104..., dimensions={0} | all-to-all | bytes 262144 | tf_op jit(solution)/shard_map/all_to_all | solution.py:433
  85.0 0.0 collective-permute-done.18.time
  85.0 0.0 collective-permute-done.17.core
  85.0 0.2 combine.1
  85.3 1.3 %collective-permute-start.19 = (bf16[784,128]{1,0:T(8,128)(2,1)S(1)}, bf16[784,128]{1,0:T(8,128)(2,1)S(1)}, u32[]{:S(2)}, u32[]{:S(2)}) collective-permute-start(bf16[784,128]{1,0:T(8,128)(2,1)S(1)} %get-tuple-element.79), channel_id=1, source_target_pairs={{16,0},{0,16},{32,24},{24,32},{8,48},{40,56},{80,64},{64,80},{96,8... | collective-permute-start | bytes 602120 | tf_op jit(solution)/shard_map/ppermute | solution.py:446
  86.6 7.8 %collective-permute-start.20 = (bf16[784,128]{1,0:T(8,128)(2,1)S(1)}, bf16[784,128]{1,0:T(8,128)(2,1)S(1)}, u32[]{:S(2)}, u32[]{:S(2)}) collective-permute-start(bf16[784,128]{1,0:T(8,128)(2,1)S(1)} %get-tuple-element.80), channel_id=1, source_target_pairs={{0,0},{32,8},{16,16},{8,32},{40,40},{24,48},{64,64},{96,72},{80,80... | collective-permute-start | bytes 602120 | tf_op jit(solution)/shard_map/ppermute | solution.py:446
  94.4 1.9 %collective-permute-start.21 = (bf16[784,128]{1,0:T(8,128)(2,1)S(1)}, bf16[784,128]{1,0:T(8,128)(2,1)S(1)}, u32[]{:S(2)}, u32[]{:S(2)}) collective-permute-start(bf16[784,128]{1,0:T(8,128)(2,1)S(1)} %get-tuple-element.81), channel_id=1, source_target_pairs={{16,8},{32,16},{0,24},{24,40},{40,48},{8,56},{80,72},{96,80},{64,8... | collective-permute-start | bytes 602120 | tf_op jit(solution)/shard_map/ppermute | solution.py:446
  96.4 1.9 %collective-permute-start.22 = (bf16[784,128]{1,0:T(8,128)(2,1)S(1)}, bf16[784,128]{1,0:T(8,128)(2,1)S(1)}, u32[]{:S(2)}, u32[]{:S(2)}) collective-permute-start(bf16[784,128]{1,0:T(8,128)(2,1)S(1)} %get-tuple-element.82), channel_id=1, source_target_pairs={{32,0},{0,8},{16,24},{40,32},{8,40},{24,56},{96,64},{64,72},{80,88... | collective-permute-start | bytes 602120 | tf_op jit(solution)/shard_map/ppermute | solution.py:446
  98.3 0.0 collective-permute-done.19.r0
  98.3 0.0 collective-permute-done.20.r1
  98.3 10.7 %collective-permute-done.21.r2 = bf16[784,128]{1,0:T(8,128)(2,1)S(1)} collective-permute-done((bf16[784,128]{1,0:T(8,128)(2,1)S(1)}, bf16[784,128]{1,0:T(8,128)(2,1)S(1)}, u32[]{:S(2)}, u32[]{:S(2)}) %collective-permute-start.21) | collective-permute-done | bytes 200736 | tf_op jit(solution)/shard_map/ppermute | solution.py:446
  109.0 0.0 collective-permute-done.22.r3
  109.1 1.1 unpack.1
  (13 shorter events, 0.1 us)
Async XLA Ops:
  0.6 43.2 %copy-start = (bf16[384,3072]{1,0:T(8,128)(2,1)S(1)}, bf16[384,3072]{1,0:T(8,128)(2,1)}, u32[]{:S(2)}) copy-start(bf16[384,3072]{1,0:T(8,128)(2,1)} %w_ref.1) | copy-start | bytes 7077892
  0.6 8.8 %collective-permute-start.7 = (bf16[256,384]{1,0:T(8,128)(2,1)}, bf16[256,384]{1,0:T(8,128)(2,1)S(1)}, u32[]{:S(2)}, u32[]{:S(2)}) collective-permute-start(bf16[256,384]{1,0:T(8,128)(2,1)} %c0), channel_id=1, source_target_pairs={{0,4},{1,5},{2,6},{3,7},{4,0},{5,1},{6,2},{7,3},{8,12},{9,13},{10,... | collective-permute-start | bytes 589832 | tf_op jit(solution)/shard_map/ppermute | solution.py:354
  0.7 9.6 %collective-permute-start.1 = (bf16[256,384]{1,0:T(8,128)(2,1)}, bf16[256,384]{1,0:T(8,128)(2,1)S(1)}, u32[]{:S(2)}, u32[]{:S(2)}) collective-permute-start(bf16[256,384]{1,0:T(8,128)(2,1)} %c0), channel_id=1, source_target_pairs={{0,1},{1,2},{2,3},{3,0},{4,5},{5,6},{6,7},{7,4},{8,9},{9,10},{10,1... | collective-permute-start | bytes 589832 | tf_op jit(solution)/shard_map/ppermute | solution.py:356
  2.0 19.5 %collective-permute-start.6 = (bf16[256,384]{1,0:T(8,128)(2,1)}, bf16[256,384]{1,0:T(8,128)(2,1)S(1)}, u32[]{:S(2)}, u32[]{:S(2)}) collective-permute-start(bf16[256,384]{1,0:T(8,128)(2,1)} %c0), channel_id=1, source_target_pairs={{0,3},{1,0},{2,1},{3,2},{4,7},{5,4},{6,5},{7,6},{8,11},{9,8},{10,9... | collective-permute-start | bytes 589832 | tf_op jit(solution)/shard_map/ppermute | solution.py:356
  3.5 19.9 %collective-permute-start.5 = (bf16[256,384]{1,0:T(8,128)(2,1)}, bf16[256,384]{1,0:T(8,128)(2,1)S(1)}, u32[]{:S(2)}, u32[]{:S(2)}) collective-permute-start(bf16[256,384]{1,0:T(8,128)(2,1)} %c0), channel_id=1, source_target_pairs={{0,2},{1,3},{2,0},{3,1},{4,6},{5,7},{6,4},{7,5},{8,10},{9,11},{10,... | collective-permute-start | bytes 589832 | tf_op jit(solution)/shard_map/ppermute | solution.py:356
  5.0 0.9 copy-start.3
  6.0 0.9 copy-start.4
  6.9 0.9 copy-start.5
  7.8 36.0 %copy-start.6 = (bf16[256,384]{1,0:T(8,128)(2,1)S(1)}, bf16[256,384]{1,0:T(8,128)(2,1)}, u32[]{:S(2)}) copy-start(bf16[256,384]{1,0:T(8,128)(2,1)} %c0) | copy-start | bytes 589828
  8.1 16.7 %collective-permute-start = (bf16[3,256,128]{2,1,0:T(8,128)(2,1)S(1)}, bf16[3,256,128]{2,1,0:T(8,128)(2,1)S(1)}, u32[]{:S(2)}, u32[]{:S(2)}) collective-permute-start(bf16[3,256,128]{2,1,0:T(8,128)(2,1)S(1)} %get-tuple-element.44), channel_id=1, source_target_pairs={{0,16},{16,0},{24,32},{32,24},{48,8},{56,40},{64,80},{80,64},{88,9... | collective-permute-start | bytes 589832 | tf_op jit(solution)/shard_map/ppermute | solution.py:362
  9.4 15.6 %collective-permute-start.10 = (bf16[256,384]{1,0:T(8,128)(2,1)S(1)}, bf16[256,384]{1,0:T(8,128)(2,1)S(1)}, u32[]{:S(2)}, u32[]{:S(2)}) collective-permute-start(bf16[256,384]{1,0:T(8,128)(2,1)S(1)} %collective-permute-done.7.c4), channel_id=1, source_target_pairs={{0,3},{1,0},{2,1},{3,2},{4,7},{5,4},{6,5},{7,6},{8,11},{9,8},{10,9... | collective-permute-start | bytes 589832 | tf_op jit(solution)/shard_map/ppermute | solution.py:356
  10.3 21.3 %collective-permute-start.2 = (bf16[3,256,128]{2,1,0:T(8,128)(2,1)S(1)}, bf16[3,256,128]{2,1,0:T(8,128)(2,1)S(1)}, u32[]{:S(2)}, u32[]{:S(2)}) collective-permute-start(bf16[3,256,128]{2,1,0:T(8,128)(2,1)S(1)} %get-tuple-element.48), channel_id=1, source_target_pairs={{0,0},{8,32},{16,16},{32,8},{40,40},{48,24},{64,64},{72,96},{80,80... | collective-permute-start | bytes 589832 | tf_op jit(solution)/shard_map/ppermute | solution.py:362
  21.5 15.9 %collective-permute-start.3 = (bf16[3,256,128]{2,1,0:T(8,128)(2,1)S(1)}, bf16[3,256,128]{2,1,0:T(8,128)(2,1)S(1)}, u32[]{:S(2)}, u32[]{:S(2)}) collective-permute-start(bf16[3,256,128]{2,1,0:T(8,128)(2,1)S(1)} %get-tuple-element.49), channel_id=1, source_target_pairs={{8,16},{16,32},{24,0},{40,24},{48,40},{56,8},{72,80},{80,96},{88,6... | collective-permute-start | bytes 589832 | tf_op jit(solution)/shard_map/ppermute | solution.py:362
  23.4 6.2 %collective-permute-start.9 = (bf16[256,384]{1,0:T(8,128)(2,1)S(1)}, bf16[256,384]{1,0:T(8,128)(2,1)S(1)}, u32[]{:S(2)}, u32[]{:S(2)}) collective-permute-start(bf16[256,384]{1,0:T(8,128)(2,1)S(1)} %collective-permute-done.7.c4), channel_id=1, source_target_pairs={{0,2},{1,3},{2,0},{3,1},{4,6},{5,7},{6,4},{7,5},{8,10},{9,11},{10,... | collective-permute-start | bytes 589832 | tf_op jit(solution)/shard_map/ppermute | solution.py:356
  24.8 6.9 %collective-permute-start.8 = (bf16[256,384]{1,0:T(8,128)(2,1)S(1)}, bf16[256,384]{1,0:T(8,128)(2,1)S(1)}, u32[]{:S(2)}, u32[]{:S(2)}) collective-permute-start(bf16[256,384]{1,0:T(8,128)(2,1)S(1)} %collective-permute-done.7.c4), channel_id=1, source_target_pairs={{0,1},{1,2},{2,3},{3,0},{4,5},{5,6},{6,7},{7,4},{8,9},{9,10},{10,1... | collective-permute-start | bytes 589832 | tf_op jit(solution)/shard_map/ppermute | solution.py:356
  25.0 13.0 %collective-permute-start.4 = (bf16[3,256,128]{2,1,0:T(8,128)(2,1)S(1)}, bf16[3,256,128]{2,1,0:T(8,128)(2,1)S(1)}, u32[]{:S(2)}, u32[]{:S(2)}) collective-permute-start(bf16[3,256,128]{2,1,0:T(8,128)(2,1)S(1)} %get-tuple-element.50), channel_id=1, source_target_pairs={{0,32},{8,0},{24,16},{32,40},{40,8},{56,24},{64,96},{72,64},{88,80... | collective-permute-start | bytes 589832 | tf_op jit(solution)/shard_map/ppermute | solution.py:362
  38.0 17.6 %copy-start.8 = (s32[256]{0:T(256)S(1)}, s32[256]{0:T(256)}, u32[]{:S(2)}) copy-start(s32[256]{0:T(256)} %param.17) | copy-start | bytes 3076
  38.0 17.7 %copy-start.1 = (bf16[256,384]{1,0:T(8,128)(2,1)S(1)}, bf16[256,384]{1,0:T(8,128)(2,1)}, u32[]{:S(2)}) copy-start(bf16[256,384]{1,0:T(8,128)(2,1)} %tk_ref.3) | copy-start | bytes 589828
  38.1 17.7 %copy-start.2 = (bf16[256,384]{1,0:T(8,128)(2,1)S(1)}, bf16[256,384]{1,0:T(8,128)(2,1)}, u32[]{:S(2)}) copy-start(bf16[256,384]{1,0:T(8,128)(2,1)} %tv_ref.3) | copy-start | bytes 589828
  38.1 17.7 %copy-start.7 = (s32[3,3]{1,0:T(4,128)S(1)}, s32[3,3]{1,0:T(4,128)}, u32[]{:S(2)}) copy-start(s32[3,3]{1,0:T(4,128)} %ext_ref.5) | copy-start | bytes 112
  38.2 15.3 %collective-permute-start.16 = (bf16[4,2,256,128]{3,2,1,0:T(8,128)(2,1)S(1)}, bf16[4,2,256,128]{3,2,1,0:T(8,128)(2,1)S(1)}, u32[]{:S(2)}, u32[]{:S(2)}) collective-permute-start(bf16[4,2,256,128]{3,2,1,0:T(8,128)(2,1)S(1)} %pad_maximum_fusion), channel_id=1, source_target_pairs={{0,8},{8,0},{16,24},{24,16},{32,40},{40,32},{64,72},{72,64},{80,88... | collective-permute-start | bytes 1572872 | tf_op jit(solution)/shard_map/ppermute | solution.py:365
  40.2 15.5 %collective-permute-start.15 = (bf16[4,2,256,128]{3,2,1,0:T(8,128)(2,1)S(1)}, bf16[4,2,256,128]{3,2,1,0:T(8,128)(2,1)S(1)}, u32[]{:S(2)}, u32[]{:S(2)}) collective-permute-start(bf16[4,2,256,128]{3,2,1,0:T(8,128)(2,1)S(1)} %pad_maximum_fusion), channel_id=1, source_target_pairs={{8,64},{24,80},{40,96},{64,8},{72,128},{80,24},{88,144},{96,40},{1... | collective-permute-start | bytes 1572872 | tf_op jit(solution)/shard_map/ppermute | solution.py:366
  45.7 14.8 %collective-permute-start.11 = (bf16[256,128]{1,0:T(8,128)(2,1)S(1)}, bf16[256,128]{1,0:T(8,128)(2,1)S(1)}, u32[]{:S(2)}, u32[]{:S(2)}) collective-permute-start(bf16[256,128]{1,0:T(8,128)(2,1)S(1)} %get-tuple-element.64), channel_id=1, source_target_pairs={{0,16},{16,0},{24,32},{32,24},{48,8},{56,40},{64,80},{80,64},{88,9... | collective-permute-start | bytes 196616 | tf_op jit(solution)/shard_map/ppermute | solution.py:376
  47.0 13.5 %collective-permute-start.12 = (bf16[256,128]{1,0:T(8,128)(2,1)S(1)}, bf16[256,128]{1,0:T(8,128)(2,1)S(1)}, u32[]{:S(2)}, u32[]{:S(2)}) collective-permute-start(bf16[256,128]{1,0:T(8,128)(2,1)S(1)} %get-tuple-element.65), channel_id=1, source_target_pairs={{0,0},{8,32},{16,16},{32,8},{40,40},{48,24},{64,64},{72,96},{80,80... | collective-permute-start | bytes 196616 | tf_op jit(solution)/shard_map/ppermute | solution.py:376
  51.5 9.0 %collective-permute-start.13 = (bf16[256,128]{1,0:T(8,128)(2,1)S(1)}, bf16[256,128]{1,0:T(8,128)(2,1)S(1)}, u32[]{:S(2)}, u32[]{:S(2)}) collective-permute-start(bf16[256,128]{1,0:T(8,128)(2,1)S(1)} %get-tuple-element.66), channel_id=1, source_target_pairs={{8,16},{16,32},{24,0},{40,24},{48,40},{56,8},{72,80},{80,96},{88,6... | collective-permute-start | bytes 196616 | tf_op jit(solution)/shard_map/ppermute | solution.py:376
  53.5 9.0 %collective-permute-start.14 = (bf16[256,128]{1,0:T(8,128)(2,1)S(1)}, bf16[256,128]{1,0:T(8,128)(2,1)S(1)}, u32[]{:S(2)}, u32[]{:S(2)}) collective-permute-start(bf16[256,128]{1,0:T(8,128)(2,1)S(1)} %get-tuple-element.67), channel_id=1, source_target_pairs={{0,32},{8,0},{24,16},{32,40},{40,8},{56,24},{64,96},{72,64},{88,80... | collective-permute-start | bytes 196616 | tf_op jit(solution)/shard_map/ppermute | solution.py:376
  66.1 19.0 %collective-permute-start.18 = (bf16[4,2,256,128]{3,2,1,0:T(8,128)(2,1)S(1)}, bf16[4,2,256,128]{3,2,1,0:T(8,128)(2,1)S(1)}, u32[]{:S(2)}, u32[]{:S(2)}) collective-permute-start(bf16[4,2,256,128]{3,2,1,0:T(8,128)(2,1)S(1)} %get-tuple-element.77), channel_id=1, source_target_pairs={{8,64},{24,80},{40,96},{64,8},{72,128},{80,24},{88,144},{96,40},{1... | collective-permute-start | bytes 1572872 | tf_op jit(solution)/shard_map/ppermute | solution.py:419
  74.9 10.1 %collective-permute-start.17 = (bf16[4,2,256,128]{3,2,1,0:T(8,128)(2,1)S(1)}, bf16[4,2,256,128]{3,2,1,0:T(8,128)(2,1)S(1)}, u32[]{:S(2)}, u32[]{:S(2)}) collective-permute-start(bf16[4,2,256,128]{3,2,1,0:T(8,128)(2,1)S(1)} %get-tuple-element.76), channel_id=1, source_target_pairs={{0,8},{8,0},{16,24},{24,16},{32,40},{40,32},{64,72},{72,64},{80,88... | collective-permute-start | bytes 1572872 | tf_op jit(solution)/shard_map/ppermute | solution.py:431
  85.3 13.0 %collective-permute-start.19 = (bf16[784,128]{1,0:T(8,128)(2,1)S(1)}, bf16[784,128]{1,0:T(8,128)(2,1)S(1)}, u32[]{:S(2)}, u32[]{:S(2)}) collective-permute-start(bf16[784,128]{1,0:T(8,128)(2,1)S(1)} %get-tuple-element.79), channel_id=1, source_target_pairs={{16,0},{0,16},{32,24},{24,32},{8,48},{40,56},{80,64},{64,80},{96,8... | collective-permute-start | bytes 602120 | tf_op jit(solution)/shard_map/ppermute | solution.py:446
  86.6 11.7 %collective-permute-start.20 = (bf16[784,128]{1,0:T(8,128)(2,1)S(1)}, bf16[784,128]{1,0:T(8,128)(2,1)S(1)}, u32[]{:S(2)}, u32[]{:S(2)}) collective-permute-start(bf16[784,128]{1,0:T(8,128)(2,1)S(1)} %get-tuple-element.80), channel_id=1, source_target_pairs={{0,0},{32,8},{16,16},{8,32},{40,40},{24,48},{64,64},{96,72},{80,80... | collective-permute-start | bytes 602120 | tf_op jit(solution)/shard_map/ppermute | solution.py:446
  94.4 14.6 %collective-permute-start.21 = (bf16[784,128]{1,0:T(8,128)(2,1)S(1)}, bf16[784,128]{1,0:T(8,128)(2,1)S(1)}, u32[]{:S(2)}, u32[]{:S(2)}) collective-permute-start(bf16[784,128]{1,0:T(8,128)(2,1)S(1)} %get-tuple-element.81), channel_id=1, source_target_pairs={{16,8},{32,16},{0,24},{24,40},{40,48},{8,56},{80,72},{96,80},{64,8... | collective-permute-start | bytes 602120 | tf_op jit(solution)/shard_map/ppermute | solution.py:446
  96.4 12.7 %collective-permute-start.22 = (bf16[784,128]{1,0:T(8,128)(2,1)S(1)}, bf16[784,128]{1,0:T(8,128)(2,1)S(1)}, u32[]{:S(2)}, u32[]{:S(2)}) collective-permute-start(bf16[784,128]{1,0:T(8,128)(2,1)S(1)} %get-tuple-element.82), channel_id=1, source_target_pairs={{32,0},{0,8},{16,24},{40,32},{8,40},{24,56},{96,64},{64,72},{80,88... | collective-permute-start | bytes 602120 | tf_op jit(solution)/shard_map/ppermute | solution.py:446

commit v3 on v2

--- a/solution.py
+++ b/solution.py
@@ -65,6 +65,21 @@
     return pairs
 
 
+def pair_head(far, h):
+    return ((h >> 1) ^ far) + 2 * (h & 1)
+
+
+def pair_pairs(far):
+    pairs = []
+    for y in range(4):
+        for zt in range(2):
+            for h in range(4):
+                head = pair_head(far, h)
+                if head < 3:
+                    pairs.append((y * 8 + zt * 4 + h, y * 8 + head * 2 + zt))
+    return pairs
+
+
 def back_pairs(phase):
     return [(b, a) for a, b in out_pairs(phase)]
 
@@ -106,28 +121,28 @@
     return (lax.axis_index("seq") >> 1) & 3
 
 
-def pack_kernel(q_ref, k_ref, v_ref, o0, o1, o2, o3, sem):
+def pack_kernel(q_ref, k_ref, v_ref, q_next, k_next, v_next, far_out, near_out):
     h = home_height()
-    copies = []
-    for phase, out in enumerate((o0, o1, o2, o3)):
-        head = jnp.minimum(sent_head(phase, h), 2)
+    core = h & 1
+    mine = pl.ds(pl.multiple_of(core * TOK, TOK), TOK)
+    theirs = pl.ds(pl.multiple_of((1 - core) * TOK, TOK), TOK)
+    for far, out in ((1, far_out), (0, near_out)):
+        head = jnp.minimum(pair_head(far, h), 2)
         columns = pl.ds(pl.multiple_of(head * DH, DH), DH)
-        for which, src in enumerate((q_ref, k_ref, v_ref)):
-            copies.append(
-                pltpu.make_async_copy(src.at[:, columns], out.at[which], sem.at[phase * 3 + which])
-            )
-    start_all(copies)
-    wait_all(copies)
-
-
-def project_kernel(c0, c1, c2, c3, c4, c5, c6, c7, w_ref, o0, o1, o2, o3):
+        for which, (own, other) in enumerate(((q_ref, q_next), (k_ref, k_next), (v_ref, v_next))):
+            out[which, mine, :] = own[:, columns]
+            out[which, theirs, :] = other[:, columns]
+
+
+def project_kernel(c0, c1, c2, c3, c4, c5, c6, c7, w_ref, keep, give):
     chunks = (c0, c1, c2, c3, c4, c5, c6, c7)
     g = lax.axis_index("head")
     h = home_height()
     gz, gx = lax.div(g, 4), lax.rem(g, 4)
     width = c0.shape[1]
-    for phase, out in enumerate((o0, o1, o2, o3)):
-        head = jnp.minimum(sent_head(phase, h), 2)
+    for which_out in range(4):
+        far, other = which_out & 1, which_out >> 1
+        head = jnp.minimum(pair_head(far, h ^ other), 2)
         rows = pl.ds(pl.multiple_of(head * DH, DH), DH)
         total = None
         for which, chunk in enumerate(chunks):
@@ -136,7 +151,21 @@
             columns = pl.ds(pl.multiple_of(src * width, width), width)
             term = dot_nt(chunk[...], w_ref[rows, columns])
             total = term if total is None else total + term
-        out[...] = total.astype(BF16)
+        (give if other else keep)[far] = total.astype(BF16)
+
+
+def assemble_kernel(keep, got, near, far):
+    core = home_height() & 1
+    mine = pl.ds(pl.multiple_of(core * TOK, TOK), TOK)
+    theirs = pl.ds(pl.multiple_of((1 - core) * TOK, TOK), TOK)
+    for which, out in enumerate((near, far)):
+        out[mine, :] = keep[which]
+        out[theirs, :] = got[which]
+
+
+def pair_rows(chip):
+    firsts = [2 * ((chip & 1) ^ far) for far in (1, 0)]
+    return [(which, first, row, slice(row * TOK, (row + 1) * TOK)) for which, first in enumerate(firsts) for row in (0, 1)]
 
 
 def window(ext_ref, chip):
@@ -173,17 +202,18 @@
 
 
 def stats_kernel(
-    ext_ref, m0, m1, m2, m3, core_kv, time_kv, tk_ref, tv_ref, tb_ref,
+    ext_ref, m_far, m_near, core_kv, time_kv, tk_ref, tv_ref, tb_ref,
     lse_ref, mean_ref,
     kb, vb, qb, sb, st, run,
 ):
     chip = work_chip()
-    for phase, msg in enumerate((m0, m1, m2, m3)):
-        h = received_height(phase, chip)
-        qb[pl.ds(pl.multiple_of(h * TOK, TOK), TOK), :] = msg[0]
-        kb[h], vb[h] = msg[1], msg[2]
-        kb[4 + h], vb[4 + h] = core_kv[phase, 0], core_kv[phase, 1]
-        kb[8 + h], vb[8 + h] = time_kv[phase, 0], time_kv[phase, 1]
+    msgs = (m_far, m_near)
+    for which, first, row, part in pair_rows(chip):
+        h = first + row
+        qb[pl.ds(pl.multiple_of(h * TOK, TOK), TOK), :] = msgs[which][0, part]
+        kb[h], vb[h] = msgs[which][1, part], msgs[which][2, part]
+        kb[4 + h], vb[4 + h] = core_kv[which, 0, part], core_kv[which, 1, part]
+        kb[8 + h], vb[8 + h] = time_kv[which, 0, part], time_kv[which, 1, part]
     block_ok, reach_h, wide = window(ext_ref, chip)
     head = jnp.minimum(chip, 2)
     columns = pl.ds(pl.multiple_of(head * DH, DH), DH)
@@ -241,18 +271,17 @@
     return probs.astype(BF16), dscores
 
 
-def place_rows(chip, refs, out):
-    for phase, ref in enumerate(refs):
-        rows = pl.ds(pl.multiple_of(received_height(phase, chip) * TOK, TOK), TOK)
-        out[rows, :] = ref[...]
+def place_rows(chip, far_rows, near_rows, out):
+    for far, rows in ((1, far_rows), (0, near_rows)):
+        first = 2 * ((chip & 1) ^ far)
+        out[pl.ds(pl.multiple_of(first * TOK, 2 * TOK), 2 * TOK), :] = rows
 
 
 def part_grads(part, m_refs, kv_ref, ext_ref, lse_ref, delta_ref, out_ref, dq_ref, kb, vb, qb, gb):
     chip = work_chip()
-    for phase in range(4):
-        h = received_height(phase, chip)
-        kb[h] = m_refs[phase][1] if part == 0 else kv_ref[phase, 0]
-        vb[h] = m_refs[phase][2] if part == 0 else kv_ref[phase, 1]
+    for which, first, row, rows in pair_rows(chip):
+        kb[first + row] = m_refs[which][1, rows] if part == 0 else kv_ref[which, 0, rows]
+        vb[first + row] = m_refs[which][2, rows] if part == 0 else kv_ref[which, 1, rows]
     block_ok, reach_h, wide = window(ext_ref, chip)
     factor = INV_ROOT * LOG2E
 
@@ -274,14 +303,14 @@
 
 
 def time_grads_kernel(
-    ext_ref, m0, m1, m2, m3, g0, g1, g2, g3, time_kv, lse_ref, mean_ref, tk_ref, tv_ref, tb_ref,
+    ext_ref, m_far, m_near, g_far, g_near, time_kv, lse_ref, mean_ref, tk_ref, tv_ref, tb_ref,
     time_out, text_ref, dq_ref, delta_ref, gb,
     kb, vb, qb,
 ):
     chip = work_chip()
-    m_refs = (m0, m1, m2, m3)
-    place_rows(chip, [ref.at[0] for ref in m_refs], qb)
-    place_rows(chip, (g0, g1, g2, g3), gb)
+    m_refs = (m_far, m_near)
+    place_rows(chip, m_far[0], m_near[0], qb)
+    place_rows(chip, g_far[...], g_near[...], gb)
     delta_ref[...] = jnp.sum(gb[...].astype(F32).T * mean_ref[...], 0, keepdims=True)
     head = jnp.minimum(chip, 2)
     columns = pl.ds(pl.multiple_of(head * DH, DH), DH)
@@ -297,12 +326,12 @@
 
 
 def near_grads_kernel(
-    ext_ref, m0, m1, m2, m3, core_kv, lse_ref, dq_in, delta_ref, gb,
+    ext_ref, m_far, m_near, core_kv, lse_ref, dq_in, delta_ref, gb,
     core_out, own_out,
     kb, vb, qb, dq_run,
 ):
-    m_refs = (m0, m1, m2, m3)
-    place_rows(work_chip(), [ref.at[0] for ref in m_refs], qb)
+    m_refs = (m_far, m_near)
+    place_rows(work_chip(), m_far[0], m_near[0], qb)
     dq_run[...] = dq_in[...]
     part_grads(1, m_refs, core_kv, ext_ref, lse_ref, delta_ref, core_out, dq_run, kb, vb, qb, gb)
     part_grads(0, m_refs, None, ext_ref, lse_ref, delta_ref, own_out, dq_run, kb, vb, qb, gb)
@@ -338,18 +367,7 @@
 
 
 def per_device(queries, keys, values, layer_grad, out_weight, text_keys, text_values, extents, text_mask):
-    block = sds((TOK, DH), BF16)
     text_bias = jnp.where(text_mask == 1, 0.0, -jnp.inf).astype(F32)[:, None]
-
-    packed = pl.pallas_call(
-        pack_kernel,
-        in_specs=[ANY] * 3,
-        out_specs=[ANY] * 4,
-        out_shape=[sds((3, TOK, DH), BF16)] * 4,
-        scratch_shapes=[pltpu.SemaphoreType.DMA((12,))],
-        compiler_params=params(),
-        name="pack_heads",
-    )(queries, keys, values)
 
     beside = lax.ppermute(layer_grad, "head", head_pairs(0, 1))
     chunks = [
@@ -357,27 +375,46 @@
         for src in (layer_grad, beside)
         for dx in range(4)
     ]
+    both = [(s, s ^ 1) for s in range(32)]
+    inputs = (queries, keys, values)
+    packed = pl.pallas_call(
+        pack_kernel,
+        in_specs=[VMEM] * 6,
+        out_specs=[VMEM] * 2,
+        out_shape=[sds((3, 2 * TOK, DH), BF16)] * 2,
+        compiler_params=params(),
+        name="pack_heads",
+    )(*inputs, *(lax.ppermute(one, "seq", both) for one in inputs))
     packed = list(packed)
-    packed[1:], chunks[1] = lax.optimization_barrier((packed[1:], chunks[1]))
-    msgs = [lax.ppermute(one, "seq", out_pairs(phase)) for phase, one in enumerate(packed)]
+    packed[1], chunks[1] = lax.optimization_barrier((packed[1], chunks[1]))
+    msgs = [lax.ppermute(one, "seq", pair_pairs(which)) for which, one in zip((1, 0), packed)]
     msgs, chunks = lax.optimization_barrier((msgs, chunks))
     kv = jnp.stack([one[1:] for one in msgs])
     core_kv = lax.ppermute(kv, "seq", core_pairs())
     time_kv = lax.ppermute(kv, "seq", time_pairs())
 
-    grads = pl.pallas_call(
+    keep, give = pl.pallas_call(
         project_kernel,
         in_specs=[VMEM] * 9,
-        out_specs=[VMEM] * 4,
-        out_shape=[block] * 4,
+        out_specs=[VMEM] * 2,
+        out_shape=[sds((2, TOK, DH), BF16)] * 2,
         compiler_params=params(),
         name="project",
     )(*chunks, out_weight)
-    grads = [lax.ppermute(one, "seq", out_pairs(phase)) for phase, one in enumerate(grads)]
+    got = lax.ppermute(give, "seq", both)
+    near, far = pl.pallas_call(
+        assemble_kernel,
+        in_specs=[VMEM] * 2,
+        out_specs=[VMEM] * 2,
+        out_shape=[sds((2 * TOK, DH), BF16)] * 2,
+        compiler_params=params(),
+        name="assemble",
+    )(keep, got)
+    grads = [lax.ppermute(one, "seq", pair_pairs(which)) for which, one in ((1, far), (0, near))]
 
     lse, mean = pl.pallas_call(
         stats_kernel,
-        in_specs=[SMEM] + [VMEM] * 9,
+        in_specs=[SMEM] + [VMEM] * 7,
         out_specs=[VMEM] * 2,
         out_shape=[sds((1, QALL), F32), sds((DH, QALL), F32)],
         scratch_shapes=[
@@ -402,7 +439,7 @@
     cost = pl.CostEstimate(flops=1000, bytes_accessed=1000, transcendentals=0)
     time_part, text_part, dq, delta, grad_rows = pl.pallas_call(
         time_grads_kernel,
-        in_specs=[SMEM] + [VMEM] * 14,
+        in_specs=[SMEM] + [VMEM] * 10,
         out_specs=[VMEM] * 5,
         out_shape=[
             half_sum,
@@ -419,7 +456,7 @@
     time_back = lax.ppermute(time_part, "seq", time_pairs())
     core_part, own_part = pl.pallas_call(
         near_grads_kernel,
-        in_specs=[SMEM] + [VMEM] * 9,
+        in_specs=[SMEM] + [VMEM] * 7,
         out_specs=[VMEM] * 2,
         out_shape=[half_sum, sds((4, 3, TOK, DH), F32)],
         scratch_shapes=scratch + [pltpu.VMEM((DH, QALL), F32)],

time: 111 us -> 107 us (0.964)
  starting transfers between devices: 57.4 us -> 47.4 us
  waiting for transfers between devices: 23.8 us -> 28.4 us
  blocking collectives: 8.18 us -> 10.2 us
    ppermute x8, starting transfers between devices: 26.1 us -> 19.5 us  [the longest x4 18.1 us: per_device(): lax.ppermute(one, 'seq', pair_pairs(which))]
    ppermute x6, waiting for transfers between devices: 4.78 us -> 9.31 us  [per_device(): lax.ppermute(src, 'head', head_pairs(dx, 0))]
    ppermute x1, starting transfers between devices: 3.97 us -> 1.92 us  [per_device(): time_back = lax.ppermute(time_part, 'seq', time_pairs())]
    all_to_all x1, blocking collectives: 8.18 us -> 10.2 us  [per_device(): lax.all_to_all(text_part.reshape(8, TEXT // 8, 2 * DH), 'seq', 0, 0, axis...]
    pallas_call x5 -> x6, Pallas kernels: 15.3 us -> 15.3 us  [the longest x1 4.92 us: per_device(): pl.pallas_call(near_grads_kernel, in_specs=[SMEM] + [VMEM] * 7, out_specs...]
  transfers between devices with their start and end apart: 23 -> 23, of which waited for: 6 -> 8; matrix products, arithmetic and copies ran while one was open for 0% -> 0% of each run, Pallas kernels for 11% -> 11%
where the time goes in v3:
time: 107 us
  starting transfers between devices  47.4 us (44%)
  waiting for transfers between devices  28.4 us (27%)
  Pallas kernels  16.6 us (16%)
  blocking collectives  10.2 us (10%)
  local copies, waits for them, and re-layouts  2.98 us (3%)
    ppermute x4, starting transfers between devices, per_device(): lax.ppermute(one, 'seq', pair_pairs(which))  18.1 us
    ppermute x4, starting transfers between devices, per_device(): lax.ppermute(one, 'seq', back_pairs(phase))  12 us
    ppermute x4, waiting for transfers between devices, per_device(): lax.ppermute(one, 'seq', back_pairs(phase))  11.7 us
    all_to_all x1, blocking collectives, per_device(): lax.all_to_all(text_part.reshape(8, TEXT // 8, 2 * DH), 'seq', 0, 0, axis...  10.2 us
    ppermute x6, waiting for transfers between devices, per_device(): lax.ppermute(src, 'head', head_pairs(dx, 0))  9.31 us
    ppermute x6, starting transfers between devices, per_device(): lax.ppermute(src, 'head', head_pairs(dx, 0))  6.82 us
    ppermute x4, waiting for transfers between devices, per_device(): lax.ppermute(one, 'seq', pair_pairs(which))  6 us
    pallas_call x1, Pallas kernels, per_device(): pl.pallas_call(near_grads_kernel, in_specs=[SMEM] + [VMEM] * 7, out_specs...  4.92 us
  transfers between devices with their start and end apart: 23, of which 8 were waited for; matrix products, arithmetic and copies ran while one was open for 0% of the time, Pallas kernels for 11%

profile of v3, /device:TPU:33, one launch (start us, length us, event | category | flops | bytes accessed | tf_op | source)
XLA Modules:
  0.0 106.5 jit_solution(10918661417122996667)
XLA Ops:
  0.6 0.0 copy-start
  0.6 0.8 collective-permute-start
  1.4 0.1 collective-permute-start.1
  1.5 0.4 collective-permute-start.2
  1.9 1.2 %collective-permute-start.4 = (bf16[256,384]{1,0:T(8,128)(2,1)}, bf16[256,384]{1,0:T(8,128)(2,1)S(1)}, u32[]{:S(2)}, u32[]{:S(2)}) collective-permute-start(bf16[256,384]{1,0:T(8,128)(2,1)} %c0), channel_id=1, source_target_pairs={{0,1},{1,2},{2,3},{3,0},{4,5},{5,6},{6,7},{7,4},{8,9},{9,10},{10,1... | collective-permute-start | bytes 589832 | tf_op jit(solution)/shard_map/ppermute | solution.py:374
  3.1 1.5 %collective-permute-start.7 = (bf16[256,384]{1,0:T(8,128)(2,1)}, bf16[256,384]{1,0:T(8,128)(2,1)S(1)}, u32[]{:S(2)}, u32[]{:S(2)}) collective-permute-start(bf16[256,384]{1,0:T(8,128)(2,1)} %c0), channel_id=1, source_target_pairs={{0,3},{1,0},{2,1},{3,2},{4,7},{5,4},{6,5},{7,6},{8,11},{9,8},{10,9... | collective-permute-start | bytes 589832 | tf_op jit(solution)/shard_map/ppermute | solution.py:374
  4.6 0.0 collective-permute-done.q_next
  4.6 1.5 %collective-permute-start.6 = (bf16[256,384]{1,0:T(8,128)(2,1)}, bf16[256,384]{1,0:T(8,128)(2,1)S(1)}, u32[]{:S(2)}, u32[]{:S(2)}) collective-permute-start(bf16[256,384]{1,0:T(8,128)(2,1)} %c0), channel_id=1, source_target_pairs={{0,2},{1,3},{2,0},{3,1},{4,6},{5,7},{6,4},{7,5},{8,10},{9,11},{10,... | collective-permute-start | bytes 589832 | tf_op jit(solution)/shard_map/ppermute | solution.py:374
  6.1 0.0 collective-permute-done.1.k_next
  6.2 0.1 collective-permute-start.8
  6.3 0.0 collective-permute-done.2.v_next
  6.3 0.9 copy-done.3
  7.2 0.9 copy-done.4
  8.1 0.9 copy-done.5
  9.1 0.1 pack_heads.1
  9.2 0.6 collective-permute-done.4.c1
  9.8 9.0 %collective-permute-start.5 = (bf16[3,512,128]{2,1,0:T(8,128)(2,1)S(1)}, bf16[3,512,128]{2,1,0:T(8,128)(2,1)S(1)}, u32[]{:S(2)}, u32[]{:S(2)}) collective-permute-start(bf16[3,512,128]{2,1,0:T(8,128)(2,1)S(1)} %get-tuple-element.40), channel_id=1, source_target_pairs={{0,0},{8,32},{16,16},{32,8},{40,40},{48,24},{64,64},{72,96},{80,80... | collective-permute-start | bytes 1179656 | tf_op jit(solution)/shard_map/ppermute | solution.py:390
  18.8 1.3 %collective-permute-start.3 = (bf16[3,512,128]{2,1,0:T(8,128)(2,1)S(1)}, bf16[3,512,128]{2,1,0:T(8,128)(2,1)S(1)}, u32[]{:S(2)}, u32[]{:S(2)}) collective-permute-start(bf16[3,512,128]{2,1,0:T(8,128)(2,1)S(1)} %get-tuple-element.38), channel_id=1, source_target_pairs={{0,16},{16,0},{24,32},{32,24},{48,8},{56,40},{64,80},{80,64},{88,9... | collective-permute-start | bytes 1179656 | tf_op jit(solution)/shard_map/ppermute | solution.py:390
  20.1 0.0 collective-permute-done.8.c4
  20.1 1.5 %collective-permute-start.11 = (bf16[256,384]{1,0:T(8,128)(2,1)S(1)}, bf16[256,384]{1,0:T(8,128)(2,1)S(1)}, u32[]{:S(2)}, u32[]{:S(2)}) collective-permute-start(bf16[256,384]{1,0:T(8,128)(2,1)S(1)} %collective-permute-done.8.c4), channel_id=1, source_target_pairs={{0,3},{1,0},{2,1},{3,2},{4,7},{5,4},{6,5},{7,6},{8,11},{9,8},{10,9... | collective-permute-start | bytes 589832 | tf_op jit(solution)/shard_map/ppermute | solution.py:374
  21.6 0.0 collective-permute-done.7.c3
  21.6 0.7 collective-permute-start.10
  22.3 0.0 collective-permute-done.6.c2
  22.3 0.4 collective-permute-start.9
  22.7 5.0 %collective-permute-done.11.c7 = bf16[256,384]{1,0:T(8,128)(2,1)S(1)} collective-permute-done((bf16[256,384]{1,0:T(8,128)(2,1)S(1)}, bf16[256,384]{1,0:T(8,128)(2,1)S(1)}, u32[]{:S(2)}, u32[]{:S(2)}) %collective-permute-start.11) | collective-permute-done | bytes 196640 | tf_op jit(solution)/shard_map/ppermute | solution.py:374
  27.8 1.6 %collective-permute-done.10.c6 = bf16[256,384]{1,0:T(8,128)(2,1)S(1)} collective-permute-done((bf16[256,384]{1,0:T(8,128)(2,1)S(1)}, bf16[256,384]{1,0:T(8,128)(2,1)S(1)}, u32[]{:S(2)}, u32[]{:S(2)}) %collective-permute-start.10) | collective-permute-done | bytes 196640 | tf_op jit(solution)/shard_map/ppermute | solution.py:374
  29.4 2.1 %collective-permute-done.9.c5 = bf16[256,384]{1,0:T(8,128)(2,1)S(1)} collective-permute-done((bf16[256,384]{1,0:T(8,128)(2,1)S(1)}, bf16[256,384]{1,0:T(8,128)(2,1)S(1)}, u32[]{:S(2)}, u32[]{:S(2)}) %collective-permute-start.9) | collective-permute-done | bytes 196640 | tf_op jit(solution)/shard_map/ppermute | solution.py:374
  31.5 0.0 collective-permute-done.5.m_near
  31.5 6.0 %collective-permute-done.3.m_far = bf16[3,512,128]{2,1,0:T(8,128)(2,1)S(1)} collective-permute-done((bf16[3,512,128]{2,1,0:T(8,128)(2,1)S(1)}, bf16[3,512,128]{2,1,0:T(8,128)(2,1)S(1)}, u32[]{:S(2)}, u32[]{:S(2)}) %collective-permute-start.3) | collective-permute-done | bytes 393248 | tf_op jit(solution)/shard_map/ppermute | solution.py:390
  37.5 0.1 pad_maximum_fusion
  37.6 0.0 copy-start.8
  37.6 0.0 copy-start.1
  37.6 0.0 copy-start.2
  37.6 0.0 copy-start.7
  37.6 2.1 %collective-permute-start.16 = (bf16[2,2,512,128]{3,2,1,0:T(8,128)(2,1)S(1)}, bf16[2,2,512,128]{3,2,1,0:T(8,128)(2,1)S(1)}, u32[]{:S(2)}, u32[]{:S(2)}) collective-permute-start(bf16[2,2,512,128]{3,2,1,0:T(8,128)(2,1)S(1)} %pad_maximum_fusion), channel_id=1, source_target_pairs={{0,8},{8,0},{16,24},{24,16},{32,40},{40,32},{64,72},{72,64},{80,88... | collective-permute-start | bytes 1572872 | tf_op jit(solution)/shard_map/ppermute | solution.py:393
  39.7 3.0 %collective-permute-start.15 = (bf16[2,2,512,128]{3,2,1,0:T(8,128)(2,1)S(1)}, bf16[2,2,512,128]{3,2,1,0:T(8,128)(2,1)S(1)}, u32[]{:S(2)}, u32[]{:S(2)}) collective-permute-start(bf16[2,2,512,128]{3,2,1,0:T(8,128)(2,1)S(1)} %pad_maximum_fusion), channel_id=1, source_target_pairs={{8,64},{24,80},{40,96},{64,8},{72,128},{80,24},{88,144},{96,40},{1... | collective-permute-start | bytes 1572872 | tf_op jit(solution)/shard_map/ppermute | solution.py:394
  42.7 1.9 %project.1 = (bf16[2,256,128]{2,1,0:T(8,128)(2,1)S(1)}, bf16[2,256,128]{2,1,0:T(8,128)(2,1)S(1)}) custom-call(bf16[256,384]{1,0:T(8,128)(2,1)S(1)} %copy-done.6, bf16[256,384]{1,0:T(8,128)(2,1)S(1)} %collective-permute-done.4.c1, bf16[256,384]{1,0:T(8,128)(2,1)S(1)} %collective-permute-done.6.c2, bf16[256,384]{1,0:T(8,128)(2,1)S(1)} %collective-permute-done.7.c3, ...), custom_call_target="tpu_custom_call" | custom-call | tf_op jit(solution)/shard_map/project/pallas_call | solution.py:396
  44.6 0.1 collective-permute-start.12
  44.7 1.3 %collective-permute-done.12.got = bf16[2,256,128]{2,1,0:T(8,128)(2,1)S(1)} collective-permute-done((bf16[2,256,128]{2,1,0:T(8,128)(2,1)S(1)}, bf16[2,256,128]{2,1,0:T(8,128)(2,1)S(1)}, u32[]{:S(2)}, u32[]{:S(2)}) %collective-permute-start.12) | collective-permute-done | bytes 131104 | tf_op jit(solution)/shard_map/ppermute | solution.py:404
  46.0 1.3 %collective-permute-start.13 = (bf16[512,128]{1,0:T(8,128)(2,1)S(1)}, bf16[512,128]{1,0:T(8,128)(2,1)S(1)}, u32[]{:S(2)}, u32[]{:S(2)}) collective-permute-start(bf16[512,128]{1,0:T(8,128)(2,1)S(1)} %get-tuple-element.54), channel_id=1, source_target_pairs={{0,16},{16,0},{24,32},{32,24},{48,8},{56,40},{64,80},{80,64},{88,9... | collective-permute-start | bytes 393224 | tf_op jit(solution)/shard_map/ppermute | solution.py:413
  47.3 6.5 %collective-permute-start.14 = (bf16[512,128]{1,0:T(8,128)(2,1)S(1)}, bf16[512,128]{1,0:T(8,128)(2,1)S(1)}, u32[]{:S(2)}, u32[]{:S(2)}) collective-permute-start(bf16[512,128]{1,0:T(8,128)(2,1)S(1)} %get-tuple-element.55), channel_id=1, source_target_pairs={{0,0},{8,32},{16,16},{32,8},{40,40},{48,24},{64,64},{72,96},{80,80... | collective-permute-start | bytes 393224 | tf_op jit(solution)/shard_map/ppermute | solution.py:413
  53.9 0.1 copy.14.tb_ref
  54.0 0.0 collective-permute-done.16.core_kv
  54.0 0.0 collective-permute-done.15.time_kv
  54.1 4.7 %softmax_stats.1 = (f32[1,1024]{1,0:T(1,128)S(1)}, f32[128,1024]{1,0:T(8,128)S(1)}) custom-call(s32[3,3]{1,0:T(4,128)S(1)} %copy-done.7, bf16[3,512,128]{2,1,0:T(8,128)(2,1)S(1)} %collective-permute-done.3.m_far, bf16[3,512,128]{2,1,0:T(8,128)(2,1)S(1)} %collective-permute-done.5.m_near, bf16[2,2,512,128]{3,2,1,0:T(8,128)(2,1)S(1)} %collective-permute-done.16.core_kv, ...), custom_call_target="tpu_custom_call" | custom-call | flops 1000 | bytes 1000 | tf_op jit(solution)/shard_map/softmax_stats/pallas_call | solution.py:415
  58.8 0.0 collective-permute-done.13.g_far
  58.8 0.0 collective-permute-done.14.g_near
  58.8 3.6 %far_grads.1 = (bf16[4,2,256,128]{3,2,1,0:T(8,128)(2,1)S(1)}, bf16[256,256]{1,0:T(8,128)(2,1)S(1)}, f32[128,1024]{1,0:T(8,128)S(1)}, f32[1,1024]{1,0:T(1,128)S(1)}, bf16[1024,128]{1,0:T(8,128)(2,1)S(1)}) custom-call(s32[3,3]{1,0:T(4,128)S(1)} %copy-done.7, bf16[3,512,128]{2,1,0:T(8,128)(2,1)S(1)} %collective-permute-done.3.m_far, ...), custom_call_target="tpu_custom_call" | custom-call | flops 1000 | bytes 1000 | tf_op jit(solution)/shard_map/far_grads/pallas_call | solution.py:440
  62.4 1.9 %collective-permute-start.18 = (bf16[4,2,256,128]{3,2,1,0:T(8,128)(2,1)S(1)}, bf16[4,2,256,128]{3,2,1,0:T(8,128)(2,1)S(1)}, u32[]{:S(2)}, u32[]{:S(2)}) collective-permute-start(bf16[4,2,256,128]{3,2,1,0:T(8,128)(2,1)S(1)} %get-tuple-element.65), channel_id=1, source_target_pairs={{8,64},{24,80},{40,96},{64,8},{72,128},{80,24},{88,144},{96,40},{1... | collective-permute-start | bytes 1572872 | tf_op jit(solution)/shard_map/ppermute | solution.py:456
  64.4 4.9 %own_grads.1 = (bf16[4,2,256,128]{3,2,1,0:T(8,128)(2,1)S(1)}, f32[4,3,256,128]{3,2,1,0:T(8,128)S(1)}) custom-call(s32[3,3]{1,0:T(4,128)S(1)} %copy-done.7, bf16[3,512,128]{2,1,0:T(8,128)(2,1)S(1)} %collective-permute-done.3.m_far, bf16[3,512,128]{2,1,0:T(8,128)(2,1)S(1)} %collective-permute-done.5.m_near, ...), custom_call_target="tpu_custom_call" | custom-call | flops 1000 | bytes 1000 | tf_op jit(solution)/shard_map/own_grads/pallas_call | solution.py:457
  69.3 1.9 %collective-permute-start.17 = (bf16[4,2,256,128]{3,2,1,0:T(8,128)(2,1)S(1)}, bf16[4,2,256,128]{3,2,1,0:T(8,128)(2,1)S(1)}, u32[]{:S(2)}, u32[]{:S(2)}) collective-permute-start(bf16[4,2,256,128]{3,2,1,0:T(8,128)(2,1)S(1)} %get-tuple-element.64), channel_id=1, source_target_pairs={{0,8},{8,0},{16,24},{24,16},{32,40},{40,32},{64,72},{72,64},{80,88... | collective-permute-start | bytes 1572872 | tf_op jit(solution)/shard_map/ppermute | solution.py:468
  71.2 10.2 %all_to_all.5.text = bf16[8,32,256]{2,1,0:T(8,128)(2,1)S(1)} all-to-all(bf16[8,32,256]{2,1,0:T(8,128)(2,1)S(1)} %bitcast.6), channel_id=1, replica_groups={{0,8,64,72,128,136,192,200},{16,24,80,88,144,152,208,216},{32,40,96,104..., dimensions={0} | all-to-all | bytes 262144 | tf_op jit(solution)/shard_map/all_to_all | solution.py:470
  81.4 0.0 collective-permute-done.18.time
  81.4 0.0 collective-permute-done.17.core
  81.4 0.2 combine.1
  81.6 1.3 %collective-permute-start.19 = (bf16[784,128]{1,0:T(8,128)(2,1)S(1)}, bf16[784,128]{1,0:T(8,128)(2,1)S(1)}, u32[]{:S(2)}, u32[]{:S(2)}) collective-permute-start(bf16[784,128]{1,0:T(8,128)(2,1)S(1)} %get-tuple-element.67), channel_id=1, source_target_pairs={{16,0},{0,16},{32,24},{24,32},{8,48},{40,56},{80,64},{64,80},{96,8... | collective-permute-start | bytes 602120 | tf_op jit(solution)/shard_map/ppermute | solution.py:483
  82.9 6.9 %collective-permute-start.20 = (bf16[784,128]{1,0:T(8,128)(2,1)S(1)}, bf16[784,128]{1,0:T(8,128)(2,1)S(1)}, u32[]{:S(2)}, u32[]{:S(2)}) collective-permute-start(bf16[784,128]{1,0:T(8,128)(2,1)S(1)} %get-tuple-element.68), channel_id=1, source_target_pairs={{0,0},{32,8},{16,16},{8,32},{40,40},{24,48},{64,64},{96,72},{80,80... | collective-permute-start | bytes 602120 | tf_op jit(solution)/shard_map/ppermute | solution.py:483
  89.9 1.9 %collective-permute-start.21 = (bf16[784,128]{1,0:T(8,128)(2,1)S(1)}, bf16[784,128]{1,0:T(8,128)(2,1)S(1)}, u32[]{:S(2)}, u32[]{:S(2)}) collective-permute-start(bf16[784,128]{1,0:T(8,128)(2,1)S(1)} %get-tuple-element.69), channel_id=1, source_target_pairs={{16,8},{32,16},{0,24},{24,40},{40,48},{8,56},{80,72},{96,80},{64,8... | collective-permute-start | bytes 602120 | tf_op jit(solution)/shard_map/ppermute | solution.py:483
  91.8 1.9 %collective-permute-start.22 = (bf16[784,128]{1,0:T(8,128)(2,1)S(1)}, bf16[784,128]{1,0:T(8,128)(2,1)S(1)}, u32[]{:S(2)}, u32[]{:S(2)}) collective-permute-start(bf16[784,128]{1,0:T(8,128)(2,1)S(1)} %get-tuple-element.70), channel_id=1, source_target_pairs={{32,0},{0,8},{16,24},{40,32},{8,40},{24,56},{96,64},{64,72},{80,88... | collective-permute-start | bytes 602120 | tf_op jit(solution)/shard_map/ppermute | solution.py:483
  93.7 0.0 collective-permute-done.19.r0
  93.7 0.3 collective-permute-done.20.r1
  94.0 11.5 %collective-permute-done.21.r2 = bf16[784,128]{1,0:T(8,128)(2,1)S(1)} collective-permute-done((bf16[784,128]{1,0:T(8,128)(2,1)S(1)}, bf16[784,128]{1,0:T(8,128)(2,1)S(1)}, u32[]{:S(2)}, u32[]{:S(2)}) %collective-permute-start.21) | collective-permute-done | bytes 200736 | tf_op jit(solution)/shard_map/ppermute | solution.py:483
  105.5 0.0 collective-permute-done.22.r3
  105.5 1.1 unpack.1
  (13 shorter events, 0.1 us)
Async XLA Ops:
  0.6 42.0 %copy-start = (bf16[384,3072]{1,0:T(8,128)(2,1)S(1)}, bf16[384,3072]{1,0:T(8,128)(2,1)}, u32[]{:S(2)}) copy-start(bf16[384,3072]{1,0:T(8,128)(2,1)} %w_ref.1) | copy-start | bytes 7077892
  0.6 4.0 %collective-permute-start = (bf16[256,384]{1,0:T(8,128)(2,1)}, bf16[256,384]{1,0:T(8,128)(2,1)S(1)}, u32[]{:S(2)}, u32[]{:S(2)}) collective-permute-start(bf16[256,384]{1,0:T(8,128)(2,1)} %q_ref.1), channel_id=1, source_target_pairs={{0,8},{8,0},{16,24},{24,16},{32,40},{40,32},{48,56},{56,48},{64,72... | collective-permute-start | bytes 589832 | tf_op jit(solution)/shard_map/ppermute | solution.py:387
  1.4 4.7 %collective-permute-start.1 = (bf16[256,384]{1,0:T(8,128)(2,1)}, bf16[256,384]{1,0:T(8,128)(2,1)S(1)}, u32[]{:S(2)}, u32[]{:S(2)}) collective-permute-start(bf16[256,384]{1,0:T(8,128)(2,1)} %k_ref.1), channel_id=1, source_target_pairs={{0,8},{8,0},{16,24},{24,16},{32,40},{40,32},{48,56},{56,48},{64,72... | collective-permute-start | bytes 589832 | tf_op jit(solution)/shard_map/ppermute | solution.py:387
  1.5 4.8 %collective-permute-start.2 = (bf16[256,384]{1,0:T(8,128)(2,1)}, bf16[256,384]{1,0:T(8,128)(2,1)S(1)}, u32[]{:S(2)}, u32[]{:S(2)}) collective-permute-start(bf16[256,384]{1,0:T(8,128)(2,1)} %v_ref.1), channel_id=1, source_target_pairs={{0,8},{8,0},{16,24},{24,16},{32,40},{40,32},{48,56},{56,48},{64,72... | collective-permute-start | bytes 589832 | tf_op jit(solution)/shard_map/ppermute | solution.py:387
  1.9 7.9 %collective-permute-start.4 = (bf16[256,384]{1,0:T(8,128)(2,1)}, bf16[256,384]{1,0:T(8,128)(2,1)S(1)}, u32[]{:S(2)}, u32[]{:S(2)}) collective-permute-start(bf16[256,384]{1,0:T(8,128)(2,1)} %c0), channel_id=1, source_target_pairs={{0,1},{1,2},{2,3},{3,0},{4,5},{5,6},{6,7},{7,4},{8,9},{9,10},{10,1... | collective-permute-start | bytes 589832 | tf_op jit(solution)/shard_map/ppermute | solution.py:374
  3.1 18.5 %collective-permute-start.7 = (bf16[256,384]{1,0:T(8,128)(2,1)}, bf16[256,384]{1,0:T(8,128)(2,1)S(1)}, u32[]{:S(2)}, u32[]{:S(2)}) collective-permute-start(bf16[256,384]{1,0:T(8,128)(2,1)} %c0), channel_id=1, source_target_pairs={{0,3},{1,0},{2,1},{3,2},{4,7},{5,4},{6,5},{7,6},{8,11},{9,8},{10,9... | collective-permute-start | bytes 589832 | tf_op jit(solution)/shard_map/ppermute | solution.py:374
  4.6 17.7 %collective-permute-start.6 = (bf16[256,384]{1,0:T(8,128)(2,1)}, bf16[256,384]{1,0:T(8,128)(2,1)S(1)}, u32[]{:S(2)}, u32[]{:S(2)}) collective-permute-start(bf16[256,384]{1,0:T(8,128)(2,1)} %c0), channel_id=1, source_target_pairs={{0,2},{1,3},{2,0},{3,1},{4,6},{5,7},{6,4},{7,5},{8,10},{9,11},{10,... | collective-permute-start | bytes 589832 | tf_op jit(solution)/shard_map/ppermute | solution.py:374
  6.2 14.0 %collective-permute-start.8 = (bf16[256,384]{1,0:T(8,128)(2,1)}, bf16[256,384]{1,0:T(8,128)(2,1)S(1)}, u32[]{:S(2)}, u32[]{:S(2)}) collective-permute-start(bf16[256,384]{1,0:T(8,128)(2,1)} %c0), channel_id=1, source_target_pairs={{0,4},{1,5},{2,6},{3,7},{4,0},{5,1},{6,2},{7,3},{8,12},{9,13},{10,... | collective-permute-start | bytes 589832 | tf_op jit(solution)/shard_map/ppermute | solution.py:372
  6.3 0.9 copy-start.3
  7.2 0.9 copy-start.4
  8.1 0.9 copy-start.5
  9.1 33.6 %copy-start.6 = (bf16[256,384]{1,0:T(8,128)(2,1)S(1)}, bf16[256,384]{1,0:T(8,128)(2,1)}, u32[]{:S(2)}) copy-start(bf16[256,384]{1,0:T(8,128)(2,1)} %c0) | copy-start | bytes 589828
  9.8 21.7 %collective-permute-start.5 = (bf16[3,512,128]{2,1,0:T(8,128)(2,1)S(1)}, bf16[3,512,128]{2,1,0:T(8,128)(2,1)S(1)}, u32[]{:S(2)}, u32[]{:S(2)}) collective-permute-start(bf16[3,512,128]{2,1,0:T(8,128)(2,1)S(1)} %get-tuple-element.40), channel_id=1, source_target_pairs={{0,0},{8,32},{16,16},{32,8},{40,40},{48,24},{64,64},{72,96},{80,80... | collective-permute-start | bytes 1179656 | tf_op jit(solution)/shard_map/ppermute | solution.py:390
  18.8 18.6 %collective-permute-start.3 = (bf16[3,512,128]{2,1,0:T(8,128)(2,1)S(1)}, bf16[3,512,128]{2,1,0:T(8,128)(2,1)S(1)}, u32[]{:S(2)}, u32[]{:S(2)}) collective-permute-start(bf16[3,512,128]{2,1,0:T(8,128)(2,1)S(1)} %get-tuple-element.38), channel_id=1, source_target_pairs={{0,16},{16,0},{24,32},{32,24},{48,8},{56,40},{64,80},{80,64},{88,9... | collective-permute-start | bytes 1179656 | tf_op jit(solution)/shard_map/ppermute | solution.py:390
  20.1 7.6 %collective-permute-start.11 = (bf16[256,384]{1,0:T(8,128)(2,1)S(1)}, bf16[256,384]{1,0:T(8,128)(2,1)S(1)}, u32[]{:S(2)}, u32[]{:S(2)}) collective-permute-start(bf16[256,384]{1,0:T(8,128)(2,1)S(1)} %collective-permute-done.8.c4), channel_id=1, source_target_pairs={{0,3},{1,0},{2,1},{3,2},{4,7},{5,4},{6,5},{7,6},{8,11},{9,8},{10,9... | collective-permute-start | bytes 589832 | tf_op jit(solution)/shard_map/ppermute | solution.py:374
  21.6 7.8 %collective-permute-start.10 = (bf16[256,384]{1,0:T(8,128)(2,1)S(1)}, bf16[256,384]{1,0:T(8,128)(2,1)S(1)}, u32[]{:S(2)}, u32[]{:S(2)}) collective-permute-start(bf16[256,384]{1,0:T(8,128)(2,1)S(1)} %collective-permute-done.8.c4), channel_id=1, source_target_pairs={{0,2},{1,3},{2,0},{3,1},{4,6},{5,7},{6,4},{7,5},{8,10},{9,11},{10,... | collective-permute-start | bytes 589832 | tf_op jit(solution)/shard_map/ppermute | solution.py:374
  22.3 9.1 %collective-permute-start.9 = (bf16[256,384]{1,0:T(8,128)(2,1)S(1)}, bf16[256,384]{1,0:T(8,128)(2,1)S(1)}, u32[]{:S(2)}, u32[]{:S(2)}) collective-permute-start(bf16[256,384]{1,0:T(8,128)(2,1)S(1)} %collective-permute-done.8.c4), channel_id=1, source_target_pairs={{0,1},{1,2},{2,3},{3,0},{4,5},{5,6},{6,7},{7,4},{8,9},{9,10},{10,1... | collective-permute-start | bytes 589832 | tf_op jit(solution)/shard_map/ppermute | solution.py:374
  37.6 16.3 %copy-start.8 = (s32[256]{0:T(256)S(1)}, s32[256]{0:T(256)}, u32[]{:S(2)}) copy-start(s32[256]{0:T(256)} %param.17) | copy-start | bytes 3076
  37.6 16.5 %copy-start.1 = (bf16[256,384]{1,0:T(8,128)(2,1)S(1)}, bf16[256,384]{1,0:T(8,128)(2,1)}, u32[]{:S(2)}) copy-start(bf16[256,384]{1,0:T(8,128)(2,1)} %tk_ref.3) | copy-start | bytes 589828
  37.6 16.5 %copy-start.2 = (bf16[256,384]{1,0:T(8,128)(2,1)S(1)}, bf16[256,384]{1,0:T(8,128)(2,1)}, u32[]{:S(2)}) copy-start(bf16[256,384]{1,0:T(8,128)(2,1)} %tv_ref.3) | copy-start | bytes 589828
  37.6 16.5 %copy-start.7 = (s32[3,3]{1,0:T(4,128)S(1)}, s32[3,3]{1,0:T(4,128)}, u32[]{:S(2)}) copy-start(s32[3,3]{1,0:T(4,128)} %ext_ref.5) | copy-start | bytes 112
  37.6 16.4 %collective-permute-start.16 = (bf16[2,2,512,128]{3,2,1,0:T(8,128)(2,1)S(1)}, bf16[2,2,512,128]{3,2,1,0:T(8,128)(2,1)S(1)}, u32[]{:S(2)}, u32[]{:S(2)}) collective-permute-start(bf16[2,2,512,128]{3,2,1,0:T(8,128)(2,1)S(1)} %pad_maximum_fusion), channel_id=1, source_target_pairs={{0,8},{8,0},{16,24},{24,16},{32,40},{40,32},{64,72},{72,64},{80,88... | collective-permute-start | bytes 1572872 | tf_op jit(solution)/shard_map/ppermute | solution.py:393
  39.7 14.4 %collective-permute-start.15 = (bf16[2,2,512,128]{3,2,1,0:T(8,128)(2,1)S(1)}, bf16[2,2,512,128]{3,2,1,0:T(8,128)(2,1)S(1)}, u32[]{:S(2)}, u32[]{:S(2)}) collective-permute-start(bf16[2,2,512,128]{3,2,1,0:T(8,128)(2,1)S(1)} %pad_maximum_fusion), channel_id=1, source_target_pairs={{8,64},{24,80},{40,96},{64,8},{72,128},{80,24},{88,144},{96,40},{1... | collective-permute-start | bytes 1572872 | tf_op jit(solution)/shard_map/ppermute | solution.py:394
  44.6 1.4 %collective-permute-start.12 = (bf16[2,256,128]{2,1,0:T(8,128)(2,1)S(1)}, bf16[2,256,128]{2,1,0:T(8,128)(2,1)S(1)}, u32[]{:S(2)}, u32[]{:S(2)}) collective-permute-start(bf16[2,256,128]{2,1,0:T(8,128)(2,1)S(1)} %get-tuple-element.53), channel_id=1, source_target_pairs={{0,8},{8,0},{16,24},{24,16},{32,40},{40,32},{48,56},{56,48},{64,72... | collective-permute-start | bytes 393224 | tf_op jit(solution)/shard_map/ppermute | solution.py:404
  46.0 12.8 %collective-permute-start.13 = (bf16[512,128]{1,0:T(8,128)(2,1)S(1)}, bf16[512,128]{1,0:T(8,128)(2,1)S(1)}, u32[]{:S(2)}, u32[]{:S(2)}) collective-permute-start(bf16[512,128]{1,0:T(8,128)(2,1)S(1)} %get-tuple-element.54), channel_id=1, source_target_pairs={{0,16},{16,0},{24,32},{32,24},{48,8},{56,40},{64,80},{80,64},{88,9... | collective-permute-start | bytes 393224 | tf_op jit(solution)/shard_map/ppermute | solution.py:413
  47.3 11.5 %collective-permute-start.14 = (bf16[512,128]{1,0:T(8,128)(2,1)S(1)}, bf16[512,128]{1,0:T(8,128)(2,1)S(1)}, u32[]{:S(2)}, u32[]{:S(2)}) collective-permute-start(bf16[512,128]{1,0:T(8,128)(2,1)S(1)} %get-tuple-element.55), channel_id=1, source_target_pairs={{0,0},{8,32},{16,16},{32,8},{40,40},{48,24},{64,64},{72,96},{80,80... | collective-permute-start | bytes 393224 | tf_op jit(solution)/shard_map/ppermute | solution.py:413
  62.4 19.0 %collective-permute-start.18 = (bf16[4,2,256,128]{3,2,1,0:T(8,128)(2,1)S(1)}, bf16[4,2,256,128]{3,2,1,0:T(8,128)(2,1)S(1)}, u32[]{:S(2)}, u32[]{:S(2)}) collective-permute-start(bf16[4,2,256,128]{3,2,1,0:T(8,128)(2,1)S(1)} %get-tuple-element.65), channel_id=1, source_target_pairs={{8,64},{24,80},{40,96},{64,8},{72,128},{80,24},{88,144},{96,40},{1... | collective-permute-start | bytes 1572872 | tf_op jit(solution)/shard_map/ppermute | solution.py:456
  69.3 12.1 %collective-permute-start.17 = (bf16[4,2,256,128]{3,2,1,0:T(8,128)(2,1)S(1)}, bf16[4,2,256,128]{3,2,1,0:T(8,128)(2,1)S(1)}, u32[]{:S(2)}, u32[]{:S(2)}) collective-permute-start(bf16[4,2,256,128]{3,2,1,0:T(8,128)(2,1)S(1)} %get-tuple-element.64), channel_id=1, source_target_pairs={{0,8},{8,0},{16,24},{24,16},{32,40},{40,32},{64,72},{72,64},{80,88... | collective-permute-start | bytes 1572872 | tf_op jit(solution)/shard_map/ppermute | solution.py:468
  81.6 12.1 %collective-permute-start.19 = (bf16[784,128]{1,0:T(8,128)(2,1)S(1)}, bf16[784,128]{1,0:T(8,128)(2,1)S(1)}, u32[]{:S(2)}, u32[]{:S(2)}) collective-permute-start(bf16[784,128]{1,0:T(8,128)(2,1)S(1)} %get-tuple-element.67), channel_id=1, source_target_pairs={{16,0},{0,16},{32,24},{24,32},{8,48},{40,56},{80,64},{64,80},{96,8... | collective-permute-start | bytes 602120 | tf_op jit(solution)/shard_map/ppermute | solution.py:483
  82.9 11.0 %collective-permute-start.20 = (bf16[784,128]{1,0:T(8,128)(2,1)S(1)}, bf16[784,128]{1,0:T(8,128)(2,1)S(1)}, u32[]{:S(2)}, u32[]{:S(2)}) collective-permute-start(bf16[784,128]{1,0:T(8,128)(2,1)S(1)} %get-tuple-element.68), channel_id=1, source_target_pairs={{0,0},{32,8},{16,16},{8,32},{40,40},{24,48},{64,64},{96,72},{80,80... | collective-permute-start | bytes 602120 | tf_op jit(solution)/shard_map/ppermute | solution.py:483
  89.9 15.6 %collective-permute-start.21 = (bf16[784,128]{1,0:T(8,128)(2,1)S(1)}, bf16[784,128]{1,0:T(8,128)(2,1)S(1)}, u32[]{:S(2)}, u32[]{:S(2)}) collective-permute-start(bf16[784,128]{1,0:T(8,128)(2,1)S(1)} %get-tuple-element.69), channel_id=1, source_target_pairs={{16,8},{32,16},{0,24},{24,40},{40,48},{8,56},{80,72},{96,80},{64,8... | collective-permute-start | bytes 602120 | tf_op jit(solution)/shard_map/ppermute | solution.py:483
  91.8 13.7 %collective-permute-start.22 = (bf16[784,128]{1,0:T(8,128)(2,1)S(1)}, bf16[784,128]{1,0:T(8,128)(2,1)S(1)}, u32[]{:S(2)}, u32[]{:S(2)}) collective-permute-start(bf16[784,128]{1,0:T(8,128)(2,1)S(1)} %get-tuple-element.70), channel_id=1, source_target_pairs={{32,0},{0,8},{16,24},{40,32},{8,40},{24,56},{96,64},{64,72},{80,88... | collective-permute-start | bytes 602120 | tf_op jit(solution)/shard_map/ppermute | solution.py:483

commit v4 on v3

--- a/solution.py
+++ b/solution.py
@@ -134,24 +134,32 @@
             out[which, theirs, :] = other[:, columns]
 
 
-def project_kernel(c0, c1, c2, c3, c4, c5, c6, c7, w_ref, keep, give):
-    chunks = (c0, c1, c2, c3, c4, c5, c6, c7)
+def project_terms(chunks, dz, w_ref, which_out):
     g = lax.axis_index("head")
+    gz, gx = lax.div(g, 4), lax.rem(g, 4)
     h = home_height()
-    gz, gx = lax.div(g, 4), lax.rem(g, 4)
-    width = c0.shape[1]
+    width = chunks[0].shape[1]
+    far, other = which_out & 1, which_out >> 1
+    head = jnp.minimum(pair_head(far, h ^ other), 2)
+    rows = pl.ds(pl.multiple_of(head * DH, DH), DH)
+    total = None
+    for dx, chunk in enumerate(chunks):
+        src = lax.rem(gz + dz, 2) * 4 + lax.rem(gx - dx + 4, 4)
+        columns = pl.ds(pl.multiple_of(src * width, width), width)
+        term = dot_nt(chunk[...], w_ref[rows, columns])
+        total = term if total is None else total + term
+    return total
+
+
+def project_first_kernel(c0, c1, c2, c3, w_ref, acc):
     for which_out in range(4):
-        far, other = which_out & 1, which_out >> 1
-        head = jnp.minimum(pair_head(far, h ^ other), 2)
-        rows = pl.ds(pl.multiple_of(head * DH, DH), DH)
-        total = None
-        for which, chunk in enumerate(chunks):
-            dz, dx = which // 4, which % 4
-            src = lax.rem(gz + dz, 2) * 4 + lax.rem(gx - dx + 4, 4)
-            columns = pl.ds(pl.multiple_of(src * width, width), width)
-            term = dot_nt(chunk[...], w_ref[rows, columns])
-            total = term if total is None else total + term
-        (give if other else keep)[far] = total.astype(BF16)
+        acc[which_out] = project_terms((c0, c1, c2, c3), 0, w_ref, which_out)
+
+
+def project_kernel(c4, c5, c6, c7, w_ref, acc, keep, give):
+    for which_out in range(4):
+        total = acc[which_out] + project_terms((c4, c5, c6, c7), 1, w_ref, which_out)
+        (give if which_out >> 1 else keep)[which_out & 1] = total.astype(BF16)
 
 
 def assemble_kernel(keep, got, near, far):
@@ -386,22 +394,29 @@
         name="pack_heads",
     )(*inputs, *(lax.ppermute(one, "seq", both) for one in inputs))
     packed = list(packed)
-    packed[1], chunks[1] = lax.optimization_barrier((packed[1], chunks[1]))
     msgs = [lax.ppermute(one, "seq", pair_pairs(which)) for which, one in zip((1, 0), packed)]
-    msgs, chunks = lax.optimization_barrier((msgs, chunks))
+    partial = pl.pallas_call(
+        project_first_kernel,
+        in_specs=[VMEM] * 5,
+        out_specs=VMEM,
+        out_shape=sds((4, TOK, DH), F32),
+        compiler_params=params(),
+        name="project_first",
+    )(*chunks[:4], out_weight)
+    keep, give = pl.pallas_call(
+        project_kernel,
+        in_specs=[VMEM] * 6,
+        out_specs=[VMEM] * 2,
+        out_shape=[sds((2, TOK, DH), BF16)] * 2,
+        compiler_params=params(),
+        name="project",
+    )(*chunks[4:], out_weight, partial)
+    got = lax.ppermute(give, "seq", both)
+    msgs, got = lax.optimization_barrier((msgs, got))
     kv = jnp.stack([one[1:] for one in msgs])
     core_kv = lax.ppermute(kv, "seq", core_pairs())
     time_kv = lax.ppermute(kv, "seq", time_pairs())
 
-    keep, give = pl.pallas_call(
-        project_kernel,
-        in_specs=[VMEM] * 9,
-        out_specs=[VMEM] * 2,
-        out_shape=[sds((2, TOK, DH), BF16)] * 2,
-        compiler_params=params(),
-        name="project",
-    )(*chunks, out_weight)
-    got = lax.ppermute(give, "seq", both)
     near, far = pl.pallas_call(
         assemble_kernel,
         in_specs=[VMEM] * 2,

time: 107 us -> 103 us (0.963)
  waiting for transfers between devices: 28.4 us -> 19.6 us
  local copies, waits for them, and re-layouts: 2.98 us -> 5.57 us
  starting transfers between devices: 47.4 us -> 49.4 us
    ppermute x6, waiting for transfers between devices: 9.31 us -> 3.37 us  [per_device(): lax.ppermute(src, 'head', head_pairs(dx, 0))]
    unnamed x18 -> x20, local copies, waits for them, and re-layouts: 2.81 us -> 5.4 us
    ppermute x4, waiting for transfers between devices: 6 us -> 3.57 us  [per_device(): lax.ppermute(one, 'seq', pair_pairs(which))]
    ppermute x4, starting transfers between devices: 18.1 us -> 20.1 us  [per_device(): lax.ppermute(one, 'seq', pair_pairs(which))]
  transfers between devices with their start and end apart: 23 -> 23, of which waited for: 8 -> 6; matrix products, arithmetic and copies ran while one was open for 0% -> 0% of each run, Pallas kernels for 11% -> 12%
where the time goes in v4:
time: 103 us; the launch traced here: 102 us
  starting transfers between devices  49.4 us (48%)
  waiting for transfers between devices  19.6 us (19%)
  Pallas kernels  16.7 us (16%)
  blocking collectives  10.2 us (10%)
  local copies, waits for them, and re-layouts  5.57 us (5%)
    ppermute x4, starting transfers between devices, per_device(): lax.ppermute(one, 'seq', pair_pairs(which))  20.1 us
    ppermute x4, starting transfers between devices, per_device(): lax.ppermute(one, 'seq', back_pairs(phase))  11.5 us
    ppermute x4, waiting for transfers between devices, per_device(): lax.ppermute(one, 'seq', back_pairs(phase))  11.3 us
    all_to_all x1, blocking collectives, per_device(): lax.all_to_all(text_part.reshape(8, TEXT // 8, 2 * DH), 'seq', 0, 0, axis...  10.2 us
    ppermute x6, starting transfers between devices, per_device(): lax.ppermute(src, 'head', head_pairs(dx, 0))  7.05 us
    unnamed x20, local copies, waits for them, and re-layouts  5.4 us
    pallas_call x1, Pallas kernels, per_device(): pl.pallas_call(near_grads_kernel, in_specs=[SMEM] + [VMEM] * 7, out_specs...  4.92 us
    pallas_call x1, Pallas kernels, per_device(): pl.pallas_call(stats_kernel, in_specs=[SMEM] + [VMEM] * 7, out_specs=[VME...  4.72 us
  transfers between devices with their start and end apart: 23, of which 6 were waited for; matrix products, arithmetic and copies ran while one was open for 0% of the time, Pallas kernels for 12%

profile of v4, /device:TPU:33, one launch (start us, length us, event | category | flops | bytes accessed | tf_op | source)
XLA Modules:
  0.0 102.4 jit_solution(15067090817708322582)
XLA Ops:
  0.6 0.8 collective-permute-start
  1.4 0.1 collective-permute-start.1
  1.5 0.4 collective-permute-start.2
  1.9 2.8 %collective-permute-start.10 = (bf16[256,384]{1,0:T(8,128)(2,1)}, bf16[256,384]{1,0:T(8,128)(2,1)S(1)}, u32[]{:S(2)}, u32[]{:S(2)}) collective-permute-start(bf16[256,384]{1,0:T(8,128)(2,1)} %c0.1), channel_id=1, source_target_pairs={{0,2},{1,3},{2,0},{3,1},{4,6},{5,7},{6,4},{7,5},{8,10},{9,11},{10,... | collective-permute-start | bytes 589832 | tf_op jit(solution)/shard_map/ppermute | solution.py:382
  4.7 0.0 collective-permute-start.5
  4.7 0.0 collective-permute-done.q_next
  4.7 0.3 collective-permute-start.9
  5.0 0.0 collective-permute-done.1.k_next
  5.0 2.4 %collective-permute-start.11 = (bf16[256,384]{1,0:T(8,128)(2,1)}, bf16[256,384]{1,0:T(8,128)(2,1)S(1)}, u32[]{:S(2)}, u32[]{:S(2)}) collective-permute-start(bf16[256,384]{1,0:T(8,128)(2,1)} %c0.1), channel_id=1, source_target_pairs={{0,3},{1,0},{2,1},{3,2},{4,7},{5,4},{6,5},{7,6},{8,11},{9,8},{10,9... | collective-permute-start | bytes 589832 | tf_op jit(solution)/shard_map/ppermute | solution.py:382
  7.4 0.0 collective-permute-done.2.v_next
  7.4 0.9 copy-done.5
  8.3 0.9 copy-done.6
  9.2 0.9 copy-done.7
  10.1 0.1 pack_heads.1
  10.3 1.3 %collective-permute-start.3 = (bf16[3,512,128]{2,1,0:T(8,128)(2,1)S(1)}, bf16[3,512,128]{2,1,0:T(8,128)(2,1)S(1)}, u32[]{:S(2)}, u32[]{:S(2)}) collective-permute-start(bf16[3,512,128]{2,1,0:T(8,128)(2,1)S(1)} %get-tuple-element.29), channel_id=1, source_target_pairs={{0,16},{16,0},{24,32},{32,24},{48,8},{56,40},{64,80},{80,64},{88,9... | collective-permute-start | bytes 1179656 | tf_op jit(solution)/shard_map/ppermute | solution.py:397
  11.6 0.0 collective-permute-done.10.c2
  11.6 10.4 %collective-permute-start.4 = (bf16[3,512,128]{2,1,0:T(8,128)(2,1)S(1)}, bf16[3,512,128]{2,1,0:T(8,128)(2,1)S(1)}, u32[]{:S(2)}, u32[]{:S(2)}) collective-permute-start(bf16[3,512,128]{2,1,0:T(8,128)(2,1)S(1)} %get-tuple-element.30), channel_id=1, source_target_pairs={{0,0},{8,32},{16,16},{32,8},{40,40},{48,24},{64,64},{72,96},{80,80... | collective-permute-start | bytes 1179656 | tf_op jit(solution)/shard_map/ppermute | solution.py:397
  22.0 0.0 collective-permute-done.5.c4
  22.0 0.1 collective-permute-start.8
  22.1 0.0 collective-permute-done.9.c1
  22.1 0.9 collective-permute-start.7
  22.9 0.0 collective-permute-done.11.c3
  22.9 0.7 collective-permute-start.6
  23.6 1.7 %copy-done = bf16[384,3072]{1,0:T(8,128)(2,1)S(1)} copy-done((bf16[384,3072]{1,0:T(8,128)(2,1)S(1)}, bf16[384,3072]{1,0:T(8,128)(2,1)}, u32[]{:S(2)}) %copy-start) | copy-done | bytes 2359320
  25.3 0.9 copy-done.4
  26.2 1.0 project_first.1.acc
  27.2 0.0 copy-start.9
  27.2 0.0 copy-start.2
  27.2 0.0 copy-start.3
  27.2 0.0 copy-start.8
  27.3 0.0 collective-permute-done.8.c7
  27.3 1.4 %collective-permute-done.7.c6 = bf16[256,384]{1,0:T(8,128)(2,1)S(1)} collective-permute-done((bf16[256,384]{1,0:T(8,128)(2,1)S(1)}, bf16[256,384]{1,0:T(8,128)(2,1)S(1)}, u32[]{:S(2)}, u32[]{:S(2)}) %collective-permute-start.7) | collective-permute-done | bytes 196640 | tf_op jit(solution)/shard_map/ppermute | solution.py:382
  28.6 2.0 %collective-permute-done.6.c5 = bf16[256,384]{1,0:T(8,128)(2,1)S(1)} collective-permute-done((bf16[256,384]{1,0:T(8,128)(2,1)S(1)}, bf16[256,384]{1,0:T(8,128)(2,1)S(1)}, u32[]{:S(2)}, u32[]{:S(2)}) %collective-permute-start.6) | collective-permute-done | bytes 196640 | tf_op jit(solution)/shard_map/ppermute | solution.py:382
  30.6 1.0 project.1
  31.6 0.1 collective-permute-start.12
  31.7 1.3 %collective-permute-done.12.got = bf16[2,256,128]{2,1,0:T(8,128)(2,1)S(1)} collective-permute-done((bf16[2,256,128]{2,1,0:T(8,128)(2,1)S(1)}, bf16[2,256,128]{2,1,0:T(8,128)(2,1)S(1)}, u32[]{:S(2)}, u32[]{:S(2)}) %collective-permute-start.12) | collective-permute-done | bytes 131104 | tf_op jit(solution)/shard_map/ppermute | solution.py:414
  33.1 3.6 %collective-permute-done.3.m_far = bf16[3,512,128]{2,1,0:T(8,128)(2,1)S(1)} collective-permute-done((bf16[3,512,128]{2,1,0:T(8,128)(2,1)S(1)}, bf16[3,512,128]{2,1,0:T(8,128)(2,1)S(1)}, u32[]{:S(2)}, u32[]{:S(2)}) %collective-permute-start.3) | collective-permute-done | bytes 393248 | tf_op jit(solution)/shard_map/ppermute | solution.py:397
  36.6 0.0 collective-permute-done.4.m_near
  36.7 0.1 pad_maximum_fusion
  36.7 1.9 %collective-permute-start.16 = (bf16[2,2,512,128]{3,2,1,0:T(8,128)(2,1)S(1)}, bf16[2,2,512,128]{3,2,1,0:T(8,128)(2,1)S(1)}, u32[]{:S(2)}, u32[]{:S(2)}) collective-permute-start(bf16[2,2,512,128]{3,2,1,0:T(8,128)(2,1)S(1)} %pad_maximum_fusion), channel_id=1, source_target_pairs={{0,8},{8,0},{16,24},{24,16},{32,40},{40,32},{64,72},{72,64},{80,88... | collective-permute-start | bytes 1572872 | tf_op jit(solution)/shard_map/ppermute | solution.py:417
  38.7 3.6 %collective-permute-start.15 = (bf16[2,2,512,128]{3,2,1,0:T(8,128)(2,1)S(1)}, bf16[2,2,512,128]{3,2,1,0:T(8,128)(2,1)S(1)}, u32[]{:S(2)}, u32[]{:S(2)}) collective-permute-start(bf16[2,2,512,128]{3,2,1,0:T(8,128)(2,1)S(1)} %pad_maximum_fusion), channel_id=1, source_target_pairs={{8,64},{24,80},{40,96},{64,8},{72,128},{80,24},{88,144},{96,40},{1... | collective-permute-start | bytes 1572872 | tf_op jit(solution)/shard_map/ppermute | solution.py:418
  42.3 1.3 %collective-permute-start.13 = (bf16[512,128]{1,0:T(8,128)(2,1)S(1)}, bf16[512,128]{1,0:T(8,128)(2,1)S(1)}, u32[]{:S(2)}, u32[]{:S(2)}) collective-permute-start(bf16[512,128]{1,0:T(8,128)(2,1)S(1)} %get-tuple-element.36), channel_id=1, source_target_pairs={{0,16},{16,0},{24,32},{32,24},{48,8},{56,40},{64,80},{80,64},{88,9... | collective-permute-start | bytes 393224 | tf_op jit(solution)/shard_map/ppermute | solution.py:428
  43.6 7.2 %collective-permute-start.14 = (bf16[512,128]{1,0:T(8,128)(2,1)S(1)}, bf16[512,128]{1,0:T(8,128)(2,1)S(1)}, u32[]{:S(2)}, u32[]{:S(2)}) collective-permute-start(bf16[512,128]{1,0:T(8,128)(2,1)S(1)} %get-tuple-element.37), channel_id=1, source_target_pairs={{0,0},{8,32},{16,16},{32,8},{40,40},{48,24},{64,64},{72,96},{80,80... | collective-permute-start | bytes 393224 | tf_op jit(solution)/shard_map/ppermute | solution.py:428
  50.8 0.1 copy.14.tb_ref
  51.0 0.0 collective-permute-done.16.core_kv
  51.0 0.0 collective-permute-done.15.time_kv
  51.0 4.7 %softmax_stats.1 = (f32[1,1024]{1,0:T(1,128)S(1)}, f32[128,1024]{1,0:T(8,128)S(1)}) custom-call(s32[3,3]{1,0:T(4,128)S(1)} %copy-done.8, bf16[3,512,128]{2,1,0:T(8,128)(2,1)S(1)} %collective-permute-done.3.m_far, bf16[3,512,128]{2,1,0:T(8,128)(2,1)S(1)} %collective-permute-done.4.m_near, bf16[2,2,512,128]{3,2,1,0:T(8,128)(2,1)S(1)} %collective-permute-done.16.core_kv, ...), custom_call_target="tpu_custom_call" | custom-call | flops 1000 | bytes 1000 | tf_op jit(solution)/shard_map/softmax_stats/pallas_call | solution.py:430
  55.7 0.0 collective-permute-done.13.g_far
  55.7 0.0 collective-permute-done.14.g_near
  55.8 3.6 %far_grads.1 = (bf16[4,2,256,128]{3,2,1,0:T(8,128)(2,1)S(1)}, bf16[256,256]{1,0:T(8,128)(2,1)S(1)}, f32[128,1024]{1,0:T(8,128)S(1)}, f32[1,1024]{1,0:T(1,128)S(1)}, bf16[1024,128]{1,0:T(8,128)(2,1)S(1)}) custom-call(s32[3,3]{1,0:T(4,128)S(1)} %copy-done.8, bf16[3,512,128]{2,1,0:T(8,128)(2,1)S(1)} %collective-permute-done.3.m_far, ...), custom_call_target="tpu_custom_call" | custom-call | flops 1000 | bytes 1000 | tf_op jit(solution)/shard_map/far_grads/pallas_call | solution.py:455
  59.4 1.9 %collective-permute-start.18 = (bf16[4,2,256,128]{3,2,1,0:T(8,128)(2,1)S(1)}, bf16[4,2,256,128]{3,2,1,0:T(8,128)(2,1)S(1)}, u32[]{:S(2)}, u32[]{:S(2)}) collective-permute-start(bf16[4,2,256,128]{3,2,1,0:T(8,128)(2,1)S(1)} %get-tuple-element.47), channel_id=1, source_target_pairs={{8,64},{24,80},{40,96},{64,8},{72,128},{80,24},{88,144},{96,40},{1... | collective-permute-start | bytes 1572872 | tf_op jit(solution)/shard_map/ppermute | solution.py:471
  61.3 4.9 %own_grads.1 = (bf16[4,2,256,128]{3,2,1,0:T(8,128)(2,1)S(1)}, f32[4,3,256,128]{3,2,1,0:T(8,128)S(1)}) custom-call(s32[3,3]{1,0:T(4,128)S(1)} %copy-done.8, bf16[3,512,128]{2,1,0:T(8,128)(2,1)S(1)} %collective-permute-done.3.m_far, bf16[3,512,128]{2,1,0:T(8,128)(2,1)S(1)} %collective-permute-done.4.m_near, ...), custom_call_target="tpu_custom_call" | custom-call | flops 1000 | bytes 1000 | tf_op jit(solution)/shard_map/own_grads/pallas_call | solution.py:472
  66.2 1.9 %collective-permute-start.17 = (bf16[4,2,256,128]{3,2,1,0:T(8,128)(2,1)S(1)}, bf16[4,2,256,128]{3,2,1,0:T(8,128)(2,1)S(1)}, u32[]{:S(2)}, u32[]{:S(2)}) collective-permute-start(bf16[4,2,256,128]{3,2,1,0:T(8,128)(2,1)S(1)} %get-tuple-element.46), channel_id=1, source_target_pairs={{0,8},{8,0},{16,24},{24,16},{32,40},{40,32},{64,72},{72,64},{80,88... | collective-permute-start | bytes 1572872 | tf_op jit(solution)/shard_map/ppermute | solution.py:483
  68.2 10.2 %all_to_all.5.text = bf16[8,32,256]{2,1,0:T(8,128)(2,1)S(1)} all-to-all(bf16[8,32,256]{2,1,0:T(8,128)(2,1)S(1)} %bitcast.6), channel_id=1, replica_groups={{0,8,64,72,128,136,192,200},{16,24,80,88,144,152,208,216},{32,40,96,104..., dimensions={0} | all-to-all | bytes 262144 | tf_op jit(solution)/shard_map/all_to_all | solution.py:485
  78.4 0.0 collective-permute-done.17.core
  78.4 0.2 combine.1
  78.6 1.3 %collective-permute-start.19 = (bf16[784,128]{1,0:T(8,128)(2,1)S(1)}, bf16[784,128]{1,0:T(8,128)(2,1)S(1)}, u32[]{:S(2)}, u32[]{:S(2)}) collective-permute-start(bf16[784,128]{1,0:T(8,128)(2,1)S(1)} %get-tuple-element.49), channel_id=1, source_target_pairs={{16,0},{0,16},{32,24},{24,32},{8,48},{40,56},{80,64},{64,80},{96,8... | collective-permute-start | bytes 602120 | tf_op jit(solution)/shard_map/ppermute | solution.py:498
  79.9 6.3 %collective-permute-start.20 = (bf16[784,128]{1,0:T(8,128)(2,1)S(1)}, bf16[784,128]{1,0:T(8,128)(2,1)S(1)}, u32[]{:S(2)}, u32[]{:S(2)}) collective-permute-start(bf16[784,128]{1,0:T(8,128)(2,1)S(1)} %get-tuple-element.50), channel_id=1, source_target_pairs={{0,0},{32,8},{16,16},{8,32},{40,40},{24,48},{64,64},{96,72},{80,80... | collective-permute-start | bytes 602120 | tf_op jit(solution)/shard_map/ppermute | solution.py:498
  86.2 1.9 %collective-permute-start.21 = (bf16[784,128]{1,0:T(8,128)(2,1)S(1)}, bf16[784,128]{1,0:T(8,128)(2,1)S(1)}, u32[]{:S(2)}, u32[]{:S(2)}) collective-permute-start(bf16[784,128]{1,0:T(8,128)(2,1)S(1)} %get-tuple-element.51), channel_id=1, source_target_pairs={{16,8},{32,16},{0,24},{24,40},{40,48},{8,56},{80,72},{96,80},{64,8... | collective-permute-start | bytes 602120 | tf_op jit(solution)/shard_map/ppermute | solution.py:498
  88.2 1.9 %collective-permute-start.22 = (bf16[784,128]{1,0:T(8,128)(2,1)S(1)}, bf16[784,128]{1,0:T(8,128)(2,1)S(1)}, u32[]{:S(2)}, u32[]{:S(2)}) collective-permute-start(bf16[784,128]{1,0:T(8,128)(2,1)S(1)} %get-tuple-element.52), channel_id=1, source_target_pairs={{32,0},{0,8},{16,24},{40,32},{8,40},{24,56},{96,64},{64,72},{80,88... | collective-permute-start | bytes 602120 | tf_op jit(solution)/shard_map/ppermute | solution.py:498
  90.1 0.0 collective-permute-done.19.r0
  90.1 1.0 collective-permute-done.20.r1
  91.1 10.3 %collective-permute-done.21.r2 = bf16[784,128]{1,0:T(8,128)(2,1)S(1)} collective-permute-done((bf16[784,128]{1,0:T(8,128)(2,1)S(1)}, bf16[784,128]{1,0:T(8,128)(2,1)S(1)}, u32[]{:S(2)}, u32[]{:S(2)}) %collective-permute-start.21) | collective-permute-done | bytes 200736 | tf_op jit(solution)/shard_map/ppermute | solution.py:498
  101.4 1.1 %unpack.1 = (bf16[256,384]{1,0:T(8,128)(2,1)}, f32[256,384]{1,0:T(8,128)}, f32[256,384]{1,0:T(8,128)}, f32[8,384]{1,0:T(8,128)}, f32[8,384]{1,0:T(8,128)}) custom-call(bf16[784,128]{1,0:T(8,128)(2,1)S(1)} %collective-permute-done.19.r0, bf16[784,128]{1,0:T(8,128)(2,1)S(1)} %collective-permute-done.20.r1, bf16[784,128]{1,0:T(8,128)(2,1)S(1)} %collective-permute-done.21.r2, ...), custom_call_target="tpu_custom_call" | custom-call | tf_op jit(solution)/shard_map/unpack/pallas_call | solution.py:501
  (16 shorter events, 0.1 us)
Async XLA Ops:
  0.6 4.0 %collective-permute-start = (bf16[256,384]{1,0:T(8,128)(2,1)}, bf16[256,384]{1,0:T(8,128)(2,1)S(1)}, u32[]{:S(2)}, u32[]{:S(2)}) collective-permute-start(bf16[256,384]{1,0:T(8,128)(2,1)} %q_ref.1), channel_id=1, source_target_pairs={{0,8},{8,0},{16,24},{24,16},{32,40},{40,32},{48,56},{56,48},{64,72... | collective-permute-start | bytes 589832 | tf_op jit(solution)/shard_map/ppermute | solution.py:395
  1.4 3.6 %collective-permute-start.1 = (bf16[256,384]{1,0:T(8,128)(2,1)}, bf16[256,384]{1,0:T(8,128)(2,1)S(1)}, u32[]{:S(2)}, u32[]{:S(2)}) collective-permute-start(bf16[256,384]{1,0:T(8,128)(2,1)} %k_ref.1), channel_id=1, source_target_pairs={{0,8},{8,0},{16,24},{24,16},{32,40},{40,32},{48,56},{56,48},{64,72... | collective-permute-start | bytes 589832 | tf_op jit(solution)/shard_map/ppermute | solution.py:395
  1.5 5.9 %collective-permute-start.2 = (bf16[256,384]{1,0:T(8,128)(2,1)}, bf16[256,384]{1,0:T(8,128)(2,1)S(1)}, u32[]{:S(2)}, u32[]{:S(2)}) collective-permute-start(bf16[256,384]{1,0:T(8,128)(2,1)} %v_ref.1), channel_id=1, source_target_pairs={{0,8},{8,0},{16,24},{24,16},{32,40},{40,32},{48,56},{56,48},{64,72... | collective-permute-start | bytes 589832 | tf_op jit(solution)/shard_map/ppermute | solution.py:395
  1.9 9.7 %collective-permute-start.10 = (bf16[256,384]{1,0:T(8,128)(2,1)}, bf16[256,384]{1,0:T(8,128)(2,1)S(1)}, u32[]{:S(2)}, u32[]{:S(2)}) collective-permute-start(bf16[256,384]{1,0:T(8,128)(2,1)} %c0.1), channel_id=1, source_target_pairs={{0,2},{1,3},{2,0},{3,1},{4,6},{5,7},{6,4},{7,5},{8,10},{9,11},{10,... | collective-permute-start | bytes 589832 | tf_op jit(solution)/shard_map/ppermute | solution.py:382
  4.7 17.3 %collective-permute-start.5 = (bf16[256,384]{1,0:T(8,128)(2,1)}, bf16[256,384]{1,0:T(8,128)(2,1)S(1)}, u32[]{:S(2)}, u32[]{:S(2)}) collective-permute-start(bf16[256,384]{1,0:T(8,128)(2,1)} %c0.1), channel_id=1, source_target_pairs={{0,4},{1,5},{2,6},{3,7},{4,0},{5,1},{6,2},{7,3},{8,12},{9,13},{10,... | collective-permute-start | bytes 589832 | tf_op jit(solution)/shard_map/ppermute | solution.py:380
  4.7 17.4 %collective-permute-start.9 = (bf16[256,384]{1,0:T(8,128)(2,1)}, bf16[256,384]{1,0:T(8,128)(2,1)S(1)}, u32[]{:S(2)}, u32[]{:S(2)}) collective-permute-start(bf16[256,384]{1,0:T(8,128)(2,1)} %c0.1), channel_id=1, source_target_pairs={{0,1},{1,2},{2,3},{3,0},{4,5},{5,6},{6,7},{7,4},{8,9},{9,10},{10,1... | collective-permute-start | bytes 589832 | tf_op jit(solution)/shard_map/ppermute | solution.py:382
  5.0 18.0 %collective-permute-start.11 = (bf16[256,384]{1,0:T(8,128)(2,1)}, bf16[256,384]{1,0:T(8,128)(2,1)S(1)}, u32[]{:S(2)}, u32[]{:S(2)}) collective-permute-start(bf16[256,384]{1,0:T(8,128)(2,1)} %c0.1), channel_id=1, source_target_pairs={{0,3},{1,0},{2,1},{3,2},{4,7},{5,4},{6,5},{7,6},{8,11},{9,8},{10,9... | collective-permute-start | bytes 589832 | tf_op jit(solution)/shard_map/ppermute | solution.py:382
  7.4 0.9 copy-start.5
  8.3 0.9 copy-start.6
  9.2 0.9 copy-start.7
  10.3 26.4 %collective-permute-start.3 = (bf16[3,512,128]{2,1,0:T(8,128)(2,1)S(1)}, bf16[3,512,128]{2,1,0:T(8,128)(2,1)S(1)}, u32[]{:S(2)}, u32[]{:S(2)}) collective-permute-start(bf16[3,512,128]{2,1,0:T(8,128)(2,1)S(1)} %get-tuple-element.29), channel_id=1, source_target_pairs={{0,16},{16,0},{24,32},{32,24},{48,8},{56,40},{64,80},{80,64},{88,9... | collective-permute-start | bytes 1179656 | tf_op jit(solution)/shard_map/ppermute | solution.py:397
  11.6 25.0 %collective-permute-start.4 = (bf16[3,512,128]{2,1,0:T(8,128)(2,1)S(1)}, bf16[3,512,128]{2,1,0:T(8,128)(2,1)S(1)}, u32[]{:S(2)}, u32[]{:S(2)}) collective-permute-start(bf16[3,512,128]{2,1,0:T(8,128)(2,1)S(1)} %get-tuple-element.30), channel_id=1, source_target_pairs={{0,0},{8,32},{16,16},{32,8},{40,40},{48,24},{64,64},{72,96},{80,80... | collective-permute-start | bytes 1179656 | tf_op jit(solution)/shard_map/ppermute | solution.py:397
  22.0 5.3 %collective-permute-start.8 = (bf16[256,384]{1,0:T(8,128)(2,1)S(1)}, bf16[256,384]{1,0:T(8,128)(2,1)S(1)}, u32[]{:S(2)}, u32[]{:S(2)}) collective-permute-start(bf16[256,384]{1,0:T(8,128)(2,1)S(1)} %collective-permute-done.5.c4), channel_id=1, source_target_pairs={{0,3},{1,0},{2,1},{3,2},{4,7},{5,4},{6,5},{7,6},{8,11},{9,8},{10,9... | collective-permute-start | bytes 589832 | tf_op jit(solution)/shard_map/ppermute | solution.py:382
  22.1 6.6 %collective-permute-start.7 = (bf16[256,384]{1,0:T(8,128)(2,1)S(1)}, bf16[256,384]{1,0:T(8,128)(2,1)S(1)}, u32[]{:S(2)}, u32[]{:S(2)}) collective-permute-start(bf16[256,384]{1,0:T(8,128)(2,1)S(1)} %collective-permute-done.5.c4), channel_id=1, source_target_pairs={{0,2},{1,3},{2,0},{3,1},{4,6},{5,7},{6,4},{7,5},{8,10},{9,11},{10,... | collective-permute-start | bytes 589832 | tf_op jit(solution)/shard_map/ppermute | solution.py:382
  22.9 7.7 %collective-permute-start.6 = (bf16[256,384]{1,0:T(8,128)(2,1)S(1)}, bf16[256,384]{1,0:T(8,128)(2,1)S(1)}, u32[]{:S(2)}, u32[]{:S(2)}) collective-permute-start(bf16[256,384]{1,0:T(8,128)(2,1)S(1)} %collective-permute-done.5.c4), channel_id=1, source_target_pairs={{0,1},{1,2},{2,3},{3,0},{4,5},{5,6},{6,7},{7,4},{8,9},{9,10},{10,1... | collective-permute-start | bytes 589832 | tf_op jit(solution)/shard_map/ppermute | solution.py:382
  23.6 1.7 %copy-start = (bf16[384,3072]{1,0:T(8,128)(2,1)S(1)}, bf16[384,3072]{1,0:T(8,128)(2,1)}, u32[]{:S(2)}) copy-start(bf16[384,3072]{1,0:T(8,128)(2,1)} %w_ref.3) | copy-start | bytes 7077892
  25.3 0.9 copy-start.4
  26.2 4.4 %copy-start.1 = (bf16[384,3072]{1,0:T(8,128)(2,1)S(1)}, bf16[384,3072]{1,0:T(8,128)(2,1)}, u32[]{:S(2)}) copy-start(bf16[384,3072]{1,0:T(8,128)(2,1)} %w_ref.3) | copy-start | bytes 7077892
  27.2 23.6 %copy-start.9 = (s32[256]{0:T(256)S(1)}, s32[256]{0:T(256)}, u32[]{:S(2)}) copy-start(s32[256]{0:T(256)} %param.17) | copy-start | bytes 3076
  27.2 23.8 %copy-start.2 = (bf16[256,384]{1,0:T(8,128)(2,1)S(1)}, bf16[256,384]{1,0:T(8,128)(2,1)}, u32[]{:S(2)}) copy-start(bf16[256,384]{1,0:T(8,128)(2,1)} %tk_ref.3) | copy-start | bytes 589828
  27.2 23.8 %copy-start.3 = (bf16[256,384]{1,0:T(8,128)(2,1)S(1)}, bf16[256,384]{1,0:T(8,128)(2,1)}, u32[]{:S(2)}) copy-start(bf16[256,384]{1,0:T(8,128)(2,1)} %tv_ref.3) | copy-start | bytes 589828
  27.2 23.8 %copy-start.8 = (s32[3,3]{1,0:T(4,128)S(1)}, s32[3,3]{1,0:T(4,128)}, u32[]{:S(2)}) copy-start(s32[3,3]{1,0:T(4,128)} %ext_ref.5) | copy-start | bytes 112
  31.6 1.4 %collective-permute-start.12 = (bf16[2,256,128]{2,1,0:T(8,128)(2,1)S(1)}, bf16[2,256,128]{2,1,0:T(8,128)(2,1)S(1)}, u32[]{:S(2)}, u32[]{:S(2)}) collective-permute-start(bf16[2,256,128]{2,1,0:T(8,128)(2,1)S(1)} %get-tuple-element.31), channel_id=1, source_target_pairs={{0,8},{8,0},{16,24},{24,16},{32,40},{40,32},{48,56},{56,48},{64,72... | collective-permute-start | bytes 393224 | tf_op jit(solution)/shard_map/ppermute | solution.py:414
  36.7 14.2 %collective-permute-start.16 = (bf16[2,2,512,128]{3,2,1,0:T(8,128)(2,1)S(1)}, bf16[2,2,512,128]{3,2,1,0:T(8,128)(2,1)S(1)}, u32[]{:S(2)}, u32[]{:S(2)}) collective-permute-start(bf16[2,2,512,128]{3,2,1,0:T(8,128)(2,1)S(1)} %pad_maximum_fusion), channel_id=1, source_target_pairs={{0,8},{8,0},{16,24},{24,16},{32,40},{40,32},{64,72},{72,64},{80,88... | collective-permute-start | bytes 1572872 | tf_op jit(solution)/shard_map/ppermute | solution.py:417
  38.7 12.3 %collective-permute-start.15 = (bf16[2,2,512,128]{3,2,1,0:T(8,128)(2,1)S(1)}, bf16[2,2,512,128]{3,2,1,0:T(8,128)(2,1)S(1)}, u32[]{:S(2)}, u32[]{:S(2)}) collective-permute-start(bf16[2,2,512,128]{3,2,1,0:T(8,128)(2,1)S(1)} %pad_maximum_fusion), channel_id=1, source_target_pairs={{8,64},{24,80},{40,96},{64,8},{72,128},{80,24},{88,144},{96,40},{1... | collective-permute-start | bytes 1572872 | tf_op jit(solution)/shard_map/ppermute | solution.py:418
  42.3 13.4 %collective-permute-start.13 = (bf16[512,128]{1,0:T(8,128)(2,1)S(1)}, bf16[512,128]{1,0:T(8,128)(2,1)S(1)}, u32[]{:S(2)}, u32[]{:S(2)}) collective-permute-start(bf16[512,128]{1,0:T(8,128)(2,1)S(1)} %get-tuple-element.36), channel_id=1, source_target_pairs={{0,16},{16,0},{24,32},{32,24},{48,8},{56,40},{64,80},{80,64},{88,9... | collective-permute-start | bytes 393224 | tf_op jit(solution)/shard_map/ppermute | solution.py:428
  43.6 12.2 %collective-permute-start.14 = (bf16[512,128]{1,0:T(8,128)(2,1)S(1)}, bf16[512,128]{1,0:T(8,128)(2,1)S(1)}, u32[]{:S(2)}, u32[]{:S(2)}) collective-permute-start(bf16[512,128]{1,0:T(8,128)(2,1)S(1)} %get-tuple-element.37), channel_id=1, source_target_pairs={{0,0},{8,32},{16,16},{32,8},{40,40},{48,24},{64,64},{72,96},{80,80... | collective-permute-start | bytes 393224 | tf_op jit(solution)/shard_map/ppermute | solution.py:428
  59.4 19.0 %collective-permute-start.18 = (bf16[4,2,256,128]{3,2,1,0:T(8,128)(2,1)S(1)}, bf16[4,2,256,128]{3,2,1,0:T(8,128)(2,1)S(1)}, u32[]{:S(2)}, u32[]{:S(2)}) collective-permute-start(bf16[4,2,256,128]{3,2,1,0:T(8,128)(2,1)S(1)} %get-tuple-element.47), channel_id=1, source_target_pairs={{8,64},{24,80},{40,96},{64,8},{72,128},{80,24},{88,144},{96,40},{1... | collective-permute-start | bytes 1572872 | tf_op jit(solution)/shard_map/ppermute | solution.py:471
  66.2 12.1 %collective-permute-start.17 = (bf16[4,2,256,128]{3,2,1,0:T(8,128)(2,1)S(1)}, bf16[4,2,256,128]{3,2,1,0:T(8,128)(2,1)S(1)}, u32[]{:S(2)}, u32[]{:S(2)}) collective-permute-start(bf16[4,2,256,128]{3,2,1,0:T(8,128)(2,1)S(1)} %get-tuple-element.46), channel_id=1, source_target_pairs={{0,8},{8,0},{16,24},{24,16},{32,40},{40,32},{64,72},{72,64},{80,88... | collective-permute-start | bytes 1572872 | tf_op jit(solution)/shard_map/ppermute | solution.py:483
  78.6 11.5 %collective-permute-start.19 = (bf16[784,128]{1,0:T(8,128)(2,1)S(1)}, bf16[784,128]{1,0:T(8,128)(2,1)S(1)}, u32[]{:S(2)}, u32[]{:S(2)}) collective-permute-start(bf16[784,128]{1,0:T(8,128)(2,1)S(1)} %get-tuple-element.49), channel_id=1, source_target_pairs={{16,0},{0,16},{32,24},{24,32},{8,48},{40,56},{80,64},{64,80},{96,8... | collective-permute-start | bytes 602120 | tf_op jit(solution)/shard_map/ppermute | solution.py:498
  79.9 11.2 %collective-permute-start.20 = (bf16[784,128]{1,0:T(8,128)(2,1)S(1)}, bf16[784,128]{1,0:T(8,128)(2,1)S(1)}, u32[]{:S(2)}, u32[]{:S(2)}) collective-permute-start(bf16[784,128]{1,0:T(8,128)(2,1)S(1)} %get-tuple-element.50), channel_id=1, source_target_pairs={{0,0},{32,8},{16,16},{8,32},{40,40},{24,48},{64,64},{96,72},{80,80... | collective-permute-start | bytes 602120 | tf_op jit(solution)/shard_map/ppermute | solution.py:498
  86.2 15.1 %collective-permute-start.21 = (bf16[784,128]{1,0:T(8,128)(2,1)S(1)}, bf16[784,128]{1,0:T(8,128)(2,1)S(1)}, u32[]{:S(2)}, u32[]{:S(2)}) collective-permute-start(bf16[784,128]{1,0:T(8,128)(2,1)S(1)} %get-tuple-element.51), channel_id=1, source_target_pairs={{16,8},{32,16},{0,24},{24,40},{40,48},{8,56},{80,72},{96,80},{64,8... | collective-permute-start | bytes 602120 | tf_op jit(solution)/shard_map/ppermute | solution.py:498
  88.2 13.2 %collective-permute-start.22 = (bf16[784,128]{1,0:T(8,128)(2,1)S(1)}, bf16[784,128]{1,0:T(8,128)(2,1)S(1)}, u32[]{:S(2)}, u32[]{:S(2)}) collective-permute-start(bf16[784,128]{1,0:T(8,128)(2,1)S(1)} %get-tuple-element.52), channel_id=1, source_target_pairs={{32,0},{0,8},{16,24},{40,32},{8,40},{24,56},{96,64},{64,72},{80,88... | collective-permute-start | bytes 602120 | tf_op jit(solution)/shard_map/ppermute | solution.py:498

commit v5 on v4

--- a/solution.py
+++ b/solution.py
@@ -121,15 +121,19 @@
     return (lax.axis_index("seq") >> 1) & 3
 
 
-def pack_kernel(q_ref, k_ref, v_ref, q_next, k_next, v_next, far_out, near_out):
+def pack_kernel(q_ref, k_ref, v_ref, q_next, k_next, v_next, far_out, near_out, q_own, k_own, v_own, sem):
+    pairs = ((q_ref, q_own), (k_ref, k_own), (v_ref, v_own))
+    copies = [pltpu.make_async_copy(src, dst, sem.at[i]) for i, (src, dst) in enumerate(pairs)]
+    start_all(copies)
     h = home_height()
     core = h & 1
     mine = pl.ds(pl.multiple_of(core * TOK, TOK), TOK)
     theirs = pl.ds(pl.multiple_of((1 - core) * TOK, TOK), TOK)
+    wait_all(copies)
     for far, out in ((1, far_out), (0, near_out)):
         head = jnp.minimum(pair_head(far, h), 2)
         columns = pl.ds(pl.multiple_of(head * DH, DH), DH)
-        for which, (own, other) in enumerate(((q_ref, q_next), (k_ref, k_next), (v_ref, v_next))):
+        for which, (own, other) in enumerate(((q_own, q_next), (k_own, k_next), (v_own, v_next))):
             out[which, mine, :] = own[:, columns]
             out[which, theirs, :] = other[:, columns]
 
@@ -387,10 +391,11 @@
     inputs = (queries, keys, values)
     packed = pl.pallas_call(
         pack_kernel,
-        in_specs=[VMEM] * 6,
+        in_specs=[ANY] * 3 + [VMEM] * 3,
         out_specs=[VMEM] * 2,
         out_shape=[sds((3, 2 * TOK, DH), BF16)] * 2,
-        compiler_params=params(),
+        scratch_shapes=[pltpu.VMEM((TOK, 3 * DH), BF16)] * 3 + [pltpu.SemaphoreType.DMA((3,))],
+        compiler_params=params(60),
         name="pack_heads",
     )(*inputs, *(lax.ppermute(one, "seq", both) for one in inputs))
     packed = list(packed)

time: 103 us -> 104 us (level)
  Pallas kernels: 16.7 us -> 19.8 us
  local copies, waits for them, and re-layouts: 5.57 us -> 3.46 us
    pallas_call x1, Pallas kernels: 0.14 us -> 3.27 us  [per_device(): pl.pallas_call(pack_kernel, in_specs=[ANY] * 3 + [VMEM] * 3, out_specs=[V...]
    unnamed x20, local copies, waits for them, and re-layouts: 5.4 us -> 3.3 us
  transfers between devices with their start and end apart: 23 -> 23, of which waited for: 6 -> 7; matrix products, arithmetic and copies ran while one was open for 0% -> 0% of each run, Pallas kernels for 12% -> 14%
where the time goes in v5:
time: 104 us
  starting transfers between devices  49.4 us (48%)
  waiting for transfers between devices  19.8 us (19%)
  Pallas kernels  19.8 us (19%)
  blocking collectives  10.2 us (10%)
  local copies, waits for them, and re-layouts  3.46 us (3%)
    ppermute x4, starting transfers between devices, per_device(): lax.ppermute(one, 'seq', pair_pairs(which))  20.1 us
    ppermute x4, starting transfers between devices, per_device(): lax.ppermute(one, 'seq', back_pairs(phase))  11.5 us
    ppermute x4, waiting for transfers between devices, per_device(): lax.ppermute(one, 'seq', back_pairs(phase))  11.3 us
    all_to_all x1, blocking collectives, per_device(): lax.all_to_all(text_part.reshape(8, TEXT // 8, 2 * DH), 'seq', 0, 0, axis...  10.2 us
    ppermute x6, starting transfers between devices, per_device(): lax.ppermute(src, 'head', head_pairs(dx, 0))  7.14 us
    pallas_call x1, Pallas kernels, per_device(): pl.pallas_call(near_grads_kernel, in_specs=[SMEM] + [VMEM] * 7, out_specs...  4.92 us
    pallas_call x1, Pallas kernels, per_device(): pl.pallas_call(stats_kernel, in_specs=[SMEM] + [VMEM] * 7, out_specs=[VME...  4.72 us
    ppermute x6, waiting for transfers between devices, per_device(): lax.ppermute(src, 'head', head_pairs(dx, 0))  4.39 us
  transfers between devices with their start and end apart: 23, of which 7 were waited for; matrix products, arithmetic and copies ran while one was open for 0% of the time, Pallas kernels for 14%

profile of v5, /device:TPU:33, one launch (start us, length us, event | category | flops | bytes accessed | tf_op | source)
XLA Modules:
  0.0 103.7 jit_solution(1305616011547645597)
XLA Ops:
  0.6 0.8 collective-permute-start
  1.4 0.1 collective-permute-start.1
  1.5 0.4 collective-permute-start.2
  1.9 2.8 %collective-permute-start.10 = (bf16[256,384]{1,0:T(8,128)(2,1)}, bf16[256,384]{1,0:T(8,128)(2,1)S(1)}, u32[]{:S(2)}, u32[]{:S(2)}) collective-permute-start(bf16[256,384]{1,0:T(8,128)(2,1)} %c0.1), channel_id=1, source_target_pairs={{0,2},{1,3},{2,0},{3,1},{4,6},{5,7},{6,4},{7,5},{8,10},{9,11},{10,... | collective-permute-start | bytes 589832 | tf_op jit(solution)/shard_map/ppermute | solution.py:386
  4.7 0.0 collective-permute-start.5
  4.7 0.0 collective-permute-done.q_next
  4.7 0.4 collective-permute-start.9
  5.1 0.0 collective-permute-done.1.k_next
  5.1 2.4 %collective-permute-start.11 = (bf16[256,384]{1,0:T(8,128)(2,1)}, bf16[256,384]{1,0:T(8,128)(2,1)S(1)}, u32[]{:S(2)}, u32[]{:S(2)}) collective-permute-start(bf16[256,384]{1,0:T(8,128)(2,1)} %c0.1), channel_id=1, source_target_pairs={{0,3},{1,0},{2,1},{3,2},{4,7},{5,4},{6,5},{7,6},{8,11},{9,8},{10,9... | collective-permute-start | bytes 589832 | tf_op jit(solution)/shard_map/ppermute | solution.py:386
  7.4 0.0 collective-permute-done.2.v_next
  7.5 0.7 copy-done.8
  8.1 3.3 %pack_heads.1 = (bf16[3,512,128]{2,1,0:T(8,128)(2,1)}, bf16[3,512,128]{2,1,0:T(8,128)(2,1)}) custom-call(bf16[256,384]{1,0:T(8,128)(2,1)} %q_ref.1, bf16[256,384]{1,0:T(8,128)(2,1)} %k_ref.1, bf16[256,384]{1,0:T(8,128)(2,1)} %v_ref.1, bf16[256,384]{1,0:T(8,128)(2,1)} %copy-done.6, bf16[256,384]{1,0:T(8,128)(2,1)} %copy-done.7, bf16[256,384]{1,0:T(8,128)(2,1)} %copy-done.8), custom_call_target="tpu_custom_call" | custom-call | tf_op jit(solution)/shard_map/pack_heads/pallas_call | solution.py:392
  11.4 1.3 %collective-permute-start.3 = (bf16[3,512,128]{2,1,0:T(8,128)(2,1)}, bf16[3,512,128]{2,1,0:T(8,128)(2,1)S(1)}, u32[]{:S(2)}, u32[]{:S(2)}) collective-permute-start(bf16[3,512,128]{2,1,0:T(8,128)(2,1)} %get-tuple-element.29), channel_id=1, source_target_pairs={{0,16},{16,0},{24,32},{32,24},{48,8},{56,40},{64,80},{80,64},{88,9... | collective-permute-start | bytes 1179656 | tf_op jit(solution)/shard_map/ppermute | solution.py:402
  12.7 0.0 collective-permute-done.10.c2
  12.7 10.3 %collective-permute-start.4 = (bf16[3,512,128]{2,1,0:T(8,128)(2,1)}, bf16[3,512,128]{2,1,0:T(8,128)(2,1)S(1)}, u32[]{:S(2)}, u32[]{:S(2)}) collective-permute-start(bf16[3,512,128]{2,1,0:T(8,128)(2,1)} %get-tuple-element.30), channel_id=1, source_target_pairs={{0,0},{8,32},{16,16},{32,8},{40,40},{48,24},{64,64},{72,96},{80,80... | collective-permute-start | bytes 1179656 | tf_op jit(solution)/shard_map/ppermute | solution.py:402
  23.0 0.0 collective-permute-done.5.c4
  23.0 0.5 collective-permute-start.8
  23.5 0.0 collective-permute-done.9.c1
  23.5 0.5 collective-permute-start.7
  24.0 0.0 collective-permute-done.11.c3
  24.0 0.7 collective-permute-start.6
  24.6 1.7 %copy-done = bf16[384,3072]{1,0:T(8,128)(2,1)S(1)} copy-done((bf16[384,3072]{1,0:T(8,128)(2,1)S(1)}, bf16[384,3072]{1,0:T(8,128)(2,1)}, u32[]{:S(2)}) %copy-start) | copy-done | bytes 2359320
  26.3 0.9 copy-done.4
  27.2 1.0 project_first.1.acc
  28.2 0.0 copy-start.9
  28.3 0.0 copy-start.2
  28.3 0.0 copy-start.3
  28.3 0.0 copy-start.5
  28.3 0.4 collective-permute-done.8.c7
  28.7 1.9 %collective-permute-done.7.c6 = bf16[256,384]{1,0:T(8,128)(2,1)S(1)} collective-permute-done((bf16[256,384]{1,0:T(8,128)(2,1)S(1)}, bf16[256,384]{1,0:T(8,128)(2,1)S(1)}, u32[]{:S(2)}, u32[]{:S(2)}) %collective-permute-start.7) | collective-permute-done | bytes 196640 | tf_op jit(solution)/shard_map/ppermute | solution.py:386
  30.6 2.0 %collective-permute-done.6.c5 = bf16[256,384]{1,0:T(8,128)(2,1)S(1)} collective-permute-done((bf16[256,384]{1,0:T(8,128)(2,1)S(1)}, bf16[256,384]{1,0:T(8,128)(2,1)S(1)}, u32[]{:S(2)}, u32[]{:S(2)}) %collective-permute-start.6) | collective-permute-done | bytes 196640 | tf_op jit(solution)/shard_map/ppermute | solution.py:386
  32.7 1.0 project.1
  33.7 0.1 collective-permute-start.12
  33.8 1.3 %collective-permute-done.12.got = bf16[2,256,128]{2,1,0:T(8,128)(2,1)S(1)} collective-permute-done((bf16[2,256,128]{2,1,0:T(8,128)(2,1)S(1)}, bf16[2,256,128]{2,1,0:T(8,128)(2,1)S(1)}, u32[]{:S(2)}, u32[]{:S(2)}) %collective-permute-start.12) | collective-permute-done | bytes 131104 | tf_op jit(solution)/shard_map/ppermute | solution.py:419
  35.1 2.8 %collective-permute-done.3.m_far = bf16[3,512,128]{2,1,0:T(8,128)(2,1)S(1)} collective-permute-done((bf16[3,512,128]{2,1,0:T(8,128)(2,1)}, bf16[3,512,128]{2,1,0:T(8,128)(2,1)S(1)}, u32[]{:S(2)}, u32[]{:S(2)}) %collective-permute-start.3) | collective-permute-done | bytes 393248 | tf_op jit(solution)/shard_map/ppermute | solution.py:402
  37.9 0.0 collective-permute-done.4.m_near
  37.9 0.1 pad_maximum_fusion
  38.0 1.9 %collective-permute-start.16 = (bf16[2,2,512,128]{3,2,1,0:T(8,128)(2,1)S(1)}, bf16[2,2,512,128]{3,2,1,0:T(8,128)(2,1)S(1)}, u32[]{:S(2)}, u32[]{:S(2)}) collective-permute-start(bf16[2,2,512,128]{3,2,1,0:T(8,128)(2,1)S(1)} %pad_maximum_fusion), channel_id=1, source_target_pairs={{0,8},{8,0},{16,24},{24,16},{32,40},{40,32},{64,72},{72,64},{80,88... | collective-permute-start | bytes 1572872 | tf_op jit(solution)/shard_map/ppermute | solution.py:422
  39.9 3.6 %collective-permute-start.15 = (bf16[2,2,512,128]{3,2,1,0:T(8,128)(2,1)S(1)}, bf16[2,2,512,128]{3,2,1,0:T(8,128)(2,1)S(1)}, u32[]{:S(2)}, u32[]{:S(2)}) collective-permute-start(bf16[2,2,512,128]{3,2,1,0:T(8,128)(2,1)S(1)} %pad_maximum_fusion), channel_id=1, source_target_pairs={{8,64},{24,80},{40,96},{64,8},{72,128},{80,24},{88,144},{96,40},{1... | collective-permute-start | bytes 1572872 | tf_op jit(solution)/shard_map/ppermute | solution.py:423
  43.5 1.3 %collective-permute-start.13 = (bf16[512,128]{1,0:T(8,128)(2,1)S(1)}, bf16[512,128]{1,0:T(8,128)(2,1)S(1)}, u32[]{:S(2)}, u32[]{:S(2)}) collective-permute-start(bf16[512,128]{1,0:T(8,128)(2,1)S(1)} %get-tuple-element.36), channel_id=1, source_target_pairs={{0,16},{16,0},{24,32},{32,24},{48,8},{56,40},{64,80},{80,64},{88,9... | collective-permute-start | bytes 393224 | tf_op jit(solution)/shard_map/ppermute | solution.py:433
  44.8 7.2 %collective-permute-start.14 = (bf16[512,128]{1,0:T(8,128)(2,1)S(1)}, bf16[512,128]{1,0:T(8,128)(2,1)S(1)}, u32[]{:S(2)}, u32[]{:S(2)}) collective-permute-start(bf16[512,128]{1,0:T(8,128)(2,1)S(1)} %get-tuple-element.37), channel_id=1, source_target_pairs={{0,0},{8,32},{16,16},{32,8},{40,40},{48,24},{64,64},{72,96},{80,80... | collective-permute-start | bytes 393224 | tf_op jit(solution)/shard_map/ppermute | solution.py:433
  52.1 0.1 copy.14.tb_ref
  52.2 0.0 collective-permute-done.16.core_kv
  52.2 0.0 collective-permute-done.15.time_kv
  52.3 4.7 %softmax_stats.1 = (f32[1,1024]{1,0:T(1,128)S(1)}, f32[128,1024]{1,0:T(8,128)S(1)}) custom-call(s32[3,3]{1,0:T(4,128)S(1)} %copy-done.5, bf16[3,512,128]{2,1,0:T(8,128)(2,1)S(1)} %collective-permute-done.3.m_far, bf16[3,512,128]{2,1,0:T(8,128)(2,1)S(1)} %collective-permute-done.4.m_near, bf16[2,2,512,128]{3,2,1,0:T(8,128)(2,1)S(1)} %collective-permute-done.16.core_kv, ...), custom_call_target="tpu_custom_call" | custom-call | flops 1000 | bytes 1000 | tf_op jit(solution)/shard_map/softmax_stats/pallas_call | solution.py:435
  57.0 0.0 collective-permute-done.13.g_far
  57.0 0.0 collective-permute-done.14.g_near
  57.0 3.6 %far_grads.1 = (bf16[4,2,256,128]{3,2,1,0:T(8,128)(2,1)S(1)}, bf16[256,256]{1,0:T(8,128)(2,1)S(1)}, f32[128,1024]{1,0:T(8,128)S(1)}, f32[1,1024]{1,0:T(1,128)S(1)}, bf16[1024,128]{1,0:T(8,128)(2,1)S(1)}) custom-call(s32[3,3]{1,0:T(4,128)S(1)} %copy-done.5, bf16[3,512,128]{2,1,0:T(8,128)(2,1)S(1)} %collective-permute-done.3.m_far, ...), custom_call_target="tpu_custom_call" | custom-call | flops 1000 | bytes 1000 | tf_op jit(solution)/shard_map/far_grads/pallas_call | solution.py:460
  60.6 1.9 %collective-permute-start.18 = (bf16[4,2,256,128]{3,2,1,0:T(8,128)(2,1)S(1)}, bf16[4,2,256,128]{3,2,1,0:T(8,128)(2,1)S(1)}, u32[]{:S(2)}, u32[]{:S(2)}) collective-permute-start(bf16[4,2,256,128]{3,2,1,0:T(8,128)(2,1)S(1)} %get-tuple-element.47), channel_id=1, source_target_pairs={{8,64},{24,80},{40,96},{64,8},{72,128},{80,24},{88,144},{96,40},{1... | collective-permute-start | bytes 1572872 | tf_op jit(solution)/shard_map/ppermute | solution.py:476
  62.6 4.9 %own_grads.1 = (bf16[4,2,256,128]{3,2,1,0:T(8,128)(2,1)S(1)}, f32[4,3,256,128]{3,2,1,0:T(8,128)S(1)}) custom-call(s32[3,3]{1,0:T(4,128)S(1)} %copy-done.5, bf16[3,512,128]{2,1,0:T(8,128)(2,1)S(1)} %collective-permute-done.3.m_far, bf16[3,512,128]{2,1,0:T(8,128)(2,1)S(1)} %collective-permute-done.4.m_near, ...), custom_call_target="tpu_custom_call" | custom-call | flops 1000 | bytes 1000 | tf_op jit(solution)/shard_map/own_grads/pallas_call | solution.py:477
  67.5 1.9 %collective-permute-start.17 = (bf16[4,2,256,128]{3,2,1,0:T(8,128)(2,1)S(1)}, bf16[4,2,256,128]{3,2,1,0:T(8,128)(2,1)S(1)}, u32[]{:S(2)}, u32[]{:S(2)}) collective-permute-start(bf16[4,2,256,128]{3,2,1,0:T(8,128)(2,1)S(1)} %get-tuple-element.46), channel_id=1, source_target_pairs={{0,8},{8,0},{16,24},{24,16},{32,40},{40,32},{64,72},{72,64},{80,88... | collective-permute-start | bytes 1572872 | tf_op jit(solution)/shard_map/ppermute | solution.py:488
  69.4 10.2 %all_to_all.5.text = bf16[8,32,256]{2,1,0:T(8,128)(2,1)S(1)} all-to-all(bf16[8,32,256]{2,1,0:T(8,128)(2,1)S(1)} %bitcast.6), channel_id=1, replica_groups={{0,8,64,72,128,136,192,200},{16,24,80,88,144,152,208,216},{32,40,96,104..., dimensions={0} | all-to-all | bytes 262144 | tf_op jit(solution)/shard_map/all_to_all | solution.py:490
  79.6 0.0 collective-permute-done.18.time
  79.6 0.0 collective-permute-done.17.core
  79.6 0.2 combine.1
  79.8 1.3 %collective-permute-start.19 = (bf16[784,128]{1,0:T(8,128)(2,1)S(1)}, bf16[784,128]{1,0:T(8,128)(2,1)S(1)}, u32[]{:S(2)}, u32[]{:S(2)}) collective-permute-start(bf16[784,128]{1,0:T(8,128)(2,1)S(1)} %get-tuple-element.49), channel_id=1, source_target_pairs={{16,0},{0,16},{32,24},{24,32},{8,48},{40,56},{80,64},{64,80},{96,8... | collective-permute-start | bytes 602120 | tf_op jit(solution)/shard_map/ppermute | solution.py:503
  81.1 6.3 %collective-permute-start.20 = (bf16[784,128]{1,0:T(8,128)(2,1)S(1)}, bf16[784,128]{1,0:T(8,128)(2,1)S(1)}, u32[]{:S(2)}, u32[]{:S(2)}) collective-permute-start(bf16[784,128]{1,0:T(8,128)(2,1)S(1)} %get-tuple-element.50), channel_id=1, source_target_pairs={{0,0},{32,8},{16,16},{8,32},{40,40},{24,48},{64,64},{96,72},{80,80... | collective-permute-start | bytes 602120 | tf_op jit(solution)/shard_map/ppermute | solution.py:503
  87.5 1.9 %collective-permute-start.21 = (bf16[784,128]{1,0:T(8,128)(2,1)S(1)}, bf16[784,128]{1,0:T(8,128)(2,1)S(1)}, u32[]{:S(2)}, u32[]{:S(2)}) collective-permute-start(bf16[784,128]{1,0:T(8,128)(2,1)S(1)} %get-tuple-element.51), channel_id=1, source_target_pairs={{16,8},{32,16},{0,24},{24,40},{40,48},{8,56},{80,72},{96,80},{64,8... | collective-permute-start | bytes 602120 | tf_op jit(solution)/shard_map/ppermute | solution.py:503
  89.4 1.9 %collective-permute-start.22 = (bf16[784,128]{1,0:T(8,128)(2,1)S(1)}, bf16[784,128]{1,0:T(8,128)(2,1)S(1)}, u32[]{:S(2)}, u32[]{:S(2)}) collective-permute-start(bf16[784,128]{1,0:T(8,128)(2,1)S(1)} %get-tuple-element.52), channel_id=1, source_target_pairs={{32,0},{0,8},{16,24},{40,32},{8,40},{24,56},{96,64},{64,72},{80,88... | collective-permute-start | bytes 602120 | tf_op jit(solution)/shard_map/ppermute | solution.py:503
  91.3 0.0 collective-permute-done.19.r0
  91.3 1.0 collective-permute-done.20.r1
  92.4 10.3 %collective-permute-done.21.r2 = bf16[784,128]{1,0:T(8,128)(2,1)S(1)} collective-permute-done((bf16[784,128]{1,0:T(8,128)(2,1)S(1)}, bf16[784,128]{1,0:T(8,128)(2,1)S(1)}, u32[]{:S(2)}, u32[]{:S(2)}) %collective-permute-start.21) | collective-permute-done | bytes 200736 | tf_op jit(solution)/shard_map/ppermute | solution.py:503
  102.6 0.0 collective-permute-done.22.r3
  102.6 1.1 %unpack.1 = (bf16[256,384]{1,0:T(8,128)(2,1)}, f32[256,384]{1,0:T(8,128)}, f32[256,384]{1,0:T(8,128)}, f32[8,384]{1,0:T(8,128)}, f32[8,384]{1,0:T(8,128)}) custom-call(bf16[784,128]{1,0:T(8,128)(2,1)S(1)} %collective-permute-done.19.r0, bf16[784,128]{1,0:T(8,128)(2,1)S(1)} %collective-permute-done.20.r1, bf16[784,128]{1,0:T(8,128)(2,1)S(1)} %collective-permute-done.21.r2, ...), custom_call_target="tpu_custom_call" | custom-call | tf_op jit(solution)/shard_map/unpack/pallas_call | solution.py:506
  (16 shorter events, 0.1 us)
Async XLA Ops:
  0.6 4.0 %collective-permute-start = (bf16[256,384]{1,0:T(8,128)(2,1)}, bf16[256,384]{1,0:T(8,128)(2,1)S(1)}, u32[]{:S(2)}, u32[]{:S(2)}) collective-permute-start(bf16[256,384]{1,0:T(8,128)(2,1)} %q_ref.1), channel_id=1, source_target_pairs={{0,8},{8,0},{16,24},{24,16},{32,40},{40,32},{48,56},{56,48},{64,72... | collective-permute-start | bytes 589832 | tf_op jit(solution)/shard_map/ppermute | solution.py:400
  1.4 3.7 %collective-permute-start.1 = (bf16[256,384]{1,0:T(8,128)(2,1)}, bf16[256,384]{1,0:T(8,128)(2,1)S(1)}, u32[]{:S(2)}, u32[]{:S(2)}) collective-permute-start(bf16[256,384]{1,0:T(8,128)(2,1)} %k_ref.1), channel_id=1, source_target_pairs={{0,8},{8,0},{16,24},{24,16},{32,40},{40,32},{48,56},{56,48},{64,72... | collective-permute-start | bytes 589832 | tf_op jit(solution)/shard_map/ppermute | solution.py:400
  1.5 5.9 %collective-permute-start.2 = (bf16[256,384]{1,0:T(8,128)(2,1)}, bf16[256,384]{1,0:T(8,128)(2,1)S(1)}, u32[]{:S(2)}, u32[]{:S(2)}) collective-permute-start(bf16[256,384]{1,0:T(8,128)(2,1)} %v_ref.1), channel_id=1, source_target_pairs={{0,8},{8,0},{16,24},{24,16},{32,40},{40,32},{48,56},{56,48},{64,72... | collective-permute-start | bytes 589832 | tf_op jit(solution)/shard_map/ppermute | solution.py:400
  1.9 10.8 %collective-permute-start.10 = (bf16[256,384]{1,0:T(8,128)(2,1)}, bf16[256,384]{1,0:T(8,128)(2,1)S(1)}, u32[]{:S(2)}, u32[]{:S(2)}) collective-permute-start(bf16[256,384]{1,0:T(8,128)(2,1)} %c0.1), channel_id=1, source_target_pairs={{0,2},{1,3},{2,0},{3,1},{4,6},{5,7},{6,4},{7,5},{8,10},{9,11},{10,... | collective-permute-start | bytes 589832 | tf_op jit(solution)/shard_map/ppermute | solution.py:386
  4.7 18.3 %collective-permute-start.5 = (bf16[256,384]{1,0:T(8,128)(2,1)}, bf16[256,384]{1,0:T(8,128)(2,1)S(1)}, u32[]{:S(2)}, u32[]{:S(2)}) collective-permute-start(bf16[256,384]{1,0:T(8,128)(2,1)} %c0.1), channel_id=1, source_target_pairs={{0,4},{1,5},{2,6},{3,7},{4,0},{5,1},{6,2},{7,3},{8,12},{9,13},{10,... | collective-permute-start | bytes 589832 | tf_op jit(solution)/shard_map/ppermute | solution.py:384
  4.7 2.8 %copy-start.6 = (bf16[256,384]{1,0:T(8,128)(2,1)}, bf16[256,384]{1,0:T(8,128)(2,1)S(1)}, u32[]{:S(2)}) copy-start(bf16[256,384]{1,0:T(8,128)(2,1)S(1)} %collective-permute-done.q_next) | copy-start | bytes 589828
  4.7 18.8 %collective-permute-start.9 = (bf16[256,384]{1,0:T(8,128)(2,1)}, bf16[256,384]{1,0:T(8,128)(2,1)S(1)}, u32[]{:S(2)}, u32[]{:S(2)}) collective-permute-start(bf16[256,384]{1,0:T(8,128)(2,1)} %c0.1), channel_id=1, source_target_pairs={{0,1},{1,2},{2,3},{3,0},{4,5},{5,6},{6,7},{7,4},{8,9},{9,10},{10,1... | collective-permute-start | bytes 589832 | tf_op jit(solution)/shard_map/ppermute | solution.py:386
  5.1 2.4 %copy-start.7 = (bf16[256,384]{1,0:T(8,128)(2,1)}, bf16[256,384]{1,0:T(8,128)(2,1)S(1)}, u32[]{:S(2)}) copy-start(bf16[256,384]{1,0:T(8,128)(2,1)S(1)} %collective-permute-done.1.k_next) | copy-start | bytes 589828
  5.1 18.9 %collective-permute-start.11 = (bf16[256,384]{1,0:T(8,128)(2,1)}, bf16[256,384]{1,0:T(8,128)(2,1)S(1)}, u32[]{:S(2)}, u32[]{:S(2)}) collective-permute-start(bf16[256,384]{1,0:T(8,128)(2,1)} %c0.1), channel_id=1, source_target_pairs={{0,3},{1,0},{2,1},{3,2},{4,7},{5,4},{6,5},{7,6},{8,11},{9,8},{10,9... | collective-permute-start | bytes 589832 | tf_op jit(solution)/shard_map/ppermute | solution.py:386
  7.4 0.7 copy-start.8
  11.4 26.5 %collective-permute-start.3 = (bf16[3,512,128]{2,1,0:T(8,128)(2,1)}, bf16[3,512,128]{2,1,0:T(8,128)(2,1)S(1)}, u32[]{:S(2)}, u32[]{:S(2)}) collective-permute-start(bf16[3,512,128]{2,1,0:T(8,128)(2,1)} %get-tuple-element.29), channel_id=1, source_target_pairs={{0,16},{16,0},{24,32},{32,24},{48,8},{56,40},{64,80},{80,64},{88,9... | collective-permute-start | bytes 1179656 | tf_op jit(solution)/shard_map/ppermute | solution.py:402
  12.7 25.2 %collective-permute-start.4 = (bf16[3,512,128]{2,1,0:T(8,128)(2,1)}, bf16[3,512,128]{2,1,0:T(8,128)(2,1)S(1)}, u32[]{:S(2)}, u32[]{:S(2)}) collective-permute-start(bf16[3,512,128]{2,1,0:T(8,128)(2,1)} %get-tuple-element.30), channel_id=1, source_target_pairs={{0,0},{8,32},{16,16},{32,8},{40,40},{48,24},{64,64},{72,96},{80,80... | collective-permute-start | bytes 1179656 | tf_op jit(solution)/shard_map/ppermute | solution.py:402
  23.0 5.7 %collective-permute-start.8 = (bf16[256,384]{1,0:T(8,128)(2,1)S(1)}, bf16[256,384]{1,0:T(8,128)(2,1)S(1)}, u32[]{:S(2)}, u32[]{:S(2)}) collective-permute-start(bf16[256,384]{1,0:T(8,128)(2,1)S(1)} %collective-permute-done.5.c4), channel_id=1, source_target_pairs={{0,3},{1,0},{2,1},{3,2},{4,7},{5,4},{6,5},{7,6},{8,11},{9,8},{10,9... | collective-permute-start | bytes 589832 | tf_op jit(solution)/shard_map/ppermute | solution.py:386
  23.5 7.2 %collective-permute-start.7 = (bf16[256,384]{1,0:T(8,128)(2,1)S(1)}, bf16[256,384]{1,0:T(8,128)(2,1)S(1)}, u32[]{:S(2)}, u32[]{:S(2)}) collective-permute-start(bf16[256,384]{1,0:T(8,128)(2,1)S(1)} %collective-permute-done.5.c4), channel_id=1, source_target_pairs={{0,2},{1,3},{2,0},{3,1},{4,6},{5,7},{6,4},{7,5},{8,10},{9,11},{10,... | collective-permute-start | bytes 589832 | tf_op jit(solution)/shard_map/ppermute | solution.py:386
  24.0 8.7 %collective-permute-start.6 = (bf16[256,384]{1,0:T(8,128)(2,1)S(1)}, bf16[256,384]{1,0:T(8,128)(2,1)S(1)}, u32[]{:S(2)}, u32[]{:S(2)}) collective-permute-start(bf16[256,384]{1,0:T(8,128)(2,1)S(1)} %collective-permute-done.5.c4), channel_id=1, source_target_pairs={{0,1},{1,2},{2,3},{3,0},{4,5},{5,6},{6,7},{7,4},{8,9},{9,10},{10,1... | collective-permute-start | bytes 589832 | tf_op jit(solution)/shard_map/ppermute | solution.py:386
  24.6 1.7 %copy-start = (bf16[384,3072]{1,0:T(8,128)(2,1)S(1)}, bf16[384,3072]{1,0:T(8,128)(2,1)}, u32[]{:S(2)}) copy-start(bf16[384,3072]{1,0:T(8,128)(2,1)} %w_ref.3) | copy-start | bytes 7077892
  26.3 0.9 copy-start.4
  27.2 5.4 %copy-start.1 = (bf16[384,3072]{1,0:T(8,128)(2,1)S(1)}, bf16[384,3072]{1,0:T(8,128)(2,1)}, u32[]{:S(2)}) copy-start(bf16[384,3072]{1,0:T(8,128)(2,1)} %w_ref.3) | copy-start | bytes 7077892
  28.2 23.8 %copy-start.9 = (s32[256]{0:T(256)S(1)}, s32[256]{0:T(256)}, u32[]{:S(2)}) copy-start(s32[256]{0:T(256)} %param.17) | copy-start | bytes 3076
  28.3 24.0 %copy-start.2 = (bf16[256,384]{1,0:T(8,128)(2,1)S(1)}, bf16[256,384]{1,0:T(8,128)(2,1)}, u32[]{:S(2)}) copy-start(bf16[256,384]{1,0:T(8,128)(2,1)} %tk_ref.3) | copy-start | bytes 589828
  28.3 24.0 %copy-start.3 = (bf16[256,384]{1,0:T(8,128)(2,1)S(1)}, bf16[256,384]{1,0:T(8,128)(2,1)}, u32[]{:S(2)}) copy-start(bf16[256,384]{1,0:T(8,128)(2,1)} %tv_ref.3) | copy-start | bytes 589828
  28.3 24.0 %copy-start.5 = (s32[3,3]{1,0:T(4,128)S(1)}, s32[3,3]{1,0:T(4,128)}, u32[]{:S(2)}) copy-start(s32[3,3]{1,0:T(4,128)} %ext_ref.5) | copy-start | bytes 112
  33.7 1.4 %collective-permute-start.12 = (bf16[2,256,128]{2,1,0:T(8,128)(2,1)S(1)}, bf16[2,256,128]{2,1,0:T(8,128)(2,1)S(1)}, u32[]{:S(2)}, u32[]{:S(2)}) collective-permute-start(bf16[2,256,128]{2,1,0:T(8,128)(2,1)S(1)} %get-tuple-element.31), channel_id=1, source_target_pairs={{0,8},{8,0},{16,24},{24,16},{32,40},{40,32},{48,56},{56,48},{64,72... | collective-permute-start | bytes 393224 | tf_op jit(solution)/shard_map/ppermute | solution.py:419
  38.0 14.2 %collective-permute-start.16 = (bf16[2,2,512,128]{3,2,1,0:T(8,128)(2,1)S(1)}, bf16[2,2,512,128]{3,2,1,0:T(8,128)(2,1)S(1)}, u32[]{:S(2)}, u32[]{:S(2)}) collective-permute-start(bf16[2,2,512,128]{3,2,1,0:T(8,128)(2,1)S(1)} %pad_maximum_fusion), channel_id=1, source_target_pairs={{0,8},{8,0},{16,24},{24,16},{32,40},{40,32},{64,72},{72,64},{80,88... | collective-permute-start | bytes 1572872 | tf_op jit(solution)/shard_map/ppermute | solution.py:422
  39.9 12.3 %collective-permute-start.15 = (bf16[2,2,512,128]{3,2,1,0:T(8,128)(2,1)S(1)}, bf16[2,2,512,128]{3,2,1,0:T(8,128)(2,1)S(1)}, u32[]{:S(2)}, u32[]{:S(2)}) collective-permute-start(bf16[2,2,512,128]{3,2,1,0:T(8,128)(2,1)S(1)} %pad_maximum_fusion), channel_id=1, source_target_pairs={{8,64},{24,80},{40,96},{64,8},{72,128},{80,24},{88,144},{96,40},{1... | collective-permute-start | bytes 1572872 | tf_op jit(solution)/shard_map/ppermute | solution.py:423
  43.5 13.4 %collective-permute-start.13 = (bf16[512,128]{1,0:T(8,128)(2,1)S(1)}, bf16[512,128]{1,0:T(8,128)(2,1)S(1)}, u32[]{:S(2)}, u32[]{:S(2)}) collective-permute-start(bf16[512,128]{1,0:T(8,128)(2,1)S(1)} %get-tuple-element.36), channel_id=1, source_target_pairs={{0,16},{16,0},{24,32},{32,24},{48,8},{56,40},{64,80},{80,64},{88,9... | collective-permute-start | bytes 393224 | tf_op jit(solution)/shard_map/ppermute | solution.py:433
  44.8 12.1 %collective-permute-start.14 = (bf16[512,128]{1,0:T(8,128)(2,1)S(1)}, bf16[512,128]{1,0:T(8,128)(2,1)S(1)}, u32[]{:S(2)}, u32[]{:S(2)}) collective-permute-start(bf16[512,128]{1,0:T(8,128)(2,1)S(1)} %get-tuple-element.37), channel_id=1, source_target_pairs={{0,0},{8,32},{16,16},{32,8},{40,40},{48,24},{64,64},{72,96},{80,80... | collective-permute-start | bytes 393224 | tf_op jit(solution)/shard_map/ppermute | solution.py:433
  60.6 19.0 %collective-permute-start.18 = (bf16[4,2,256,128]{3,2,1,0:T(8,128)(2,1)S(1)}, bf16[4,2,256,128]{3,2,1,0:T(8,128)(2,1)S(1)}, u32[]{:S(2)}, u32[]{:S(2)}) collective-permute-start(bf16[4,2,256,128]{3,2,1,0:T(8,128)(2,1)S(1)} %get-tuple-element.47), channel_id=1, source_target_pairs={{8,64},{24,80},{40,96},{64,8},{72,128},{80,24},{88,144},{96,40},{1... | collective-permute-start | bytes 1572872 | tf_op jit(solution)/shard_map/ppermute | solution.py:476
  67.5 12.1 %collective-permute-start.17 = (bf16[4,2,256,128]{3,2,1,0:T(8,128)(2,1)S(1)}, bf16[4,2,256,128]{3,2,1,0:T(8,128)(2,1)S(1)}, u32[]{:S(2)}, u32[]{:S(2)}) collective-permute-start(bf16[4,2,256,128]{3,2,1,0:T(8,128)(2,1)S(1)} %get-tuple-element.46), channel_id=1, source_target_pairs={{0,8},{8,0},{16,24},{24,16},{32,40},{40,32},{64,72},{72,64},{80,88... | collective-permute-start | bytes 1572872 | tf_op jit(solution)/shard_map/ppermute | solution.py:488
  79.8 11.5 %collective-permute-start.19 = (bf16[784,128]{1,0:T(8,128)(2,1)S(1)}, bf16[784,128]{1,0:T(8,128)(2,1)S(1)}, u32[]{:S(2)}, u32[]{:S(2)}) collective-permute-start(bf16[784,128]{1,0:T(8,128)(2,1)S(1)} %get-tuple-element.49), channel_id=1, source_target_pairs={{16,0},{0,16},{32,24},{24,32},{8,48},{40,56},{80,64},{64,80},{96,8... | collective-permute-start | bytes 602120 | tf_op jit(solution)/shard_map/ppermute | solution.py:503
  81.1 11.2 %collective-permute-start.20 = (bf16[784,128]{1,0:T(8,128)(2,1)S(1)}, bf16[784,128]{1,0:T(8,128)(2,1)S(1)}, u32[]{:S(2)}, u32[]{:S(2)}) collective-permute-start(bf16[784,128]{1,0:T(8,128)(2,1)S(1)} %get-tuple-element.50), channel_id=1, source_target_pairs={{0,0},{32,8},{16,16},{8,32},{40,40},{24,48},{64,64},{96,72},{80,80... | collective-permute-start | bytes 602120 | tf_op jit(solution)/shard_map/ppermute | solution.py:503
  87.5 15.1 %collective-permute-start.21 = (bf16[784,128]{1,0:T(8,128)(2,1)S(1)}, bf16[784,128]{1,0:T(8,128)(2,1)S(1)}, u32[]{:S(2)}, u32[]{:S(2)}) collective-permute-start(bf16[784,128]{1,0:T(8,128)(2,1)S(1)} %get-tuple-element.51), channel_id=1, source_target_pairs={{16,8},{32,16},{0,24},{24,40},{40,48},{8,56},{80,72},{96,80},{64,8... | collective-permute-start | bytes 602120 | tf_op jit(solution)/shard_map/ppermute | solution.py:503
  89.4 13.2 %collective-permute-start.22 = (bf16[784,128]{1,0:T(8,128)(2,1)S(1)}, bf16[784,128]{1,0:T(8,128)(2,1)S(1)}, u32[]{:S(2)}, u32[]{:S(2)}) collective-permute-start(bf16[784,128]{1,0:T(8,128)(2,1)S(1)} %get-tuple-element.52), channel_id=1, source_target_pairs={{32,0},{0,8},{16,24},{40,32},{8,40},{24,56},{96,64},{64,72},{80,88... | collective-permute-start | bytes 602120 | tf_op jit(solution)/shard_map/ppermute | solution.py:503
